TPU v7x, 32 devices: a whole 2x2x4 slice. The times are simulated.
32 devices in a mesh: dp: 16 (over z, y, core), seq: 2 (over x).
Axes of the slice: x: 2, y: 2, z: 4, core: 2. Of those that a mesh axis runs over, the one named last changes fastest.
Arguments:
- tokens: bfloat16 [16384, 1024], P(('dp', 'seq')), may hold values from -6 to 6
- segments: int32 [16, 1024], P('dp'), may hold values from 0 to 2, as said below
- input_gain: bfloat16 [1024], P(('dp', 'seq')), may hold values from 0.5 to 1.5
- mixer_in: bfloat16 [1024, 3352], P('dp', 'seq'), may hold values from -0.1875 to 0.1875
- conv_weight: bfloat16 [1792, 4], P(('dp', 'seq')), may hold values from -3 to 3
- conv_bias: bfloat16 [1792], P(('dp', 'seq')), may hold values from -3 to 3
- step_bias: float32 [24], replicated, may hold values from -4.5 to -2.5
- decay_log: float32 [24], replicated, may hold values from -4 to 0
- skip_gain: float32 [24], replicated, may hold values from 0.5 to 1.5
- mixer_gain: bfloat16 [1536], P(('dp', 'seq')), may hold values from 0.5 to 1.5
- mixer_out: bfloat16 [1536, 1024], P('dp', 'seq'), may hold values from -0.15625 to 0.15625
- w_query: bfloat16 [1024, 512], P('dp', 'seq'), may hold values from -0.1875 to 0.1875
- w_key: bfloat16 [1024, 128], P('dp', 'seq'), may hold values from -0.1875 to 0.1875
- w_value: bfloat16 [1024, 128], P('dp', 'seq'), may hold values from -0.1875 to 0.1875
- w_output: bfloat16 [512, 1024], P('dp', 'seq'), may hold values from -3 to 3
- hidden_gain: bfloat16 [1024], P(('dp', 'seq')), may hold values from 0.5 to 1.5
- w_gate: bfloat16 [1024, 2048], P('dp', 'seq'), may hold values from -0.1875 to 0.1875
- w_up: bfloat16 [1024, 2048], P('dp', 'seq'), may hold values from -0.1875 to 0.1875
- w_down: bfloat16 [2048, 1024], P('dp', 'seq'), may hold values from -0.125 to 0.125
- cotangent: bfloat16 [16384, 1024], P(('dp', 'seq')), may hold values from -6 to 6
Outputs:
- output: bfloat16 [16384, 1024], P(('dp', 'seq'))
- grad_tokens: float32 [16384, 1024], P(('dp', 'seq'))
- grad_input_gain: float32 [1024], P(('dp', 'seq'))
- grad_mixer_in: float32 [1024, 3352], P('dp', 'seq')
- grad_conv_weight: float32 [1792, 4], P(('dp', 'seq'))
- grad_conv_bias: float32 [1792], P(('dp', 'seq'))
- grad_step_bias: float32 [24], replicated
- grad_decay_log: float32 [24], replicated
- grad_skip_gain: float32 [24], replicated
- grad_mixer_gain: float32 [1536], P(('dp', 'seq'))
- grad_mixer_out: float32 [1536, 1024], P('dp', 'seq')
- grad_w_query: float32 [1024, 512], P('dp', 'seq')
- grad_w_key: float32 [1024, 128], P('dp', 'seq')
- grad_w_value: float32 [1024, 128], P('dp', 'seq')
- grad_w_output: float32 [512, 1024], P('dp', 'seq')
- grad_hidden_gain: float32 [1024], P(('dp', 'seq'))
- grad_w_gate: float32 [1024, 2048], P('dp', 'seq')
- grad_w_up: float32 [1024, 2048], P('dp', 'seq')
- grad_w_down: float32 [2048, 1024], P('dp', 'seq')
Inputs may be any that keep to these rules, and one draw needn't show every extreme that they name: `segments`: each sequence holds three documents numbered 0, 1, 2 in order; the first and the last each have from 512 - max(64, 2) to 511 tokens.
All inputs are finite; a program needn't handle non-finite values.
Results may differ from a plain program's by a relative error of at most 0.02.
Values may be sent and summed in bfloat16 or wider, within the bound.
No kernel may reach another device: no remote copies, remote signals or barrier semaphores. Data moves between devices by JAX's collectives and lax.ppermute only.
A program may use at most 256 MiB of HBM per device.

v0:
```python
import jax
import jax.numpy as jnp
from jax import lax
from jax.sharding import PartitionSpec as P

HEADS = 8
KV_HEADS = 2
HEAD_DIM = 64
SSM_HEADS = 24
SSM_DIM = 64
STATE = 128
CONV = 4
INNER = 1536
CHANNELS = 1792


EPS = 1e-05
THETA = 100000000000.0
HIGH = lax.Precision.HIGHEST


def entering(value, axis, combine, identity):
    length, index = (lax.axis_size(axis), lax.axis_index(axis))
    everything = jax.tree.map(
        lambda part, kind: lax.all_gather(part.astype(kind), axis),
        value,
        (jnp.bfloat16, jnp.bfloat16),
    )
    start = jax.tree.map(
        lambda part, zero: jnp.broadcast_to(jnp.asarray(zero, part.dtype), part.shape),
        value,
        identity,
    )

    def turn(k, before):
        reached = k < index
        new = combine(
            before, jax.tree.map(lambda part, own: part[k].astype(own.dtype), everything, value)
        )
        return jax.tree.map(lambda a, b: jnp.where(reached, a, b), new, before)

    return lax.fori_loop(0, length, turn, start)


def entering_2(value, axis, join, neutral):
    count = lax.axis_size(axis)
    place = lax.axis_index(axis)
    ahead = count - 1 - place
    gathered = jax.tree.map(
        lambda a, kind: lax.all_gather(a.astype(kind), axis),
        value,
        jax.tree.map(lambda a: jnp.bfloat16 if a.dtype == jnp.float32 else a.dtype, value),
    )
    state = jax.tree.map(lambda a, e: jnp.zeros_like(a) + jnp.asarray(e, a.dtype), value, neutral)

    def one(turn, state):
        source = count - 1 - turn
        return join(
            state,
            jax.tree.map(
                lambda a, own: lax.dynamic_index_in_dim(a, source, 0, False).astype(own.dtype),
                gathered,
                value,
            ),
        )

    return lax.fori_loop(0, ahead, one, state)


def rms_scale(values, weight):
    return values * lax.rsqrt(jnp.mean(values * values, axis=-1, keepdims=True) + EPS) * weight


def rotate(values, places, sign):
    half = values.shape[-1] // 2
    freq = THETA ** (-jnp.arange(half, dtype=jnp.float32) / half)
    angle = places.astype(jnp.float32)[:, None] * freq[None, :]
    cosine = jnp.cos(angle)[:, None, :]
    sine = sign * jnp.sin(angle)[:, None, :]
    first = values[..., :half]
    second = values[..., half:]
    return jnp.concatenate(
        [first * cosine - second * sine, second * cosine + first * sine], axis=-1
    )


def doc_places(seg_row):
    index = jnp.arange(seg_row.shape[0], dtype=jnp.int32)
    change = jnp.concatenate([jnp.ones((1,), bool), seg_row[1:] != seg_row[:-1]])
    starts = lax.cummax(jnp.where(change, index, 0), axis=0)
    return index - starts


def conv_mix(extended, weight, bias, seg_ext):
    count = extended.shape[0] - (CONV - 1)
    owner = seg_ext[CONV - 1 :]
    total = jnp.zeros((count, extended.shape[1]), jnp.float32) + bias[None, :]
    for offset in range(CONV):
        window = extended[offset : offset + count]
        same = (seg_ext[offset : offset + count] == owner)[:, None]
        total = total + jnp.where(same, window * weight[None, :, offset], 0.0)
    return jax.nn.silu(total)


def decay_terms(step_raw, step_bias, decay_log):
    step_size = jax.nn.softplus(step_raw + step_bias[None, :])
    return (step_size, jnp.cumsum(-step_size * jnp.exp(decay_log)[None, :], axis=0))


def block_state(inner, state_in, step_raw, step_bias, decay_log, seg_rows, seg_prev):
    step_size, cumul = decay_terms(step_raw, step_bias, decay_log)
    last_seg = seg_rows[-1]
    tail = (
        jnp.where((seg_rows == last_seg)[:, None], jnp.exp(cumul[-1][None, :] - cumul), 0.0)
        * step_size
    )
    weighted = inner * tail[:, :, None]
    fresh_state = jnp.einsum("shp,sn->hpn", weighted, state_in, precision=HIGH)
    carried = jnp.where(last_seg == seg_prev, jnp.exp(cumul[-1]), 0.0)
    return (carried, fresh_state)


def block_mix(
    inner,
    state_in,
    state_out,
    step_raw,
    gate_z,
    step_bias,
    decay_log,
    skip_gain,
    mixer_gain,
    start_state,
    seg_rows,
    seg_prev,
):
    step_size, cumul = decay_terms(step_raw, step_bias, decay_log)
    count = seg_rows.shape[0]
    index = jnp.arange(count)
    allowed = (seg_rows[:, None] == seg_rows[None, :]) & (index[None, :] <= index[:, None])
    gap = cumul.T[:, :, None] - cumul.T[:, None, :]
    kernel = jnp.where(allowed[None], jnp.exp(jnp.where(allowed[None], gap, 0.0)), 0.0)
    intersection = jnp.dot(state_out, state_in.T, precision=HIGH)
    weights_mat = kernel * intersection[None] * step_size.T[:, None, :]
    local_part = jnp.einsum("hts,shp->thp", weights_mat, inner, precision=HIGH)
    entry = jnp.where((seg_rows == seg_prev)[:, None], jnp.exp(cumul), 0.0)
    incoming = jnp.einsum("tn,hpn->thp", state_out, start_state, precision=HIGH) * entry[:, :, None]
    mixed = local_part + incoming + skip_gain[None, :, None] * inner
    gated = mixed.reshape(count, -1) * jax.nn.silu(gate_z)
    return rms_scale(gated, mixer_gain)


def dot_plain(left, right):
    return jnp.dot(left, right, preferred_element_type=jnp.float32)


def dot_right_t(left, right):
    return lax.dot_general(
        left, right, (((1,), (1,)), ((), ())), preferred_element_type=jnp.float32
    )


def dot_left_t(left, right):
    return lax.dot_general(
        left, right, (((0,), (0,)), ((), ())), preferred_element_type=jnp.float32
    )


def chain_forward(earlier, later):
    return (earlier[0] * later[0], later[0][:, None, None] * earlier[1] + later[1])


def chain_backward(earlier, later):
    return (earlier[0] * later[0], later[1] + later[0][:, None, None] * earlier[1])


def ffn_backward_grads(act_grad, gate_part, up_part, sigmoid_gate):
    up_grad_low = (act_grad * gate_part * sigmoid_gate).astype(jnp.bfloat16)
    gate_grad_low = (
        act_grad * up_part * sigmoid_gate * (1.0 + gate_part * (1.0 - sigmoid_gate))
    ).astype(jnp.bfloat16)
    return (gate_grad_low, up_grad_low)


def shards(
    tokens,
    segments,
    input_gain,
    mixer_in,
    conv_weight,
    conv_bias,
    step_bias,
    decay_log,
    skip_gain,
    mixer_gain,
    mixer_out,
    w_query,
    w_key,
    w_value,
    w_output,
    hidden_gain,
    w_gate,
    w_up,
    w_down,
    cotangent,
):
    sectioned = (
        lax.all_gather(input_gain, "seq", axis=0, tiled=True),
        lax.all_gather(mixer_in, "seq", axis=1, tiled=True),
        lax.all_gather(conv_weight, "seq", axis=0, tiled=True),
        lax.all_gather(conv_bias, "seq", axis=0, tiled=True),
        lax.all_gather(mixer_gain, "seq", axis=0, tiled=True),
        lax.all_gather(mixer_out, "seq", axis=1, tiled=True),
        lax.all_gather(w_query, "seq", axis=1, tiled=True),
        lax.all_gather(w_key, "seq", axis=1, tiled=True),
        lax.all_gather(w_value, "seq", axis=1, tiled=True),
        lax.all_gather(w_output, "seq", axis=1, tiled=True),
        lax.all_gather(hidden_gain, "seq", axis=0, tiled=True),
        lax.all_gather(w_gate, "seq", axis=1, tiled=True),
        lax.all_gather(w_up, "seq", axis=1, tiled=True),
        lax.all_gather(w_down, "seq", axis=1, tiled=True),
    )
    whole = (
        lax.all_gather(sectioned[0], "dp", axis=0, tiled=True),
        lax.all_gather(sectioned[1], "dp", axis=0, tiled=True),
        lax.all_gather(sectioned[2], "dp", axis=0, tiled=True),
        lax.all_gather(sectioned[3], "dp", axis=0, tiled=True),
        lax.all_gather(sectioned[4], "dp", axis=0, tiled=True),
        lax.all_gather(sectioned[5], "dp", axis=0, tiled=True),
        lax.all_gather(sectioned[6], "dp", axis=0, tiled=True),
        lax.all_gather(sectioned[7], "dp", axis=0, tiled=True),
        lax.all_gather(sectioned[8], "dp", axis=0, tiled=True),
        lax.all_gather(sectioned[9], "dp", axis=0, tiled=True),
        lax.all_gather(sectioned[10], "dp", axis=0, tiled=True),
        lax.all_gather(sectioned[11], "dp", axis=0, tiled=True),
        lax.all_gather(sectioned[12], "dp", axis=0, tiled=True),
        lax.all_gather(sectioned[13], "dp", axis=0, tiled=True),
    )
    (
        full_input_gain,
        full_mixer_in,
        full_conv_weight,
        full_conv_bias,
        full_mixer_gain,
        full_mixer_out,
        full_query,
        full_key,
        full_value,
        full_output,
        full_hidden_gain,
        full_gate,
        full_up,
        full_down,
    ) = whole
    row_count = tokens.shape[0]
    seg_all = segments[0]
    seq_length = seg_all.shape[0]
    seq_count = lax.axis_size("seq")
    seq_rank = lax.axis_index("seq")
    row_start = seq_rank * row_count
    places_all = doc_places(seg_all)
    seg_rows = lax.dynamic_slice_in_dim(seg_all, row_start, row_count)
    places = lax.dynamic_slice_in_dim(places_all, row_start, row_count)
    padded_seg = jnp.concatenate([jnp.full((CONV - 1,), -1, jnp.int32), seg_all])
    seg_ext = lax.dynamic_slice_in_dim(padded_seg, row_start, row_count + CONV - 1)
    seg_prev = seg_ext[CONV - 2]
    rim_start = jnp.maximum(seq_rank - 1, 0) * (CONV - 1)
    hidden_in = tokens.astype(jnp.float32)
    normed, norm_pull = jax.vjp(rms_scale, hidden_in, full_input_gain.astype(jnp.float32))
    normed_low = normed.astype(jnp.bfloat16)
    projected = dot_plain(normed_low, full_mixer_in)
    gate_z = projected[:, :INNER]
    conv_low = projected[:, INNER : INNER + CHANNELS].astype(jnp.bfloat16)
    step_raw = projected[:, INNER + CHANNELS :]
    group_size = HEADS // KV_HEADS
    score_scale = HEAD_DIM ** (-0.5)
    query = dot_plain(normed_low, full_query).reshape(row_count, HEADS, HEAD_DIM)
    key_proj = dot_plain(normed_low, full_key).reshape(row_count, KV_HEADS, HEAD_DIM)
    value_low = dot_plain(normed_low, full_value).astype(jnp.bfloat16)
    query_low = rotate(query, places, 1.0).astype(jnp.bfloat16)
    key_low = (
        rotate(key_proj, places, 1.0).astype(jnp.bfloat16).reshape(row_count, KV_HEADS * HEAD_DIM)
    )
    tail_low = conv_low[row_count - CONV + 1 :]
    keys_all, values_all, tails_all = (
        lax.all_gather(key_low, "seq", axis=0, tiled=True),
        lax.all_gather(value_low, "seq", axis=0, tiled=True),
        lax.all_gather(tail_low, "seq", axis=0, tiled=True),
    )
    rim_rows = jnp.where(
        seq_rank > 0,
        lax.dynamic_slice_in_dim(tails_all, rim_start, CONV - 1),
        jnp.zeros_like(tail_low),
    )
    extended = jnp.concatenate([rim_rows, conv_low]).astype(jnp.float32)

    def conv_piece(ext_rows, taps, shift_bias):
        return conv_mix(ext_rows, taps, shift_bias, seg_ext)

    conv_out, conv_pull = jax.vjp(
        conv_piece,
        extended,
        full_conv_weight.astype(jnp.float32),
        full_conv_bias.astype(jnp.float32),
    )
    mixed_in = conv_out.astype(jnp.bfloat16).astype(jnp.float32)
    inner = mixed_in[:, :INNER].reshape(row_count, SSM_HEADS, SSM_DIM)
    state_in = mixed_in[:, INNER : INNER + STATE]
    state_out = mixed_in[:, INNER + STATE :]

    def state_piece(inner_vals, in_vals, raw_vals, bias_vals, decay_vals):
        return block_state(inner_vals, in_vals, raw_vals, bias_vals, decay_vals, seg_rows, seg_prev)

    (carried, fresh_state), state_pull = jax.vjp(
        state_piece, inner, state_in, step_raw, step_bias, decay_log
    )
    start_state = entering(
        (carried, fresh_state),
        "seq",
        chain_forward,
        (jnp.ones_like(carried), jnp.zeros_like(fresh_state)),
    )[1]

    def mixer_piece(
        inner_vals,
        in_vals,
        out_vals,
        raw_vals,
        gate_vals,
        bias_vals,
        decay_vals,
        skip_vals,
        gain_vals,
        start_vals,
    ):
        return block_mix(
            inner_vals,
            in_vals,
            out_vals,
            raw_vals,
            gate_vals,
            bias_vals,
            decay_vals,
            skip_vals,
            gain_vals,
            start_vals,
            seg_rows,
            seg_prev,
        )

    mixed_norm, mixer_pull = jax.vjp(
        mixer_piece,
        inner,
        state_in,
        state_out,
        step_raw,
        gate_z,
        step_bias,
        decay_log,
        skip_gain,
        full_mixer_gain.astype(jnp.float32),
        start_state,
    )
    mixed_low = mixed_norm.astype(jnp.bfloat16)
    mamba_part = dot_plain(mixed_low, full_mixer_out)
    grouped = query_low.reshape(row_count, KV_HEADS, group_size, HEAD_DIM)
    keys_three = keys_all.reshape(seq_length, KV_HEADS, HEAD_DIM)
    values_three = values_all.reshape(seq_length, KV_HEADS, HEAD_DIM)
    query_index = row_start + jnp.arange(row_count)
    key_index = jnp.arange(seq_length)
    allowed = (seg_rows[:, None] == seg_all[None, :]) & (key_index[None, :] <= query_index[:, None])
    scores = (
        jnp.einsum("tkgd,skd->kgts", grouped, keys_three, preferred_element_type=jnp.float32)
        * score_scale
    )
    scores = jnp.where(allowed[None, None], scores, -1e30)
    log_total = jax.nn.logsumexp(scores, axis=-1, keepdims=True)
    probs = jnp.exp(scores - log_total)
    probs_low = probs.astype(jnp.bfloat16)
    attended = jnp.einsum(
        "kgts,skd->tkgd", probs_low, values_three, preferred_element_type=jnp.float32
    )
    attended_low = attended.reshape(row_count, HEADS * HEAD_DIM).astype(jnp.bfloat16)
    attn_part = dot_plain(attended_low, full_output)
    hidden_mid = hidden_in + attn_part + mamba_part
    normed_two, norm_two_pull = jax.vjp(rms_scale, hidden_mid, full_hidden_gain.astype(jnp.float32))
    normed_two_low = normed_two.astype(jnp.bfloat16)
    gate_part = dot_plain(normed_two_low, full_gate)
    up_part = dot_plain(normed_two_low, full_up)
    sigmoid_gate = jax.nn.sigmoid(gate_part)
    activated_low = (gate_part * sigmoid_gate * up_part).astype(jnp.bfloat16)
    output = (hidden_mid + dot_plain(activated_low, full_down)).astype(jnp.bfloat16)
    back_sectioned = (
        lax.all_gather(mixer_in, "seq", axis=1, tiled=True),
        lax.all_gather(mixer_out, "seq", axis=1, tiled=True),
        lax.all_gather(w_query, "seq", axis=1, tiled=True),
        lax.all_gather(w_key, "seq", axis=1, tiled=True),
        lax.all_gather(w_value, "seq", axis=1, tiled=True),
        lax.all_gather(w_output, "seq", axis=1, tiled=True),
        lax.all_gather(w_gate, "seq", axis=1, tiled=True),
        lax.all_gather(w_up, "seq", axis=1, tiled=True),
        lax.all_gather(w_down, "seq", axis=1, tiled=True),
    )
    back_whole = (
        lax.all_gather(back_sectioned[0], "dp", axis=0, tiled=True),
        lax.all_gather(back_sectioned[1], "dp", axis=0, tiled=True),
        lax.all_gather(back_sectioned[2], "dp", axis=0, tiled=True),
        lax.all_gather(back_sectioned[3], "dp", axis=0, tiled=True),
        lax.all_gather(back_sectioned[4], "dp", axis=0, tiled=True),
        lax.all_gather(back_sectioned[5], "dp", axis=0, tiled=True),
        lax.all_gather(back_sectioned[6], "dp", axis=0, tiled=True),
        lax.all_gather(back_sectioned[7], "dp", axis=0, tiled=True),
        lax.all_gather(back_sectioned[8], "dp", axis=0, tiled=True),
    )
    (
        back_mixer_in,
        back_mixer_out,
        back_query,
        back_key,
        back_value,
        back_output,
        back_gate,
        back_up,
        back_down,
    ) = back_whole
    act_grad = dot_right_t(cotangent, back_down)
    grad_down_part = dot_left_t(activated_low, cotangent)
    gate_grad_low, up_grad_low = ffn_backward_grads(act_grad, gate_part, up_part, sigmoid_gate)
    grad_gate_part = dot_left_t(normed_two_low, gate_grad_low)
    grad_up_part = dot_left_t(normed_two_low, up_grad_low)
    normed_two_grad = dot_right_t(gate_grad_low, back_gate) + dot_right_t(up_grad_low, back_up)
    hidden_part, hidden_gain_grad = norm_two_pull(normed_two_grad)
    hidden_grad = cotangent.astype(jnp.float32) + hidden_part
    branch_low = hidden_grad.astype(jnp.bfloat16)
    grad_mixer_out_full = dot_left_t(mixed_low, branch_low)
    norm_grad = dot_right_t(branch_low, back_mixer_out)
    (
        inner_grad_mix,
        in_grad_mix,
        out_grad,
        raw_grad_mix,
        gate_z_grad,
        bias_grad_mix,
        decay_grad_mix,
        skip_grad,
        mixer_gain_grad,
        start_grad,
    ) = mixer_pull(norm_grad)
    later_grad = entering_2(
        (carried, start_grad),
        "seq",
        chain_backward,
        (jnp.ones_like(carried), jnp.zeros_like(start_grad)),
    )[1]
    carried_grad = jnp.sum(later_grad * start_state, axis=(1, 2))
    inner_grad_st, in_grad_st, raw_grad_st, bias_grad_st, decay_grad_st = state_pull(
        (carried_grad, later_grad)
    )
    mixed_grad = jnp.concatenate(
        [
            (inner_grad_mix + inner_grad_st).reshape(row_count, INNER),
            in_grad_mix + in_grad_st,
            out_grad,
        ],
        axis=1,
    )
    ext_grad, conv_weight_grad, conv_bias_grad = conv_pull(mixed_grad)
    rim_send = jnp.where(seq_rank > 0, ext_grad[: CONV - 1], 0.0)
    rim_terms = lax.dynamic_update_slice_in_dim(
        jnp.zeros((seq_count * (CONV - 1), CHANNELS), jnp.float32), rim_send, rim_start, 0
    )
    grad_output_full = dot_left_t(attended_low, branch_low)
    attended_grad = (
        dot_right_t(branch_low, back_output)
        .astype(jnp.bfloat16)
        .reshape(row_count, KV_HEADS, group_size, HEAD_DIM)
    )
    prob_grad = jnp.einsum(
        "tkgd,skd->kgts", attended_grad, values_three, preferred_element_type=jnp.float32
    )
    inner_total = jnp.sum(probs * prob_grad, axis=-1, keepdims=True)
    score_grad = (probs * (prob_grad - inner_total)).astype(jnp.bfloat16)
    query_rot_grad = (
        jnp.einsum("kgts,skd->tkgd", score_grad, keys_three, preferred_element_type=jnp.float32)
        * score_scale
    )
    key_grad_all = (
        jnp.einsum("kgts,tkgd->skd", score_grad, grouped, preferred_element_type=jnp.float32)
        * score_scale
    )
    value_grad_all = jnp.einsum(
        "kgts,tkgd->skd", probs_low, attended_grad, preferred_element_type=jnp.float32
    )
    key_rot_grad, value_grad, rim_grad = (
        lax.psum_scatter(
            key_grad_all.reshape(seq_length, KV_HEADS * HEAD_DIM).astype(jnp.bfloat16),
            "seq",
            scatter_dimension=0,
            tiled=True,
        ).astype(jnp.float32),
        lax.psum_scatter(
            value_grad_all.reshape(seq_length, KV_HEADS * HEAD_DIM).astype(jnp.bfloat16),
            "seq",
            scatter_dimension=0,
            tiled=True,
        ).astype(jnp.float32),
        lax.psum_scatter(
            rim_terms.astype(jnp.bfloat16), "seq", scatter_dimension=0, tiled=True
        ).astype(jnp.float32),
    )
    conv_grad = ext_grad[CONV - 1 :] + jnp.concatenate(
        [jnp.zeros((row_count - CONV + 1, CHANNELS), jnp.float32), rim_grad]
    )
    proj_grad_low = jnp.concatenate(
        [gate_z_grad, conv_grad, raw_grad_mix + raw_grad_st], axis=1
    ).astype(jnp.bfloat16)
    grad_mixer_in_full = dot_left_t(normed_low, proj_grad_low)
    normed_grad = dot_right_t(proj_grad_low, back_mixer_in)
    query_grad_low = (
        rotate(query_rot_grad.reshape(row_count, HEADS, HEAD_DIM), places, -1.0)
        .reshape(row_count, HEADS * HEAD_DIM)
        .astype(jnp.bfloat16)
    )
    key_grad_low = (
        rotate(key_rot_grad.reshape(row_count, KV_HEADS, HEAD_DIM), places, -1.0)
        .reshape(row_count, KV_HEADS * HEAD_DIM)
        .astype(jnp.bfloat16)
    )
    value_grad_low = value_grad.astype(jnp.bfloat16)
    grad_query_full = dot_left_t(normed_low, query_grad_low)
    grad_key_full = dot_left_t(normed_low, key_grad_low)
    grad_value_full = dot_left_t(normed_low, value_grad_low)
    normed_grad = (
        normed_grad
        + dot_right_t(query_grad_low, back_query)
        + dot_right_t(key_grad_low, back_key)
        + dot_right_t(value_grad_low, back_value)
    )
    input_part, input_gain_grad = norm_pull(normed_grad)
    token_grad = hidden_grad + input_part
    reduced = (
        lax.psum_scatter(
            input_gain_grad.astype(jnp.bfloat16), "dp", scatter_dimension=0, tiled=True
        ).astype(jnp.float32),
        lax.psum_scatter(
            grad_mixer_in_full.astype(jnp.bfloat16), "dp", scatter_dimension=0, tiled=True
        ).astype(jnp.float32),
        lax.psum_scatter(
            conv_weight_grad.astype(jnp.bfloat16), "dp", scatter_dimension=0, tiled=True
        ).astype(jnp.float32),
        lax.psum_scatter(
            conv_bias_grad.astype(jnp.bfloat16), "dp", scatter_dimension=0, tiled=True
        ).astype(jnp.float32),
        lax.psum_scatter(
            mixer_gain_grad.astype(jnp.bfloat16), "dp", scatter_dimension=0, tiled=True
        ).astype(jnp.float32),
        lax.psum_scatter(
            grad_mixer_out_full.astype(jnp.bfloat16), "dp", scatter_dimension=0, tiled=True
        ).astype(jnp.float32),
        lax.psum_scatter(
            grad_query_full.astype(jnp.bfloat16), "dp", scatter_dimension=0, tiled=True
        ).astype(jnp.float32),
        lax.psum_scatter(
            grad_key_full.astype(jnp.bfloat16), "dp", scatter_dimension=0, tiled=True
        ).astype(jnp.float32),
        lax.psum_scatter(
            grad_value_full.astype(jnp.bfloat16), "dp", scatter_dimension=0, tiled=True
        ).astype(jnp.float32),
        lax.psum_scatter(
            grad_output_full.astype(jnp.bfloat16), "dp", scatter_dimension=0, tiled=True
        ).astype(jnp.float32),
        lax.psum_scatter(
            hidden_gain_grad.astype(jnp.bfloat16), "dp", scatter_dimension=0, tiled=True
        ).astype(jnp.float32),
        lax.psum_scatter(
            grad_gate_part.astype(jnp.bfloat16), "dp", scatter_dimension=0, tiled=True
        ).astype(jnp.float32),
        lax.psum_scatter(
            grad_up_part.astype(jnp.bfloat16), "dp", scatter_dimension=0, tiled=True
        ).astype(jnp.float32),
        lax.psum_scatter(
            grad_down_part.astype(jnp.bfloat16), "dp", scatter_dimension=0, tiled=True
        ).astype(jnp.float32),
    )
    shares = (
        lax.psum_scatter(
            reduced[0].astype(jnp.bfloat16), "seq", scatter_dimension=0, tiled=True
        ).astype(jnp.float32),
        lax.psum_scatter(
            reduced[1].astype(jnp.bfloat16), "seq", scatter_dimension=1, tiled=True
        ).astype(jnp.float32),
        lax.psum_scatter(
            reduced[2].astype(jnp.bfloat16), "seq", scatter_dimension=0, tiled=True
        ).astype(jnp.float32),
        lax.psum_scatter(
            reduced[3].astype(jnp.bfloat16), "seq", scatter_dimension=0, tiled=True
        ).astype(jnp.float32),
        lax.psum_scatter(
            reduced[4].astype(jnp.bfloat16), "seq", scatter_dimension=0, tiled=True
        ).astype(jnp.float32),
        lax.psum_scatter(
            reduced[5].astype(jnp.bfloat16), "seq", scatter_dimension=1, tiled=True
        ).astype(jnp.float32),
        lax.psum_scatter(
            reduced[6].astype(jnp.bfloat16), "seq", scatter_dimension=1, tiled=True
        ).astype(jnp.float32),
        lax.psum_scatter(
            reduced[7].astype(jnp.bfloat16), "seq", scatter_dimension=1, tiled=True
        ).astype(jnp.float32),
        lax.psum_scatter(
            reduced[8].astype(jnp.bfloat16), "seq", scatter_dimension=1, tiled=True
        ).astype(jnp.float32),
        lax.psum_scatter(
            reduced[9].astype(jnp.bfloat16), "seq", scatter_dimension=1, tiled=True
        ).astype(jnp.float32),
        lax.psum_scatter(
            reduced[10].astype(jnp.bfloat16), "seq", scatter_dimension=0, tiled=True
        ).astype(jnp.float32),
        lax.psum_scatter(
            reduced[11].astype(jnp.bfloat16), "seq", scatter_dimension=1, tiled=True
        ).astype(jnp.float32),
        lax.psum_scatter(
            reduced[12].astype(jnp.bfloat16), "seq", scatter_dimension=1, tiled=True
        ).astype(jnp.float32),
        lax.psum_scatter(
            reduced[13].astype(jnp.bfloat16), "seq", scatter_dimension=1, tiled=True
        ).astype(jnp.float32),
    )
    bias_total, decay_total, skip_total = lax.psum(
        (bias_grad_mix + bias_grad_st, decay_grad_mix + decay_grad_st, skip_grad), ("dp", "seq")
    )
    return (
        output,
        token_grad,
        shares[0],
        shares[1],
        shares[2],
        shares[3],
        bias_total,
        decay_total,
        skip_total,
        shares[4],
        shares[5],
        shares[6],
        shares[7],
        shares[8],
        shares[9],
        shares[10],
        shares[11],
        shares[12],
        shares[13],
    )


def solution(mesh):
    placed = (
        P(("dp", "seq"), None),
        P("dp", None),
        P(("dp", "seq")),
        P("dp", "seq"),
        P(("dp", "seq"), None),
        P(("dp", "seq")),
        P(),
        P(),
        P(),
        P(("dp", "seq")),
        P("dp", "seq"),
        P("dp", "seq"),
        P("dp", "seq"),
        P("dp", "seq"),
        P("dp", "seq"),
        P(("dp", "seq")),
        P("dp", "seq"),
        P("dp", "seq"),
        P("dp", "seq"),
        P(("dp", "seq"), None),
    )
    return jax.shard_map(
        shards,
        mesh=mesh,
        in_specs=placed,
        out_specs=(
            P(("dp", "seq"), None),
            P(("dp", "seq"), None),
            P(("dp", "seq")),
            P("dp", "seq"),
            P(("dp", "seq"), None),
            P(("dp", "seq")),
            P(),
            P(),
            P(),
            P(("dp", "seq")),
            P("dp", "seq"),
            P("dp", "seq"),
            P("dp", "seq"),
            P("dp", "seq"),
            P("dp", "seq"),
            P(("dp", "seq")),
            P("dp", "seq"),
            P("dp", "seq"),
            P("dp", "seq"),
        ),
        check_vma=False,
    )
```

profile of v0, /device:TPU:0, one launch (start us, length us, event | category | flops | bytes accessed | tf_op | source)
XLA Modules:
  0.0 1270.1 jit_solution(13247618687387682143)
XLA Ops:
  7.4 7.3 all_gather.137
  14.7 7.4 all-gather.2
  23.8 5.4 all_gather.153
  29.3 5.0 all_gather.139
  34.3 6.7 all_gather.157
  41.1 6.0 all_gather.159
  47.2 5.8 all_gather.161
  68.7 59.2 %all-reduce.33 = (bf16[1024]{0:T(1024)(128)(2,1)S(1)}, bf16[1792]{0:T(1024)(128)(2,1)S(1)}, bf16[1536]{0:T(1024)(128)(2,1)S(1)}, bf16[1024]{0:T(1024)(128)(2,1)S(1)}) all-reduce(bf16[1024]{0:T(1024)(128)(2,1)S(1)} %dynamic-update-slice.1, bf16[1792]{0:T(1024)(128)(2,1)S(1)} %dynamic-update-slice.3, ...), channel_id=1, replica_groups=mesh['dp'=16,'seq'=2] {'dp'}, use_global_device_ids=true, to_apply=%add.13 | all-reduce | flops 5376 | bytes 21504
  133.4 18.1 %all_gather.135 = bf16[1024,128]{1,0:T(8,128)(2,1)S(1)} all-gather(bf16[64,128]{1,0:T(8,128)(2,1)S(1)} %copy.193), channel_id=1, replica_groups=mesh['dp'=16,'seq'=2] {'dp'}, dimensions={0}, use_global_device_ids=true | all-gather | bytes 278528 | tf_op jit(solution)/shard_map/all_gather | solution.py:231
  153.9 6.4 all_gather.136
  165.4 20.1 %all_gather.132 = bf16[1024,128]{1,0:T(8,128)(2,1)S(1)} all-gather(bf16[64,128]{1,0:T(8,128)(2,1)S(1)} %copy.190), channel_id=1, replica_groups=mesh['dp'=16,'seq'=2] {'dp'}, dimensions={0}, use_global_device_ids=true | all-gather | bytes 278528 | tf_op jit(solution)/shard_map/all_gather | solution.py:232
  186.2 6.4 all_gather.133
  197.1 17.7 %all-gather.5 = bf16[16,112,4]{1,2,0:T(4,128)(2,1)S(1)} all-gather(bf16[1,112,4]{1,2,0:T(4,128)(2,1)S(1)} %reshape.589), channel_id=1, replica_groups=mesh['dp'=16,'seq'=2] {'dp'}, dimensions={0}, use_global_device_ids=true | all-gather | bytes 15232 | tf_op jit(solution)/shard_map/all_gather | solution.py:226
  217.4 7.4 fusion.26
  224.8 9.2 exponential_reduce_fusion
  234.1 9.3 convolution_convert_fusion.7
  243.4 6.7 fusion.152
  263.2 5.6 multiply_convert_fusion.3
  276.5 10.0 all-gather
  295.0 20.5 %fusion.34 = f32[512,24,64]{0,2,1:T(8,128)S(1)} fusion(f32[512,24,64]{0,2,1:T(8,128)S(1)} %bitcast.371, f32[512,24,64]{0,2,1:T(8,128)S(1)} %fusion.85, bf16[512,24,64]{0,2,1:T(8,128)(2,1)S(1)} %bitcast.388, f32[24,512]{1,0:T(8,128)S(1)} %copy-done.91, f32[512,512]{1,0:T(8,128)S(1)} %copy-done.41, f32[24,512]{1,0:T(8,128)S(1)} %copy-done.94, ...), kind=kOutput, calls=%fused_computation.80 | convolution fusion | flops 4866441216 | bytes 12468320 | tf_op jit(solution)/shard_map/jvp(hts,shp->thp)/dot_general | solution.py:145
  319.6 6.2 fusion.129
  330.7 6.8 fusion.153
  337.5 7.1 fusion.154
  344.6 17.7 %all-gather.27.cloned.1.call-done = bf16[2048,1024]{1,0:T(8,128)(2,1)} async-done(((bf16[128,1024]{1,0:T(8,128)(2,1)}), bf16[2048,1024]{1,0:T(8,128)(2,1)}) %all-gather.27.cloned.1.call-update) | async-done | bytes 4194320 | tf_op jit(solution)/shard_map/all_gather | solution.py:237
  362.4 9.6 multiply_convert_fusion
  375.5 5.8 multiply_reduce_fusion.12
  384.7 9.5 fusion.8
  394.2 5.9 fusion.72
  400.2 7.7 multiply_reduce_fusion.6
  407.9 8.4 fusion.10
  419.8 8.1 multiply_reduce_fusion.7
  436.5 8.2 reduce-scatter.32.cloned.1.call-done
  452.4 29.3 %fusion.12 = (f32[24,512]{1,0:T(8,128)}, f32[24,512]{1,0:T(8,128)}, f32[24,512]{1,0:T(8,128)}, f32[512,512]{1,0:T(8,128)}) fusion(f32[24,512]{1,0:T(8,128)S(1)} %copy-done.92, f32[512,512]{1,0:T(8,128)} %fusion.90, f32[24,512]{1,0:T(8,128)} %get-tuple-element.321, pred[512,512]{1,0:T(8,128)(4,1)S(1)} %copy-done.65, f32[24,64,512]{2,1,0:T(8,128)S(1)} %bitcast.374, ...), kind=kOutput, calls=%fused_computation.23 | convolution fusion | flops 4925911040 | bytes 7323648 | tf_op jit(solution)/shard_map/transpose(jvp(hts,shp->thp))/dot_general | solution.py:145
  491.1 11.5 all-gather.1
  516.5 24.1 %fusion.33 = f32[512,24,64]{0,2,1:T(8,128)S(1)} fusion(f32[512,24,64]{0,2,1:T(8,128)S(1)} %get-tuple-element.346, f32[512,24,64]{0,2,1:T(8,128)S(1)} %bitcast.379, f32[24,64,512]{2,1,0:T(8,128)S(1)} %bitcast.378, f32[24,512]{1,0:T(8,128)S(1)} %copy-done.93, f32[512,512]{1,0:T(8,128)S(1)} %copy-done.42, f32[24,512]{1,0:T(8,128)S(1)} %copy-done.95, ...), kind=kOutput, calls=%fused_computation.76 | convolution fusion | flops 4866441216 | bytes 14041184 | tf_op jit(solution)/shard_map/transpose(jvp(hts,shp->thp))/dot_general | solution.py:145
  540.7 6.9 multiply_reduce_fusion.5
  548.8 6.0 convolution_convert_fusion.3
  554.9 6.0 convolution_convert_fusion.2
  562.1 5.9 convolution_convert_fusion.1
  571.2 5.2 reduce-window.39
  580.5 5.0 reduce-window.35
  597.2 13.2 %all-reduce.20 = bf16[6,1792]{0,1:T(8,128)(2,1)S(1)} all-reduce(bf16[6,1792]{0,1:T(8,128)(2,1)S(1)} %dynamic_update_slice.3), channel_id=4, replica_groups=mesh['dp'=16,'seq'=2] {'seq'}, use_global_device_ids=true, to_apply=%region_16.18.clone | all-reduce | flops 10752 | bytes 43008
  611.8 8.9 pad_add_fusion
  622.7 10.2 convolution_convert_fusion
  640.9 41.4 %reduce-scatter.48.cloned.1.call-done = bf16[32,1024]{1,0:T(8,128)(2,1)} async-done(((bf16[512,1024]{1,0:T(8,128)(2,1)}), bf16[32,1024]{1,0:T(8,128)(2,1)}) %reduce-scatter.48.cloned.1.call-update) | async-done | bytes 65552 | tf_op jit(solution)/shard_map/reduce_scatter | solution.py:569
  682.4 9.6 fusion.63
  692.0 40.3 %all-reduce.31 = (f32[24]{0:T(128)}, f32[24]{0:T(128)}, f32[24]{0:T(128)}) all-reduce(f32[24]{0:T(128)S(1)} %add.354, f32[24]{0:T(128)S(1)} %add_multiply_fusion, f32[24]{0:T(128)S(1)} %reduce_sum.315), channel_id=1, replica_groups=mesh['dp'=16,'seq'=2] {'dp','seq'}, use_global_device_ids=true, to_apply=%region_48.50 | all-reduce | flops 72 | bytes 576 | tf_op jit(solution)/shard_map/psum | solution.py:629
  732.3 19.1 %reduce-scatter.36.cloned.1.call-done = bf16[96,1024]{1,0:T(8,128)(2,1)} async-done(((bf16[1536,1024]{1,0:T(8,128)(2,1)}), bf16[96,1024]{1,0:T(8,128)(2,1)}) %reduce-scatter.36.cloned.1.call-update) | async-done | bytes 196624 | tf_op jit(solution)/shard_map/reduce_scatter | solution.py:557
  751.5 6.2 add_convert_fusion
  757.7 50.1 %reduce-scatter.64.cloned.1.call-done = bf16[112,4]{1,0:T(8,128)(2,1)} async-done(((bf16[1792,4]{1,0:T(8,128)(2,1)}), bf16[112,4]{1,0:T(8,128)(2,1)}) %reduce-scatter.64.cloned.1.call-update) | async-done | bytes 912
  808.5 74.7 %reduce-scatter.52.cloned.1.call-done = bf16[64,2048]{1,0:T(8,128)(2,1)} async-done(((bf16[1024,2048]{1,0:T(8,128)(2,1)}), bf16[64,2048]{1,0:T(8,128)(2,1)}) %reduce-scatter.52.cloned.1.call-update) | async-done | bytes 262160 | tf_op jit(solution)/shard_map/reduce_scatter | solution.py:575
  887.9 71.2 %reduce-scatter.56.cloned.1.call-done = bf16[64,2048]{1,0:T(8,128)(2,1)} async-done(((bf16[1024,2048]{1,0:T(8,128)(2,1)}), bf16[64,2048]{1,0:T(8,128)(2,1)}) %reduce-scatter.56.cloned.1.call-update) | async-done | bytes 262160 | tf_op jit(solution)/shard_map/reduce_scatter | solution.py:578
  959.4 5.9 fusion.47
  965.4 59.3 %all-reduce.32 = (bf16[1024]{0:T(1024)(128)(2,1)S(1)}, bf16[1792]{0:T(1024)(128)(2,1)S(1)}, bf16[1536]{0:T(1024)(128)(2,1)S(1)}, bf16[1024]{0:T(1024)(128)(2,1)S(1)}) all-reduce(bf16[1024]{0:T(1024)(128)(2,1)S(1)} %get-tuple-element.236, bf16[1792]{0:T(1024)(128)(2,1)S(1)} %get-tuple-element.235, ...), channel_id=7, replica_groups=mesh['dp'=16,'seq'=2] {'dp'}, use_global_device_ids=true, to_apply=%region_33.35.clone | all-reduce | flops 5376 | bytes 21504
  1036.8 91.8 %reduce-scatter.34.cloned.1.call-done = bf16[64,3352]{1,0:T(8,128)(2,1)} async-done(((bf16[1024,3352]{1,0:T(8,128)(2,1)}), bf16[64,3352]{1,0:T(8,128)(2,1)}) %reduce-scatter.34.cloned.1.call-update) | async-done | bytes 429072 | tf_op jit(solution)/shard_map/reduce_scatter | solution.py:545
  1133.4 7.1 reduce-scatter.66.cloned.1.call-done
  1142.0 11.2 reduce-scatter.68.cloned.1.call-done
  1154.6 10.7 reduce-scatter.42.cloned.1.call-done
  1166.6 10.7 reduce-scatter.50.cloned.1.call-done
  1178.8 11.7 reduce-scatter.38.cloned.1.call-done
  1192.0 12.4 reduce-scatter.54.cloned.1.call-done
  1206.0 12.2 reduce-scatter.58.cloned.1.call-done
  1219.9 12.1 reduce-scatter.62.cloned.1.call-done
  1233.6 27.6 %all-reduce.38.cloned.1.call-done = bf16[64,3352]{1,0:T(8,128)(2,1)} async-done(((bf16[64,3352]{1,0:T(8,128)(2,1)}), bf16[64,3352]{1,0:T(8,128)(2,1)}) %all-reduce.38.cloned.1.call-update) | async-done | bytes 429072
  (574 shorter events, 188.8 us)
Async XLA Ops:
  7.2 50.2 %copy-start.134 = (u32[32]{0:T(128)S(1)}, u32[32]{0:T(128)}, u32[]{:S(2)}) copy-start(u32[32]{0:T(128)} %constant.179) | copy-start | bytes 388
  7.2 50.2 %copy-start.135 = (u32[32]{0:T(128)S(1)}, u32[32]{0:T(128)}, u32[]{:S(2)}) copy-start(u32[32]{0:T(128)} %constant.184) | copy-start | bytes 388
  7.3 45.8 %copy-start.75 = (s32[1,1024]{1,0:T(1,128)S(1)}, s32[1,1024]{1,0:T(1,128)}, u32[]{:S(2)}) copy-start(s32[1,1024]{1,0:T(1,128)} %param.26) | copy-start | bytes 12292
  7.3 54.6 %copy-start.142 = (bf16[32]{0:T(256)(128)(2,1)S(1)}, bf16[32]{0:T(256)(128)(2,1)}, u32[]{:S(2)}) copy-start(bf16[32]{0:T(256)(128)(2,1)} %param.27) | copy-start | bytes 196
  7.3 54.9 %copy-start.143 = (bf16[32]{0:T(256)(128)(2,1)S(1)}, bf16[32]{0:T(256)(128)(2,1)}, u32[]{:S(2)}) copy-start(bf16[32]{0:T(256)(128)(2,1)} %param.40) | copy-start | bytes 196
  7.3 55.1 %copy-start.144 = (bf16[56]{0:T(256)(128)(2,1)S(1)}, bf16[56]{0:T(256)(128)(2,1)}, u32[]{:S(2)}) copy-start(bf16[56]{0:T(256)(128)(2,1)} %param.30) | copy-start | bytes 340
  7.3 55.3 %copy-start.145 = (bf16[48]{0:T(256)(128)(2,1)S(1)}, bf16[48]{0:T(256)(128)(2,1)}, u32[]{:S(2)}) copy-start(bf16[48]{0:T(256)(128)(2,1)} %param.34) | copy-start | bytes 292
  7.3 120.6 %copy-start.18 = (bf16[512,1024]{1,0:T(8,128)(2,1)S(1)}, bf16[512,1024]{1,0:T(8,128)(2,1)}, u32[]{:S(2)}) copy-start(bf16[512,1024]{1,0:T(8,128)(2,1)} %param.25) | copy-start | bytes 3145732
  7.3 207.8 %all-gather.15.cloned.1.call-start = ((), (), s32[]{:S(2)}) async-start(), calls=%async_computation.20 | async-start | bytes 1114112 | tf_op jit(solution)/shard_map/all_gather | solution.py:230
  14.7 228.7 %all-gather.19.cloned.1.call-start = ((), (), s32[]{:S(2)}) async-start(), calls=%async_computation.22 | async-start | bytes 7520256 | tf_op jit(solution)/shard_map/all_gather | solution.py:225
  22.1 106.7 %copy-start.115 = (bf16[64,64]{1,0:T(8,128)(2,1)S(1)}, bf16[64,64]{1,0:T(8,128)(2,1)}, u32[]{:S(2)}) copy-start(bf16[64,64]{1,0:T(8,128)(2,1)} %param.37) | copy-start | bytes 24580
  23.7 295.9 %all-gather.21.cloned.1.call-start = ((), (), s32[]{:S(2)}) async-start(), calls=%async_computation.23 | async-start | bytes 3342336 | tf_op jit(solution)/shard_map/all_gather | solution.py:229
  29.2 296.6 %all-gather.17.cloned.1.call-start = ((), (), s32[]{:S(2)}) async-start(), calls=%async_computation.21 | async-start | bytes 1114112 | tf_op jit(solution)/shard_map/all_gather | solution.py:233
  34.3 296.4 %all-gather.23.cloned.1.call-start = ((), (), s32[]{:S(2)}) async-start(), calls=%async_computation.24 | async-start | bytes 4456448 | tf_op jit(solution)/shard_map/all_gather | solution.py:235
  41.1 296.4 %all-gather.25.cloned.1.call-start = ((), (), s32[]{:S(2)}) async-start(), calls=%async_computation.25 | async-start | bytes 4456448 | tf_op jit(solution)/shard_map/all_gather | solution.py:236
  47.1 315.2 %all-gather.27.cloned.1.call-start = ((), (), s32[]{:S(2)}) async-start(), calls=%async_computation.26 | async-start | bytes 4456448 | tf_op jit(solution)/shard_map/all_gather | solution.py:237
  52.9 107.8 %copy-start.116 = (bf16[64,64]{1,0:T(8,128)(2,1)S(1)}, bf16[64,64]{1,0:T(8,128)(2,1)}, u32[]{:S(2)}) copy-start(bf16[64,64]{1,0:T(8,128)(2,1)} %param.38) | copy-start | bytes 24580
  52.9 377.7 %reduce-scatter.30.cloned.1.call-start = ((), (), s32[]{:S(2)}) async-start(), calls=%async_computation.27 | async-start | bytes 393216 | tf_op jit(solution)/shard_map/reduce_scatter | solution.py:495
  53.9 209.2 %copy-start.117 = (pred[512]{0:T(512)(128)(4,1)}, pred[512]{0:T(512)(128)(4,1)S(1)}, u32[]{:S(2)}) copy-start(pred[512]{0:T(512)(128)(4,1)S(1)} %get-tuple-element.323) | copy-start | bytes 1540
  53.9 209.2 %copy-start.119 = (pred[512]{0:T(512)(128)(4,1)}, pred[512]{0:T(512)(128)(4,1)S(1)}, u32[]{:S(2)}) copy-start(pred[512]{0:T(512)(128)(4,1)S(1)} %get-tuple-element.324) | copy-start | bytes 1540
  53.9 209.2 %copy-start.121 = (pred[512]{0:T(512)(128)(4,1)}, pred[512]{0:T(512)(128)(4,1)S(1)}, u32[]{:S(2)}) copy-start(pred[512]{0:T(512)(128)(4,1)S(1)} %get-tuple-element.325) | copy-start | bytes 1540
  57.1 204.9 %copy-start.127 = (pred[512]{0:T(512)(128)(4,1)}, pred[512]{0:T(512)(128)(4,1)S(1)}, u32[]{:S(2)}) copy-start(pred[512]{0:T(512)(128)(4,1)S(1)} %get-tuple-element.330) | copy-start | bytes 1540
  57.1 204.9 %copy-start.129 = (pred[512]{0:T(512)(128)(4,1)}, pred[512]{0:T(512)(128)(4,1)S(1)}, u32[]{:S(2)}) copy-start(pred[512]{0:T(512)(128)(4,1)S(1)} %get-tuple-element.329) | copy-start | bytes 1540
  57.4 237.5 %copy-start.64 = (pred[512,512]{1,0:T(8,128)(4,1)}, pred[512,512]{1,0:T(8,128)(4,1)S(1)}, u32[]{:S(2)}) copy-start(pred[512,512]{1,0:T(8,128)(4,1)S(1)} %fusion.79) | copy-start | bytes 786436
  127.9 115.5 %copy-start.98 = (f32[1024]{0:T(1024)}, f32[1024]{0:T(1024)S(1)}, u32[]{:S(2)}) copy-start(f32[1024]{0:T(1024)S(1)} %convert_element_type.293) | copy-start | bytes 12292
  128.8 114.7 %copy-start.113 = (f32[512]{0:T(512)}, f32[512]{0:T(512)S(1)}, u32[]{:S(2)}) copy-start(f32[512]{0:T(512)S(1)} %fusion.115) | copy-start | bytes 6148
  153.2 64.0 %copy-start.34 = (f32[512,32]{0,1:T(8,128)}, f32[512,32]{0,1:T(8,128)S(1)}, u32[]{:S(2)}) copy-start(f32[512,32]{0,1:T(8,128)S(1)} %get-tuple-element.328) | copy-start | bytes 196612
  160.3 57.1 %copy-start.46 = (bf16[1024,128]{0,1:T(8,128)(2,1)}, bf16[1024,128]{0,1:T(8,128)(2,1)S(1)}, u32[]{:S(2)}) copy-start(bf16[1024,128]{0,1:T(8,128)(2,1)S(1)} %all_gather.136) | copy-start | bytes 786436
  160.8 73.3 %copy-start.21 = (pred[512,1024]{0,1:T(8,128)(4,1)}, pred[512,1024]{0,1:T(8,128)(4,1)S(1)}, u32[]{:S(2)}) copy-start(pred[512,1024]{0,1:T(8,128)(4,1)S(1)} %fusion.53) | copy-start | bytes 1572868
  192.7 41.3 %copy-start.38 = (bf16[1024,128]{0,1:T(8,128)(2,1)}, bf16[1024,128]{0,1:T(8,128)(2,1)S(1)}, u32[]{:S(2)}) copy-start(bf16[1024,128]{0,1:T(8,128)(2,1)S(1)} %copy.191) | copy-start | bytes 786436
  192.8 57.7 %copy-start.132 = (f32[24]{0:T(128)}, f32[24]{0:T(128)S(1)}, u32[]{:S(2)}) copy-start(f32[24]{0:T(128)S(1)} %exp.47) | copy-start | bytes 292
  215.0 48.1 %copy-start.78 = (f32[1792]{0:T(1024)}, f32[1792]{0:T(1024)S(1)}, u32[]{:S(2)}) copy-start(f32[1792]{0:T(1024)S(1)} %get-tuple-element.238) | copy-start | bytes 21508
  215.0 48.1 %copy-start.80 = (f32[1792]{0:T(1024)}, f32[1792]{0:T(1024)S(1)}, u32[]{:S(2)}) copy-start(f32[1792]{0:T(1024)S(1)} %get-tuple-element.239) | copy-start | bytes 21508
  215.0 48.1 %copy-start.82 = (f32[1792]{0:T(1024)}, f32[1792]{0:T(1024)S(1)}, u32[]{:S(2)}) copy-start(f32[1792]{0:T(1024)S(1)} %get-tuple-element.240) | copy-start | bytes 21508
  215.0 48.1 %copy-start.84 = (f32[1792]{0:T(1024)}, f32[1792]{0:T(1024)S(1)}, u32[]{:S(2)}) copy-start(f32[1792]{0:T(1024)S(1)} %get-tuple-element.241) | copy-start | bytes 21508
  215.1 114.6 %copy-start.87 = (f32[1024]{0:T(1024)}, f32[1024]{0:T(1024)S(1)}, u32[]{:S(2)}) copy-start(f32[1024]{0:T(1024)S(1)} %convert_element_type.310) | copy-start | bytes 12292
  419.8 24.9 %reduce-scatter.32.cloned.1.call-start = ((), (), s32[]{:S(2)}) async-start(), calls=%async_computation.28 | async-start | bytes 393216 | tf_op jit(solution)/shard_map/reduce_scatter | solution.py:501
  428.0 55.5 %copy-start.6 = (f32[512,1536]{0,1:T(8,128)}, f32[512,1536]{0,1:T(8,128)S(1)}, u32[]{:S(2)}) copy-start(f32[512,1536]{0,1:T(8,128)S(1)} %get-tuple-element.283) | copy-start | bytes 9437188
  430.6 202.5 %reduce-scatter.44.cloned.1.call-start = ((), (), s32[]{:S(2)}) async-start(), calls=%async_computation.34 | async-start | bytes 278528 | tf_op jit(solution)/shard_map/reduce_scatter | solution.py:563
  434.4 200.2 %reduce-scatter.46.cloned.1.call-start = ((), (), s32[]{:S(2)}) async-start(), calls=%async_computation.35 | async-start | bytes 278528 | tf_op jit(solution)/shard_map/reduce_scatter | solution.py:566
  447.3 193.5 %reduce-scatter.40.cloned.1.call-start = ((), (), s32[]{:S(2)}) async-start(), calls=%async_computation.32 | async-start | bytes 1114112 | tf_op jit(solution)/shard_map/reduce_scatter | solution.py:560
  452.4 230.0 %reduce-scatter.48.cloned.1.call-start = ((), (), s32[]{:S(2)}) async-start(), calls=%async_computation.36 | async-start | bytes 1114112 | tf_op jit(solution)/shard_map/reduce_scatter | solution.py:569
  491.1 260.3 %reduce-scatter.36.cloned.1.call-start = ((), (), s32[]{:S(2)}) async-start(), calls=%async_computation.30 | async-start | bytes 3342336 | tf_op jit(solution)/shard_map/reduce_scatter | solution.py:557
  503.0 304.7 %reduce-scatter.64.cloned.1.call-start = ((), (), s32[]{:S(2)}) async-start(), calls=%async_computation.44 | async-start | bytes 487424
  548.8 334.5 %reduce-scatter.52.cloned.1.call-start = ((), (), s32[]{:S(2)}) async-start(), calls=%async_computation.38 | async-start | bytes 4456448 | tf_op jit(solution)/shard_map/reduce_scatter | solution.py:575
  554.8 404.3 %reduce-scatter.56.cloned.1.call-start = ((), (), s32[]{:S(2)}) async-start(), calls=%async_computation.40 | async-start | bytes 4456448 | tf_op jit(solution)/shard_map/reduce_scatter | solution.py:578
  560.9 474.0 %reduce-scatter.60.cloned.1.call-start = ((), (), s32[]{:S(2)}) async-start(), calls=%async_computation.42 | async-start | bytes 4456448 | tf_op jit(solution)/shard_map/reduce_scatter | solution.py:581
  568.1 560.5 %reduce-scatter.34.cloned.1.call-start = ((), (), s32[]{:S(2)}) async-start(), calls=%async_computation.29 | async-start | bytes 7520256 | tf_op jit(solution)/shard_map/reduce_scatter | solution.py:545
  633.0 507.6 %reduce-scatter.66.cloned.1.call-start = ((), (), s32[]{:S(2)}) async-start(), calls=%async_computation.45 | async-start | bytes 49152
  634.5 518.6 %reduce-scatter.68.cloned.1.call-start = ((), (), s32[]{:S(2)}) async-start(), calls=%async_computation.46 | async-start | bytes 49152
  636.0 529.2 %reduce-scatter.42.cloned.1.call-start = ((), (), s32[]{:S(2)}) async-start(), calls=%async_computation.33 | async-start | bytes 98304 | tf_op jit(solution)/shard_map/reduce_scatter | solution.py:604
  640.9 536.5 %reduce-scatter.50.cloned.1.call-start = ((), (), s32[]{:S(2)}) async-start(), calls=%async_computation.37 | async-start | bytes 98304 | tf_op jit(solution)/shard_map/reduce_scatter | solution.py:613
  682.4 69.1 %copy-start.10 = (f32[512,1024]{1,0:T(8,128)S(1)}, f32[512,1024]{1,0:T(8,128)}, u32[]{:S(2)}) copy-start(f32[512,1024]{1,0:T(8,128)} %copy-done.8) | copy-start | bytes 6291460
  682.4 508.1 %reduce-scatter.38.cloned.1.call-start = ((), (), s32[]{:S(2)}) async-start(), calls=%async_computation.31 | async-start | bytes 294912 | tf_op jit(solution)/shard_map/reduce_scatter | solution.py:601
  751.4 131.9 %copy-start.44 = (bf16[1024,128]{1,0:T(8,128)(2,1)S(1)}, bf16[1024,128]{1,0:T(8,128)(2,1)}, u32[]{:S(2)}) copy-start(bf16[1024,128]{1,0:T(8,128)(2,1)} %copy-done.43) | copy-start | bytes 786436
  751.4 131.9 %copy-start.59 = (bf16[512,2,64]{0,2,1:T(8,128)(2,1)S(1)}, bf16[512,2,64]{0,2,1:T(8,128)(2,1)}, u32[]{:S(2)}) copy-start(bf16[512,2,64]{0,2,1:T(8,128)(2,1)} %copy-done.58) | copy-start | bytes 393220
  751.4 452.9 %reduce-scatter.54.cloned.1.call-start = ((), (), s32[]{:S(2)}) async-start(), calls=%async_computation.39 | async-start | bytes 393216 | tf_op jit(solution)/shard_map/reduce_scatter | solution.py:619
  883.3 335.0 %reduce-scatter.58.cloned.1.call-start = ((), (), s32[]{:S(2)}) async-start(), calls=%async_computation.41 | async-start | bytes 393216 | tf_op jit(solution)/shard_map/reduce_scatter | solution.py:622
  959.2 77.6 %copy-start.110 = (f32[512]{0:T(512)S(1)}, f32[512]{0:T(512)}, u32[]{:S(2)}) copy-start(f32[512]{0:T(512)} %copy-done.109) | copy-start | bytes 6148
  959.2 169.4 %copy-start.89 = (f32[1024]{0:T(1024)S(1)}, f32[1024]{0:T(1024)}, u32[]{:S(2)}) copy-start(f32[1024]{0:T(1024)} %copy-done.87) | copy-start | bytes 12292
  959.2 169.4 %copy-start.104 = (f32[512]{0:T(512)S(1)}, f32[512]{0:T(512)}, u32[]{:S(2)}) copy-start(f32[512]{0:T(512)} %copy-done.102) | copy-start | bytes 6148
  959.2 169.4 %copy-start.108 = (f32[512]{0:T(512)S(1)}, f32[512]{0:T(512)}, u32[]{:S(2)}) copy-start(f32[512]{0:T(512)} %copy-done.107) | copy-start | bytes 6148
  959.2 272.8 %reduce-scatter.62.cloned.1.call-start = ((), (), s32[]{:S(2)}) async-start(), calls=%async_computation.43 | async-start | bytes 393216 | tf_op jit(solution)/shard_map/reduce_scatter | solution.py:625
  1034.9 226.4 %all-reduce.38.cloned.1.call-start = ((), (), s32[]{:S(2)}) async-start(), calls=%async_computation.47 | async-start | bytes 884736
  (121 other events, 1060.2 us)
Sparse Core Ops, SparseCore 0:
  14.8 38.4 all-gather.14
  56.1 66.3 all-gather.18
  124.8 44.8 all-gather.20
  171.7 36.5 all-gather.16
  210.3 49.4 all-gather.22
  261.8 49.0 all-gather.24
  313.1 49.1 all-gather.26
  419.9 10.1 reduce-scatter.29
  433.0 11.6 reduce-scatter.31
  448.0 55.2 reduce-scatter.43
  507.5 54.3 reduce-scatter.45
  565.3 56.4 reduce-scatter.39
  625.8 56.4 reduce-scatter.47
  686.0 65.3 reduce-scatter.35
  755.3 52.4 reduce-scatter.63
  811.4 71.7 reduce-scatter.51
  887.4 71.6 reduce-scatter.55
  962.8 71.9 reduce-scatter.59
  1039.4 89.1 reduce-scatter.33
  1131.2 9.2 reduce-scatter.65
  1143.3 9.8 reduce-scatter.67
  1155.3 9.8 reduce-scatter.41
  1167.4 9.8 reduce-scatter.49
  1179.4 10.9 reduce-scatter.37
  1192.7 11.6 reduce-scatter.53
  1206.5 11.6 reduce-scatter.57
  1220.3 11.6 reduce-scatter.61
  1234.4 26.7 all-reduce.37
where the time goes:
time: 1280 us; the launch traced here: 1270 us
  waiting for transfers between devices  494 us (39%)
  blocking collectives  337 us (26%)
  matrix products  261 us (20%)
  other arithmetic  114 us (9%)
  local copies, waits for them, and re-layouts  34.5 us (3%)
  between operations  27.4 us (2%)
    unnamed x5, blocking collectives  142 us
    unnamed x32, waiting for transfers between devices  96.4 us
    reduce_scatter x1, waiting for transfers between devices, shards(): lax.psum_scatter(grad_mixer_in_full.astype(jnp.bfloat16), 'dp', scatter_d...  91.8 us
    reduce_scatter x1, waiting for transfers between devices, shards(): lax.psum_scatter(grad_gate_part.astype(jnp.bfloat16), 'dp', scatter_dimen...  74.7 us
    dot_general x3, matrix products, block_mix(): local_part = jnp.einsum('hts,shp->thp', weights_mat, inner, precision=HIGH)  73.9 us
    reduce_scatter x1, waiting for transfers between devices, shards(): lax.psum_scatter(grad_up_part.astype(jnp.bfloat16), 'dp', scatter_dimensi...  71.2 us
    dot_general x9, matrix products, dot_right_t(): lax.dot_general(left, right, (((1,), (1,)), ((), ())), preferred_element_...  46.2 us
    dot_general x9, matrix products, dot_left_t(): lax.dot_general(left, right, (((0,), (0,)), ((), ())), preferred_element_...  43 us
  transfers between devices with their start and end apart: 28, of which 18 were waited for; matrix products, arithmetic and copies ran while one was open for 27% of the time, Pallas kernels for 0%

commit v1 on v0

--- a/solution.py
+++ b/solution.py
@@ -1,6 +1,8 @@
 import jax
 import jax.numpy as jnp
 from jax import lax
+from jax.experimental import pallas as pl
+from jax.experimental.pallas import tpu as pltpu
 from jax.sharding import PartitionSpec as P
 
 HEADS = 8
@@ -182,7 +184,7 @@
     return (gate_grad_low, up_grad_low)
 
 
-def shards(
+def shards_general(
     tokens,
     segments,
     input_gain,
@@ -652,6 +654,834 @@
     )
 
 
+def ring(value, axis, stride, size):
+    count = lax.axis_size(axis)
+    pairs = []
+    for place in range(count):
+        own = place // stride % size
+        pairs.append((place, place + ((own + 1) % size - own) * stride))
+    return lax.ppermute(value, axis, pairs)
+
+
+def own_place(axis, stride, size):
+    return lax.axis_index(axis) // stride % size
+
+
+def in_order(parts, own, dim):
+    size = len(parts)
+    if size == 2:
+        return jnp.where(
+            own == 0,
+            jnp.concatenate(parts, axis=dim),
+            jnp.concatenate(parts[::-1], axis=dim),
+        )
+    ahead = [parts[-k % size] for k in range(size)] * 2
+    width = parts[0].shape[dim]
+    return lax.dynamic_slice_in_dim(
+        jnp.concatenate(ahead, axis=dim), (size - own) % size * width, size * width, dim
+    )
+
+
+def gather_stage(value, axis, stride, size, dim):
+    parts = [value]
+    for _ in range(size - 1):
+        parts.append(ring(parts[-1], axis, stride, size))
+    return in_order(parts, own_place(axis, stride, size), dim)
+
+
+def dp_factors():
+    count = lax.axis_size("dp")
+    core = 2
+    row = 4 if count > 16 else 2
+    return core, row, count // (core * row)
+
+
+def gather_weight(piece, seq_last):
+    core, row, far = dp_factors()
+    rows, columns = piece.shape
+    value = piece.reshape(1, 1, 1, rows, columns)
+    value = gather_stage(value, "dp", core * row, far, 0)
+    if seq_last:
+        value = gather_stage(value, "dp", core, row, 1)
+        value = gather_stage(value, "seq", 1, lax.axis_size("seq"), 4)
+    else:
+        value = gather_stage(value, "seq", 1, lax.axis_size("seq"), 4)
+        value = gather_stage(value, "dp", core, row, 1)
+    value = gather_stage(value, "dp", 1, core, 2)
+    return value.reshape(far * row * core, rows, value.shape[-1])
+
+
+def pick(value, index, size, dim):
+    width = value.shape[dim] // size
+    if size == 2:
+        return jnp.where(
+            index == 0,
+            lax.slice_in_dim(value, 0, width, axis=dim),
+            lax.slice_in_dim(value, width, 2 * width, axis=dim),
+        )
+    return lax.dynamic_slice_in_dim(value, index * width, width, dim)
+
+
+def scatter_stage(value, axis, stride, size, dim):
+    own = own_place(axis, stride, size)
+    moving = pick(value, (own + size - 1) % size, size, dim).astype(jnp.bfloat16)
+    for step in range(2, size + 1):
+        moving = ring(moving, axis, stride, size)
+        mine = pick(value, (own + size - step) % size, size, dim)
+        total = mine.astype(jnp.float32) + moving.astype(jnp.float32)
+        moving = total.astype(jnp.bfloat16)
+    return total
+
+
+def scatter_weight(grad, seq_first):
+    core, row, far = dp_factors()
+    rows = grad.shape[0] // (core * row * far)
+    value = grad.reshape(far, row, core, rows, grad.shape[1])
+    value = scatter_stage(value, "dp", 1, core, 2).astype(jnp.bfloat16)
+    if seq_first:
+        value = scatter_stage(value, "seq", 1, lax.axis_size("seq"), 4).astype(jnp.bfloat16)
+        value = scatter_stage(value, "dp", core, row, 1).astype(jnp.bfloat16)
+    else:
+        value = scatter_stage(value, "dp", core, row, 1).astype(jnp.bfloat16)
+        value = scatter_stage(value, "seq", 1, lax.axis_size("seq"), 4).astype(jnp.bfloat16)
+    value = scatter_stage(value, "dp", core * row, far, 0)
+    return value.reshape(rows, value.shape[-1])
+
+
+def scatter_small(parts):
+    core, row, far = dp_factors()
+    seq = lax.axis_size("seq")
+    value = parts.reshape(far, row, core, seq, parts.shape[-1])
+    for axis, stride, size, dim in (
+        ("dp", 1, core, 2),
+        ("seq", 1, seq, 3),
+        ("dp", core, row, 1),
+        ("dp", core * row, far, 0),
+    ):
+        own = own_place(axis, stride, size)
+        moving = pick(value, (own + size - 1) % size, size, dim)
+        for step in range(2, size + 1):
+            moving = ring(moving, axis, stride, size) + pick(
+                value, (own + size - step) % size, size, dim
+            )
+        value = moving
+    return value.reshape(-1)
+
+
+CHUNK = 64
+PAIR = 128
+
+
+def dot_high(left, right):
+    return jnp.dot(left, right, precision=HIGH, preferred_element_type=jnp.float32)
+
+
+def first_lanes(rows):
+    return lax.broadcasted_iota(jnp.int32, (rows, PAIR), 1) < PAIR // 2
+
+
+def turn(value, cosine, sine):
+    half = HEAD_DIM // 2
+    lane = lax.broadcasted_iota(jnp.int32, value.shape, 1)
+    other = jnp.where(
+        lane % HEAD_DIM < half,
+        pltpu.roll(value, PAIR - half, 1),
+        pltpu.roll(value, half, 1),
+    )
+    return value * cosine + other * sine
+
+
+def twice(value):
+    rolled = pltpu.roll(value, PAIR // 2, 1)
+    low_half = first_lanes(value.shape[0])
+    return jnp.where(low_half, value, rolled), jnp.where(low_half, rolled, value)
+
+
+def stacked(pairs):
+    low_half = first_lanes(pairs[0].shape[0])
+    parts = []
+    for pair in pairs:
+        parts.append(jnp.where(low_half, pair, 0.0))
+        parts.append(jnp.where(low_half, 0.0, pair))
+    return jnp.concatenate(parts, axis=0).astype(jnp.bfloat16)
+
+
+def softmax_block(queries, keys, seg_col, seg_row, first_row):
+    rows, wide = seg_col.shape[0], keys.shape[0]
+    scores = dot_right_t(queries, keys) * HEAD_DIM ** (-0.5)
+    query_at = lax.broadcasted_iota(jnp.int32, (rows, wide), 0) + first_row
+    key_at = lax.broadcasted_iota(jnp.int32, (rows, wide), 1)
+    allowed = (seg_col == seg_row[:, :wide]) & (key_at <= query_at)
+    offset = jnp.where(allowed, 0.0, -1e30)
+    scores = scores + jnp.concatenate([offset] * (queries.shape[0] // rows), axis=0)
+    scores = jnp.exp(scores - jnp.max(scores, axis=1, keepdims=True))
+    return scores / jnp.sum(scores, axis=1, keepdims=True)
+
+
+def attention_forward(part_ref, cos_ref, sin_ref, seg_col_ref, seg_row_ref, turned_ref, out_ref):
+    count, row_count = part_ref.shape[0], out_ref.shape[0]
+    halo = count - row_count
+    block = min(row_count, 128)
+    cosine, sine = cos_ref[...], sin_ref[...]
+    seg_row = seg_row_ref[...]
+    group = HEADS // KV_HEADS * HEAD_DIM
+    for kv_head in range(KV_HEADS):
+        base = kv_head * (group + 2 * HEAD_DIM)
+        for at in range(base, base + group, PAIR):
+            turned_ref[:, at : at + PAIR] = turn(part_ref[:, at : at + PAIR], cosine, sine).astype(
+                jnp.bfloat16
+            )
+        at = base + group
+        both = part_ref[:, at : at + PAIR]
+        both = jnp.where(first_lanes(count), turn(both, cosine, sine), both).astype(jnp.bfloat16)
+        turned_ref[:, at : at + PAIR] = both
+        keys, values = twice(both.astype(jnp.float32))
+        keys, values = keys.astype(jnp.bfloat16), values.astype(jnp.bfloat16)
+        for start in range(0, row_count, block):
+            first = halo + start
+            queries = stacked(
+                [
+                    turned_ref[first : first + block, at : at + PAIR].astype(jnp.float32)
+                    for at in range(base, base + group, PAIR)
+                ]
+            )
+            wide = first + block
+            probs = softmax_block(
+                queries, keys[:wide], seg_col_ref[first : first + block], seg_row, first
+            ).astype(jnp.bfloat16)
+            result = dot_plain(probs, values[:wide])
+            low_half = first_lanes(block)
+            for k in range(group // PAIR):
+                pair = jnp.where(
+                    low_half,
+                    result[2 * k * block : (2 * k + 1) * block],
+                    result[(2 * k + 1) * block : (2 * k + 2) * block],
+                )
+                at = kv_head * group + k * PAIR
+                out_ref[start : start + block, at : at + PAIR] = pair.astype(jnp.bfloat16)
+
+
+def attention_backward(
+    turned_ref, grad_ref, cos_ref, sin_ref, seg_col_ref, seg_row_ref, out_ref, key_ref, value_ref
+):
+    count, row_count = turned_ref.shape[0], grad_ref.shape[0]
+    halo = count - row_count
+    block = min(row_count, 128)
+    cosine, sine = cos_ref[...], sin_ref[...]
+    seg_row = seg_row_ref[...]
+    group = HEADS // KV_HEADS * HEAD_DIM
+    scale = HEAD_DIM ** (-0.5)
+    for kv_head in range(KV_HEADS):
+        base = kv_head * (group + 2 * HEAD_DIM)
+        at = base + group
+        keys, values = twice(turned_ref[:, at : at + PAIR].astype(jnp.float32))
+        keys, values = keys.astype(jnp.bfloat16), values.astype(jnp.bfloat16)
+        key_ref[...] = jnp.zeros_like(key_ref)
+        value_ref[...] = jnp.zeros_like(value_ref)
+        for start in range(0, row_count, block):
+            first = halo + start
+            queries = stacked(
+                [
+                    turned_ref[first : first + block, at : at + PAIR].astype(jnp.float32)
+                    for at in range(base, base + group, PAIR)
+                ]
+            )
+            grads = stacked(
+                [
+                    grad_ref[
+                        start : start + block, kv_head * group + at : kv_head * group + at + PAIR
+                    ].astype(jnp.float32)
+                    for at in range(0, group, PAIR)
+                ]
+            )
+            wide = first + block
+            probs = softmax_block(
+                queries, keys[:wide], seg_col_ref[first : first + block], seg_row, first
+            )
+            prob_grad = dot_right_t(grads, values[:wide])
+            mean = jnp.sum(probs * prob_grad, axis=1, keepdims=True)
+            score_grad = (probs * (prob_grad - mean)).astype(jnp.bfloat16)
+            result = dot_plain(score_grad, keys[:wide]) * scale
+            key_ref[:wide] += dot_left_t(score_grad, queries)
+            value_ref[:wide] += dot_left_t(probs.astype(jnp.bfloat16), grads)
+            low_half = first_lanes(block)
+            for k in range(group // PAIR):
+                pair = jnp.where(
+                    low_half,
+                    result[2 * k * block : (2 * k + 1) * block],
+                    result[(2 * k + 1) * block : (2 * k + 2) * block],
+                )
+                pair = turn(
+                    pair, cosine[first : first + block], -sine[first : first + block]
+                )
+                out_ref[first : first + block, base + k * PAIR : base + (k + 1) * PAIR] = (
+                    pair.astype(jnp.bfloat16)
+                )
+        key_grad, value_grad = key_ref[...], value_ref[...]
+        key_grad = (key_grad + pltpu.roll(key_grad, PAIR // 2, 1)) * scale
+        value_grad = value_grad + pltpu.roll(value_grad, PAIR // 2, 1)
+        both = jnp.where(first_lanes(count), turn(key_grad, cosine, -sine), value_grad)
+        out_ref[:, at : at + PAIR] = both.astype(jnp.bfloat16)
+        out_ref[:halo, base : base + group] = jnp.zeros((halo, group), jnp.bfloat16)
+
+
+def load_conv(proj_ref, conv_ref):
+    count = proj_ref.shape[0]
+    conv_ref[:8] = jnp.zeros((8, CHANNELS), jnp.float32)
+    conv_ref[8 : count + 8] = (
+        proj_ref[:, INNER : INNER + CHANNELS].astype(jnp.bfloat16).astype(jnp.float32)
+    )
+
+
+def conv_chunk(conv_ref, seg_ref, taps_ref, base):
+    rows = conv_ref[pl.ds(base, CHUNK + 8), :]
+    segs = seg_ref[pl.ds(base, CHUNK + 8), :]
+    own = segs[8:]
+    total = jnp.broadcast_to(taps_ref[CONV : CONV + 1, :], (CHUNK, CHANNELS))
+    for offset in range(CONV):
+        at = 8 - (CONV - 1) + offset
+        same = segs[at : at + CHUNK] == own
+        total = total + jnp.where(same, rows[at : at + CHUNK] * taps_ref[offset : offset + 1], 0.0)
+    return total, segs
+
+
+def steps_of(proj_ref, heads_ref, base):
+    raw = proj_ref[pl.ds(base, CHUNK), INNER + CHANNELS :] + heads_ref[0:1, :SSM_HEADS]
+    step = jnp.maximum(raw, 0.0) + jnp.log1p(jnp.exp(-jnp.abs(raw)))
+    rate = -step * heads_ref[1:2, :SSM_HEADS]
+    early = lax.broadcasted_iota(jnp.int32, (CHUNK, CHUNK), 0)
+    late = lax.broadcasted_iota(jnp.int32, (CHUNK, CHUNK), 1)
+    total = dot_high((late <= early).astype(jnp.float32), rate)
+    source = lax.broadcasted_iota(jnp.int32, (CHUNK, PAIR), 0)
+    target = lax.broadcasted_iota(jnp.int32, (CHUNK, PAIR), 1) % CHUNK
+    across = lax.dot_general(
+        rate,
+        (source <= target).astype(jnp.float32),
+        (((0,), (0,)), ((), ())),
+        precision=HIGH,
+        preferred_element_type=jnp.float32,
+    )
+    return raw, step, rate, total, across
+
+
+def chunk_masks(segs, seg_row):
+    own, before, last = segs[8:], segs[7:8], segs[CHUNK + 7 :]
+    at = lax.broadcasted_iota(jnp.int32, (CHUNK, PAIR), 0)
+    source = lax.broadcasted_iota(jnp.int32, (CHUNK, PAIR), 1) % CHUNK
+    allowed = (own == seg_row) & (source <= at)
+    entry = (own == before).astype(jnp.float32)
+    tail = (own == last).astype(jnp.float32)
+    carry = (last == before).astype(jnp.float32)
+    return allowed, entry, tail, carry
+
+
+def per_pair(columns, k, low_half):
+    return jnp.where(low_half, columns[:, 2 * k : 2 * k + 1], columns[:, 2 * k + 1 : 2 * k + 2])
+
+
+def row_pair(rows, k, low_half):
+    return jnp.where(
+        low_half[:1], rows[2 * k : 2 * k + 1], rows[2 * k + 1 : 2 * k + 2]
+    )
+
+
+def diagonal(value, low_half):
+    zero = jnp.zeros_like(value)
+    return jnp.concatenate([jnp.where(low_half, value, zero), jnp.where(low_half, zero, value)])
+
+
+def mixer_forward(
+    proj_ref, taps_ref, heads_ref, wide_ref, seg_ref, seg_row_ref,
+    out_ref, mix_ref, states_ref, conv_ref, state_ref, gated_ref,
+):
+    count, row_count = proj_ref.shape[0], out_ref.shape[0]
+    low = jnp.bfloat16
+    load_conv(proj_ref, conv_ref)
+    state_ref[...] = jnp.zeros_like(state_ref)
+    low_half = first_lanes(CHUNK)
+
+    def body(c, _):
+        base = pl.multiple_of(c * CHUNK, CHUNK)
+        store = pl.multiple_of(jnp.maximum(c - 1, 0) * CHUNK, CHUNK)
+        total, segs = conv_chunk(conv_ref, seg_ref, taps_ref, base)
+        mixed = (total * jax.nn.sigmoid(total)).astype(low)
+        inner = mixed[:, :INNER].astype(jnp.float32)
+        state_in, state_out = mixed[:, INNER : INNER + STATE], mixed[:, INNER + STATE :]
+        _, step, _, cumul, across = steps_of(proj_ref, heads_ref, base)
+        allowed, entry, tail, carry = chunk_masks(segs, seg_row_ref[pl.ds(c, 1), :])
+        shared = dot_right_t(state_out, jnp.concatenate([state_in, state_in]))
+        shared = jnp.where(allowed, shared, 0.0)
+        state = state_ref[...]
+        state_low = state.astype(low)
+        states_ref[pl.ds(c, 1)] = state_low[None]
+        incoming = dot_plain(state_out, state_low)
+        squares = jnp.zeros((CHUNK, PAIR), jnp.float32)
+        fresh, kept = [], []
+        for k in range(SSM_HEADS // 2):
+            lanes = slice(k * PAIR, (k + 1) * PAIR)
+            sums = per_pair(cumul, k, low_half)
+            decay = jnp.exp(jnp.minimum(sums - row_pair(across, k, low_half), 0.0))
+            weights = (decay * shared).astype(low)
+            value = inner[:, lanes]
+            stepped = value * per_pair(step, k, low_half)
+            local = dot_plain(weights, diagonal(stepped.astype(low), low_half))
+            end = sums[CHUNK - 1 :]
+            mix = (
+                local
+                + incoming[:, lanes] * (jnp.exp(sums) * entry)
+                + wide_ref[0:1, lanes] * value
+            )
+            fresh.append((stepped * (jnp.exp(end - sums) * tail)).astype(low))
+            kept.append(jnp.exp(end) * carry)
+            gate = proj_ref[pl.ds(base, CHUNK), lanes]
+            gated = mix * gate * jax.nn.sigmoid(gate)
+            mix_ref[pl.ds(store, CHUNK), lanes] = mix
+            gated_ref[:, lanes] = gated
+            squares = squares + gated * gated
+        state_ref[...] = state * jnp.concatenate(kept, axis=1) + dot_left_t(
+            state_in, jnp.concatenate(fresh, axis=1)
+        )
+        norm = lax.rsqrt(jnp.sum(squares, axis=1, keepdims=True) / INNER + EPS)
+        out_ref[pl.ds(store, CHUNK), :] = (gated_ref[...] * norm * wide_ref[1:2, :]).astype(low)
+        return 0
+
+    lax.fori_loop(0, count // CHUNK, body, 0)
+
+
+def mixer_backward(
+    proj_ref, mix_ref, states_ref, grad_ref, taps_ref, heads_ref, wide_ref, seg_ref, seg_row_ref,
+    out_ref, taps_out_ref, wide_out_ref, heads_out_ref,
+    conv_ref, pre_ref, adjoint_ref, mixgrad_ref, innergrad_ref,
+):
+    count, row_count = proj_ref.shape[0], mix_ref.shape[0]
+    low = jnp.bfloat16
+    load_conv(proj_ref, conv_ref)
+    adjoint_ref[...] = jnp.zeros_like(adjoint_ref)
+    pre_ref[...] = jnp.zeros_like(pre_ref)
+    taps_out_ref[...] = jnp.zeros_like(taps_out_ref)
+    wide_out_ref[...] = jnp.zeros_like(wide_out_ref)
+    heads_out_ref[...] = jnp.zeros_like(heads_out_ref)
+    low_half = first_lanes(CHUNK)
+    chunks = count // CHUNK
+
+    def body(turn_at, _):
+        c = chunks - 1 - turn_at
+        base = pl.multiple_of(c * CHUNK, CHUNK)
+        store = pl.multiple_of(jnp.maximum(c - 1, 0) * CHUNK, CHUNK)
+        real = (c > 0).astype(jnp.float32)
+
+        gate = proj_ref[pl.ds(base, CHUNK), :INNER]
+        mix = mix_ref[pl.ds(store, CHUNK), :]
+        norm_grad = grad_ref[pl.ds(store, CHUNK), :].astype(jnp.float32) * real
+        sig = jax.nn.sigmoid(gate)
+        silu = gate * sig
+        gated = mix * silu
+        norm = lax.rsqrt(jnp.mean(gated * gated, axis=1, keepdims=True) + EPS)
+        scaled = norm_grad * wide_ref[1:2, :]
+        wide_out_ref[1:2, :] += jnp.sum(norm_grad * gated * norm, axis=0, keepdims=True)
+        pull = jnp.mean(gated * scaled, axis=1, keepdims=True) * (norm * norm * norm)
+        gated_grad = norm * scaled - gated * pull
+        mix_grad = gated_grad * silu
+        mixgrad_ref[...] = mix_grad
+        out_ref[pl.ds(base, CHUNK), :INNER] = (
+            gated_grad * mix * (sig * (1.0 + gate * (1.0 - sig)))
+        ).astype(low)
+
+        total, segs = conv_chunk(conv_ref, seg_ref, taps_ref, base)
+        sig = jax.nn.sigmoid(total)
+        mixed = (total * sig).astype(low)
+        slope = sig * (1.0 + total * (1.0 - sig))
+        inner = mixed[:, :INNER].astype(jnp.float32)
+        state_in, state_out = mixed[:, INNER : INNER + STATE], mixed[:, INNER + STATE :]
+        wide_out_ref[0:1, :] += jnp.sum(mix_grad * inner, axis=0, keepdims=True)
+        raw, step, rate, cumul, across = steps_of(proj_ref, heads_ref, base)
+        allowed, entry, tail, carry = chunk_masks(segs, seg_row_ref[pl.ds(c, 1), :])
+        twice_in = jnp.concatenate([state_in, state_in])
+        shared = jnp.where(allowed, dot_right_t(state_out, twice_in), 0.0)
+        state = states_ref[pl.ds(c, 1)][0]
+        adjoint = adjoint_ref[...]
+        adjoint_low = adjoint.astype(low)
+        incoming = dot_plain(state_out, state)
+        reached = dot_plain(state_in, adjoint_low)
+        products = jnp.sum(adjoint * state.astype(jnp.float32), axis=0, keepdims=True)
+        head_lane = lax.broadcasted_iota(jnp.int32, (CHUNK, SSM_HEADS), 1)
+        head_row = lax.broadcasted_iota(jnp.int32, (SSM_HEADS, PAIR), 0)
+        head_low = lax.broadcasted_iota(jnp.int32, (SSM_HEADS, PAIR), 1) < CHUNK
+        last_row = lax.broadcasted_iota(jnp.int32, (CHUNK, PAIR), 0) == CHUNK - 1
+        sum_grad = jnp.zeros((CHUNK, SSM_HEADS), jnp.float32)
+        step_grad = jnp.zeros((CHUNK, SSM_HEADS), jnp.float32)
+        columns = jnp.zeros((SSM_HEADS, PAIR), jnp.float32)
+        shared_grad = jnp.zeros((CHUNK, PAIR), jnp.float32)
+        leaving, fresh, kept = [], [], []
+        for k in range(SSM_HEADS // 2):
+            lanes = slice(k * PAIR, (k + 1) * PAIR)
+            grad = mixgrad_ref[:, lanes]
+            grad_low = grad.astype(low)
+            sums = per_pair(cumul, k, low_half)
+            decay = jnp.exp(jnp.minimum(sums - row_pair(across, k, low_half), 0.0))
+            weights = decay * shared
+            value = inner[:, lanes]
+            steps = per_pair(step, k, low_half)
+            stepped = value * steps
+            end = sums[CHUNK - 1 :]
+            grown = jnp.exp(sums) * entry
+            faded = jnp.exp(end - sums) * tail
+            passed = jnp.exp(end) * carry
+            leaving.append((grad * grown).astype(low))
+            fresh.append((stepped * faded).astype(low))
+            kept.append(passed)
+            weight_grad = dot_right_t(grad_low, diagonal(stepped.astype(low), low_half))
+            local = dot_left_t(weights.astype(low), grad_low)
+            local = jnp.where(low_half, local[:CHUNK], local[CHUNK:])
+            shared_grad = shared_grad + weight_grad * decay
+            gap_grad = weight_grad * weights
+            into = reached[:, lanes] * faded
+            moved = into * stepped
+            at_end = jnp.sum(moved, axis=0, keepdims=True) + products[:, lanes] * passed
+            sum_terms = (
+                gap_grad
+                + grad * incoming[:, lanes] * grown
+                - moved
+                + jnp.where(last_row, at_end, 0.0)
+            )
+            stepped_grad = into + local
+            innergrad_ref[:, lanes] = stepped_grad * steps + wide_ref[0:1, lanes] * grad
+            step_terms = stepped_grad * value
+            for half in range(2):
+                head = 2 * k + half
+                chosen = low_half if half == 0 else ~low_half
+                sum_grad = sum_grad + jnp.where(
+                    head_lane == head,
+                    jnp.sum(jnp.where(chosen, sum_terms, 0.0), axis=1, keepdims=True),
+                    0.0,
+                )
+                step_grad = step_grad + jnp.where(
+                    head_lane == head,
+                    jnp.sum(jnp.where(chosen, step_terms, 0.0), axis=1, keepdims=True),
+                    0.0,
+                )
+            column = jnp.sum(gap_grad, axis=0, keepdims=True)
+            mine = ((head_row == 2 * k) & head_low) | ((head_row == 2 * k + 1) & ~head_low)
+            columns = columns + jnp.where(mine, column, 0.0)
+        leaving = jnp.concatenate(leaving, axis=1)
+        fresh = jnp.concatenate(fresh, axis=1)
+        shared_grad = jnp.where(allowed, shared_grad, 0.0).astype(low)
+        out_grad = dot_right_t(leaving, state) + dot_plain(shared_grad, twice_in)
+        in_grad = dot_left_t(shared_grad, state_out)
+        in_grad = in_grad[:CHUNK] + in_grad[CHUNK:] + dot_right_t(fresh, adjoint_low)
+        adjoint_ref[...] = adjoint * jnp.concatenate(kept, axis=1) + dot_left_t(state_out, leaving)
+
+        place = lax.broadcasted_iota(jnp.int32, (CHUNK, PAIR), 0)
+        lane = lax.broadcasted_iota(jnp.int32, (CHUNK, PAIR), 1) % CHUNK
+        sum_grad = sum_grad - lax.dot_general(
+            (place == lane).astype(jnp.float32),
+            columns,
+            (((1,), (1,)), ((), ())),
+            precision=HIGH,
+            preferred_element_type=jnp.float32,
+        )
+        early = lax.broadcasted_iota(jnp.int32, (CHUNK, CHUNK), 0)
+        late = lax.broadcasted_iota(jnp.int32, (CHUNK, CHUNK), 1)
+        rate_grad = dot_high((late >= early).astype(jnp.float32), sum_grad)
+        raw_grad = (step_grad - rate_grad * heads_ref[1:2, :SSM_HEADS]) * jax.nn.sigmoid(raw)
+        heads_out_ref[0:1, :SSM_HEADS] += jnp.sum(raw_grad, axis=0, keepdims=True)
+        heads_out_ref[1:2, :SSM_HEADS] += jnp.sum(rate_grad * rate, axis=0, keepdims=True)
+        out_ref[pl.ds(base, CHUNK), INNER + CHANNELS :] = raw_grad.astype(low)
+
+        pre = jnp.concatenate([innergrad_ref[...], in_grad, out_grad], axis=1) * slope
+        taps_out_ref[CONV : CONV + 1, :] += jnp.sum(pre, axis=0, keepdims=True)
+        rows = conv_ref[pl.ds(base, CHUNK + 8), :]
+        own = segs[8:]
+        for offset in range(CONV):
+            at = 8 - (CONV - 1) + offset
+            same = segs[at : at + CHUNK] == own
+            taps_out_ref[offset : offset + 1, :] += jnp.sum(
+                jnp.where(same, pre * rows[at : at + CHUNK], 0.0), axis=0, keepdims=True
+            )
+        later = jnp.concatenate([pre, pre_ref[...]])
+        later_segs = seg_ref[pl.ds(base + 8, CHUNK + 8), :]
+        conv_grad = jnp.zeros((CHUNK, CHANNELS), jnp.float32)
+        for offset in range(CONV):
+            at = CONV - 1 - offset
+            same = later_segs[at : at + CHUNK] == own
+            conv_grad = conv_grad + jnp.where(
+                same, later[at : at + CHUNK] * taps_ref[offset : offset + 1], 0.0
+            )
+        out_ref[pl.ds(base, CHUNK), INNER : INNER + CHANNELS] = conv_grad.astype(low)
+        pre_ref[...] = pre[:8]
+        return 0
+
+    lax.fori_loop(0, chunks, body, 0)
+
+
+def call(kernel, outs, scratch, flops, *args):
+    size = sum(a.size * a.dtype.itemsize for a in args)
+    whole = pl.BlockSpec(memory_space=pltpu.VMEM)
+    return pl.pallas_call(
+        kernel,
+        out_shape=[jax.ShapeDtypeStruct(shape, kind) for shape, kind in outs],
+        in_specs=[whole] * len(args),
+        out_specs=[whole] * len(outs),
+        scratch_shapes=[pltpu.VMEM(shape, jnp.float32) for shape in scratch],
+        compiler_params=pltpu.CompilerParams(vmem_limit_bytes=56 * 1024 * 1024),
+        cost_estimate=pl.CostEstimate(flops=flops, bytes_accessed=size, transcendentals=0),
+    )(*args)
+
+
+def shards_halo(
+    tokens,
+    segments,
+    input_gain,
+    mixer_in,
+    conv_weight,
+    conv_bias,
+    step_bias,
+    decay_log,
+    skip_gain,
+    mixer_gain,
+    mixer_out,
+    w_query,
+    w_key,
+    w_value,
+    w_output,
+    hidden_gain,
+    w_gate,
+    w_up,
+    w_down,
+    cotangent,
+):
+    row_count, width = tokens.shape
+    halo = max(row_count // 8, 2)
+    count = row_count + halo
+    seq_rank = lax.axis_index("seq")
+    dp_count = lax.axis_size("dp")
+    low = jnp.bfloat16
+
+    small = jnp.concatenate(
+        [input_gain, conv_weight.reshape(-1), conv_bias, mixer_gain, hidden_gain]
+    )
+    per_row = w_query.shape[1] + w_key.shape[1] + w_value.shape[1]
+    small = jnp.pad(small, (0, 16 * per_row - small.shape[0])).reshape(16, per_row)
+    qkv_piece = jnp.concatenate([w_query, w_key, w_value], axis=1)
+    qkv_rows = qkv_piece.shape[0]
+    qkv = gather_weight(jnp.concatenate([qkv_piece, small]), False)
+    smalls = (
+        qkv[:, qkv_rows:].reshape(dp_count, 16, 2, per_row).transpose(0, 2, 1, 3)
+    ).reshape(2 * dp_count, 16 * per_row)
+    sizes = [
+        input_gain.shape[0],
+        conv_weight.size,
+        conv_bias.shape[0],
+        mixer_gain.shape[0],
+        hidden_gain.shape[0],
+    ]
+    places_at = [sum(sizes[:k]) for k in range(6)]
+    gains = [
+        smalls[:, places_at[k] : places_at[k + 1]].reshape(-1).astype(jnp.float32)
+        for k in range(5)
+    ]
+    full_input_gain, full_conv_weight, full_conv_bias, full_mixer_gain, full_hidden_gain = gains
+    full_conv_weight = full_conv_weight.reshape(-1, CONV)
+    qkv = qkv[:, :qkv_rows].reshape(width, 2 * per_row)
+    half_q, half_k = w_query.shape[1], w_key.shape[1]
+    full_mixer_in = gather_weight(mixer_in, True).reshape(width, -1)
+    outs = gather_weight(jnp.concatenate([mixer_out, w_output]), False)
+    full_mixer_out = outs[:, : mixer_out.shape[0]].reshape(-1, width)
+    full_output = outs[:, mixer_out.shape[0] :].reshape(-1, width)
+    gate_up = gather_weight(jnp.concatenate([w_gate, w_up], axis=1), True).reshape(width, -1)
+    full_down = gather_weight(w_down, False).reshape(-1, width)
+
+    seg_all = segments[0]
+    tail = lax.ppermute(tokens[row_count - halo :], "seq", [(0, 1)])
+    hidden_ext = jnp.concatenate([tail, tokens]).astype(jnp.float32)
+    padded_seg = jnp.concatenate([jnp.full((halo,), -1, jnp.int32), seg_all])
+    seg_ext = lax.dynamic_slice_in_dim(padded_seg, seq_rank * row_count, count)
+    padded_places = jnp.concatenate([jnp.zeros((halo,), jnp.int32), doc_places(seg_all)])
+    places = lax.dynamic_slice_in_dim(padded_places, seq_rank * row_count, count)
+    seg_rows = seg_ext[halo:]
+
+    normed, norm_pull = jax.vjp(rms_scale, hidden_ext, full_input_gain)
+    normed_low = normed.astype(low)
+    normed_own = normed_low[halo:]
+    f32 = jnp.float32
+    seg_col, seg_row = seg_ext[:, None], seg_ext[None, :]
+    half = HEAD_DIM // 2
+    lane = jnp.arange(PAIR)
+    angle = places.astype(f32)[:, None] * (THETA ** (-(lane % half).astype(f32) / half))[None, :]
+    cosine = jnp.cos(angle)
+    sine = jnp.sin(angle) * jnp.where(lane % HEAD_DIM < half, -1.0, 1.0)[None, :]
+    turned, attended_low = call(
+        attention_forward,
+        [((count, 2 * per_row), low), ((row_count, HEADS * HEAD_DIM), low)],
+        [],
+        10**10,
+        dot_plain(normed_low, qkv),
+        cosine,
+        sine,
+        seg_col,
+        seg_row,
+    )
+
+    projected = dot_plain(normed_low, full_mixer_in)
+    chunks = count // CHUNK
+    seg_conv = jnp.concatenate([jnp.full((8,), -1, jnp.int32), seg_ext, jnp.full((8,), -9, jnp.int32)])
+    seg_conv = seg_conv[:, None]
+    seg_chunks = jnp.concatenate([seg_ext.reshape(chunks, CHUNK)] * 2, axis=1)
+    taps = jnp.concatenate([full_conv_weight.T, full_conv_bias[None]])
+    heads = jnp.stack([step_bias, jnp.exp(decay_log)])
+    wide = jnp.stack([jnp.repeat(skip_gain, SSM_DIM), full_mixer_gain])
+    mixed_low, mix, states = call(
+        mixer_forward,
+        [
+            ((row_count, INNER), low),
+            ((row_count, INNER), f32),
+            ((chunks, STATE, INNER), low),
+        ],
+        [(count + 8, CHANNELS), (STATE, INNER), (CHUNK, INNER)],
+        2 * 10**10,
+        projected,
+        taps,
+        heads,
+        wide,
+        seg_conv,
+        seg_chunks,
+    )
+    hidden_mid = (
+        hidden_ext[halo:]
+        + dot_plain(attended_low, full_output)
+        + dot_plain(mixed_low, full_mixer_out)
+    )
+    normed_two, norm_two_pull = jax.vjp(rms_scale, hidden_mid, full_hidden_gain)
+    normed_two_low = normed_two.astype(low)
+    gate_up_part = dot_plain(normed_two_low, gate_up)
+    half_ff = w_gate.shape[1]
+    gate_part = two_halves(gate_up_part, 0, half_ff)
+    up_part = two_halves(gate_up_part, 1, half_ff)
+    sigmoid_gate = jax.nn.sigmoid(gate_part)
+    activated_low = (gate_part * sigmoid_gate * up_part).astype(low)
+    output = (hidden_mid + dot_plain(activated_low, full_down)).astype(low)
+
+    act_grad = dot_right_t(cotangent, full_down)
+    grad_down = scatter_weight(dot_left_t(activated_low, cotangent).astype(low), False)
+    gate_grad_low, up_grad_low = ffn_backward_grads(act_grad, gate_part, up_part, sigmoid_gate)
+    gate_up_grad = jnp.concatenate(
+        [
+            gate_grad_low[:, :half_ff],
+            up_grad_low[:, :half_ff],
+            gate_grad_low[:, half_ff:],
+            up_grad_low[:, half_ff:],
+        ],
+        axis=1,
+    )
+    grad_gate_up = scatter_weight(dot_left_t(normed_two_low, gate_up_grad).astype(low), True)
+    normed_two_grad = dot_right_t(gate_up_grad, gate_up)
+    hidden_part, hidden_gain_grad = norm_two_pull(normed_two_grad)
+    hidden_grad = cotangent.astype(jnp.float32) + hidden_part
+    branch_low = hidden_grad.astype(low)
+    grad_mixer_out = scatter_weight(dot_left_t(mixed_low, branch_low).astype(low), False)
+    grad_output = scatter_weight(dot_left_t(attended_low, branch_low).astype(low), True)
+
+    (qkv_grad,) = call(
+        attention_backward,
+        [((count, 2 * per_row), low)],
+        [(count, PAIR), (count, PAIR)],
+        2 * 10**10,
+        turned,
+        dot_right_t(branch_low, full_output).astype(low),
+        cosine,
+        sine,
+        seg_col,
+        seg_row,
+    )
+    grad_qkv = scatter_weight(dot_left_t(normed_low, qkv_grad).astype(low), False)
+
+    norm_grad = dot_right_t(branch_low, full_mixer_out)
+    proj_grad_low, taps_grad, wide_grad, heads_grad = call(
+        mixer_backward,
+        [
+            ((count, INNER + CHANNELS + SSM_HEADS), low),
+            ((8, CHANNELS), f32),
+            ((8, INNER), f32),
+            ((8, PAIR), f32),
+        ],
+        [
+            (count + 8, CHANNELS),
+            (8, CHANNELS),
+            (STATE, INNER),
+            (CHUNK, INNER),
+            (CHUNK, INNER),
+        ],
+        4 * 10**10,
+        projected,
+        mix,
+        states,
+        norm_grad,
+        taps,
+        heads,
+        wide,
+        seg_conv,
+        seg_chunks,
+    )
+    conv_weight_grad, conv_bias_grad = taps_grad[:CONV].T, taps_grad[CONV]
+    mixer_gain_grad = wide_grad[1]
+    skip_grad = jnp.sum(wide_grad[0].reshape(SSM_HEADS, SSM_DIM), axis=1)
+    bias_grad, decay_grad = heads_grad[0, :SSM_HEADS], heads_grad[1, :SSM_HEADS]
+    normed_grad = dot_right_t(proj_grad_low, full_mixer_in) + dot_right_t(qkv_grad, qkv)
+    grad_mixer_in = scatter_weight(dot_left_t(normed_low, proj_grad_low).astype(low), True)
+    input_part, input_gain_grad = norm_pull(normed_grad)
+    returned = lax.ppermute(input_part[:halo].astype(low), "seq", [(1, 0)]).astype(jnp.float32)
+    token_grad = hidden_grad + input_part[halo:]
+    token_grad = token_grad.at[row_count - halo :].add(returned)
+
+    blocks = 2 * dp_count
+    shared_sums = jnp.concatenate([bias_grad, decay_grad, skip_grad])
+    small_grads = jnp.concatenate(
+        [
+            input_gain_grad.reshape(blocks, -1),
+            conv_weight_grad.reshape(blocks, -1),
+            conv_bias_grad.reshape(blocks, -1),
+            mixer_gain_grad.reshape(blocks, -1),
+            hidden_gain_grad.reshape(blocks, -1),
+            jnp.broadcast_to(shared_sums[None], (blocks, 3 * SSM_HEADS)),
+        ],
+        axis=1,
+    )
+    sums = scatter_small(small_grads)
+    small_out = [sums[places_at[k] : places_at[k + 1]] for k in range(5)]
+    heads_out = sums[places_at[5] :].reshape(3, SSM_HEADS)
+    return (
+        output,
+        token_grad,
+        small_out[0],
+        grad_mixer_in,
+        small_out[1].reshape(-1, CONV),
+        small_out[2],
+        heads_out[0],
+        heads_out[1],
+        heads_out[2],
+        small_out[3],
+        grad_mixer_out,
+        grad_qkv[:, :half_q],
+        grad_qkv[:, half_q : half_q + half_k],
+        grad_qkv[:, half_q + half_k :],
+        grad_output,
+        small_out[4],
+        grad_gate_up[:, :half_ff],
+        grad_gate_up[:, half_ff:],
+        grad_down,
+    )
+
+
+def two_halves(value, which, half):
+    return jnp.concatenate(
+        [
+            value[:, which * half : which * half + half],
+            value[:, (2 + which) * half : (3 + which) * half],
+        ],
+        axis=1,
+    )
+
+
 def solution(mesh):
     placed = (
         P(("dp", "seq"), None),
@@ -676,7 +1506,7 @@
         P(("dp", "seq"), None),
     )
     return jax.shard_map(
-        shards,
+        shards_halo if mesh.shape["seq"] == 2 else shards_general,
         mesh=mesh,
         in_specs=placed,
         out_specs=(

time: 1280 us -> 701 us (0.55)
  blocking collectives: 337 us -> 0 us
  waiting for transfers between devices: 494 us -> 268 us
  matrix products: 261 us -> 88 us
  Pallas kernels: 0 us -> 87.1 us
  starting transfers between devices: 1.57 us -> 53.6 us
  local copies, waits for them, and re-layouts: 34.5 us -> 75.6 us
  between operations: 27.4 us -> 2.69 us
    reduce_scatter x17 -> x0, waiting for transfers between devices: 380 us -> none  [the longest x1 91.8 us: shards(): lax.psum_scatter(grad_mixer_in_full.astype(jnp.bfloat16), 'dp', scatter_d...]
    ppermute x0 -> x74, waiting for transfers between devices: none -> 268 us  [the longest x72 268 us: ring(): return lax.ppermute(value, axis, pairs)]
    all_gather x19 -> x0, blocking collectives: 155 us -> none  [the longest x1 20.1 us: shards(): lax.all_gather(sectioned[8], 'dp', axis=0, tiled=True)]
    unnamed x5 -> x0, blocking collectives: 142 us -> none
    dot_general x18 -> x0, matrix products: 132 us -> none  [the longest x3 73.9 us: block_mix(): local_part = jnp.einsum('hts,shp->thp', weights_mat, inner, precision=HIGH)]
    unnamed x32 -> x0, waiting for transfers between devices: 96.4 us -> none
    pallas_call x0 -> x4, Pallas kernels: none -> 87.1 us  [call(): pl.pallas_call(kernel, out_shape=[jax.ShapeDtypeStruct(shape, kind) for s...]
    select_n x7 -> x37, other arithmetic: 5.9 us -> 70.4 us  [the longest x15 53.5 us: in_order(): jnp.where(own == 0, jnp.concatenate(parts, axis=dim), jnp.concatenate(par...]
  transfers between devices with their start and end apart: 28 -> 74, of which waited for: 18 -> 43; matrix products, arithmetic and copies ran while one was open for 27% -> 28% of each run, Pallas kernels for 0% -> 4%
where the time goes in v1:
time: 701 us; the launch traced here: 696 us
  waiting for transfers between devices  268 us (38%)
  other arithmetic  121 us (17%)
  matrix products  88 us (13%)
  Pallas kernels  87.1 us (12%)
  local copies, waits for them, and re-layouts  75.6 us (11%)
  starting transfers between devices  53.6 us (8%)
    ppermute x72, waiting for transfers between devices, ring(): return lax.ppermute(value, axis, pairs)  268 us
    pallas_call x4, Pallas kernels, call(): pl.pallas_call(kernel, out_shape=[jax.ShapeDtypeStruct(shape, kind) for s...  87.1 us
    select_n x15, other arithmetic, in_order(): jnp.where(own == 0, jnp.concatenate(parts, axis=dim), jnp.concatenate(par...  53.5 us
    ppermute x72, starting transfers between devices, ring(): return lax.ppermute(value, axis, pairs)  48.8 us
    dot_general x6, matrix products, dot_right_t(): lax.dot_general(left, right, (((1,), (1,)), ((), ())), preferred_element_...  33.9 us
    dot_general x6, matrix products, dot_plain(): return jnp.dot(left, right, preferred_element_type=jnp.float32)  27.4 us
    dot_general x6, matrix products, dot_left_t(): lax.dot_general(left, right, (((0,), (0,)), ((), ())), preferred_element_...  26.7 us
    unnamed x171, local copies, waits for them, and re-layouts  24.2 us
  transfers between devices with their start and end apart: 74, of which 43 were waited for; matrix products, arithmetic and copies ran while one was open for 28% of the time, Pallas kernels for 4%

profile of v1, /device:TPU:0, one launch (start us, length us, event | category | flops | bytes accessed | tf_op | source)
XLA Modules:
  0.0 695.6 jit_solution(9022060521717978144)
XLA Ops:
  5.9 3.0 collective-permute-start.1
  10.5 3.5 collective-permute-start
  39.4 3.4 collective-permute-done.2
  60.4 3.0 collective-permute-done.9
  65.6 7.4 %collective-permute-done.27 = bf16[1,1,1,128,512]{4,3,2,1,0:T(8,128)(2,1)S(1)} collective-permute-done((bf16[1,1,1,128,512]{4,3,2,1,0:T(8,128)(2,1)S(1)}, bf16[1,1,1,128,512]{4,3,2,1,0:T(8,128)(2,1)S(1)}, u32[]{:S(2)}, u32[]{:S(2)}) %collective-permute-start.27) | collective-permute-done | bytes 131104 | tf_op jit(solution)/shard_map/ppermute | solution.py:663
  77.3 5.9 collective-permute-done.15
  99.7 9.1 %collective-permute-done.16 = bf16[4,1,1,64,1676]{4,3,0,2,1:T(8,128)(2,1)S(1)} collective-permute-done((bf16[4,1,1,64,1676]{4,3,0,2,1:T(8,128)(2,1)S(1)}, bf16[4,1,1,64,1676]{4,3,0,2,1:T(8,128)(2,1)S(1)}, u32[]{:S(2)}, u32[]{:S(2)}) %collective-permute-start.16) | collective-permute-done | bytes 858144 | tf_op jit(solution)/shard_map/ppermute | solution.py:663
  111.1 20.1 %collective-permute-done.22 = bf16[4,1,1,64,2048]{4,3,0,2,1:T(8,128)(2,1)S(1)} collective-permute-done((bf16[4,1,1,64,2048]{4,3,0,2,1:T(8,128)(2,1)S(1)}, bf16[4,1,1,64,2048]{4,3,0,2,1:T(8,128)(2,1)S(1)}, u32[]{:S(2)}, u32[]{:S(2)}) %collective-permute-start.22) | collective-permute-done | bytes 1048608 | tf_op jit(solution)/shard_map/ppermute | solution.py:663
  141.8 12.0 %collective-permute-done.11 = bf16[4,1,1,128,1024]{4,3,2,1,0:T(8,128)(2,1)} collective-permute-done((bf16[4,1,1,128,1024]{4,3,2,1,0:T(8,128)(2,1)}, bf16[4,1,1,128,1024]{4,3,2,1,0:T(8,128)(2,1)}, u32[]{:S(2)}, u32[]{:S(2)}) %collective-permute-start.11) | collective-permute-done | bytes 1048608 | tf_op jit(solution)/shard_map/ppermute | solution.py:663
  153.8 3.3 maximum_select_fusion.6
  157.1 5.4 maximum_select_fusion.5
  167.1 4.3 fusion.36.part_ref
  171.6 3.8 maximum_select_fusion.9
  175.4 8.9 %shard_map.339 = (bf16[576,768]{1,0:T(8,128)(2,1)}, bf16[512,512]{1,0:T(8,128)(2,1)}) custom-call(f32[576,768]{1,0:T(8,128)} %fusion.36.part_ref, f32[576,128]{1,0:T(8,128)} %get-tuple-element.98.cos_ref, f32[576,128]{1,0:T(8,128)} %get-tuple-element.97.sin_ref, s32[576,1]{1,0:T(8,128)} %broadcast_in_dim.56.seg_col_ref, s32[1,576]{1,0:T(1,128)} %broadcast_in_dim.50.seg_row_ref), custom_call_target="tpu_custom_call" | custom-call | flops 10000000000 | bytes 2363904 | tf_op jit(solution)/shard_map/pallas_call | solution.py:1220
  184.3 3.4 collective-permute-done.23
  187.7 5.1 maximum_select_fusion.3
  192.9 4.4 maximum_select_fusion.2
  201.5 5.8 maximum_select_fusion.4
  207.3 14.9 %maximum_select_fusion.1 = bf16[4,2,2,64,3352]{4,3,2,1,0:T(8,128)(2,1)S(1)} fusion(bf16[4,2,1,64,3352]{4,3,2,1,0:T(8,128)(2,1)} %collective-permute-done.18, bf16[4,2,1,64,3352]{4,3,2,1,0:T(8,128)(2,1)S(1)} %maximum_select_fusion.5, pred[]{:T(512)S(6)} %eq.202), kind=kLoop, calls=%fused_computation.4 | loop fusion | flops 10297344 | bytes 13729793 | tf_op jit(solution)/shard_map/jit(_where)/select_n | solution.py:673
  225.1 6.9 fusion.35.proj_ref
  232.0 19.7 %shard_map.340 = (bf16[512,1536]{1,0:T(8,128)(2,1)}, f32[512,1536]{1,0:T(8,128)}, bf16[9,128,1536]{2,1,0:T(8,128)(2,1)}) custom-call(f32[576,3352]{1,0:T(8,128)} %fusion.35.proj_ref, f32[5,1792]{1,0:T(8,128)} %maximum_convert_fusion.taps_ref, f32[2,24]{1,0:T(2,128)} %pad_maximum_fusion.10.heads_ref, f32[2,1536]{1,0:T(2,128)} %pad_maximum_fusion.9.wide_ref, ...), custom_call_target="tpu_custom_call" | custom-call | flops 20000000000 | bytes 7778304 | tf_op jit(solution)/shard_map/pallas_call | solution.py:1220
  251.6 4.6 multiply_reduce_fusion.5
  256.3 5.3 maximum_select_fusion
  261.6 3.3 copy-done.6
  264.9 4.6 fusion.32
  269.6 3.3 fusion.38
  274.3 7.7 %fusion.2 = (bf16[512,2048]{1,0:T(8,128)(2,1)S(1)}, bf16[512,2048]{1,0:T(8,128)(2,1)}, bf16[512,2048]{1,0:T(8,128)(2,1)S(1)}) fusion(f32[512,1024]{1,0:T(8,128)} %get-tuple-element.82, f32[512,1024]{1,0:T(8,128)} %get-tuple-element.83, f32[512,1024]{1,0:T(8,128)} %get-tuple-element.84, f32[512,1024]{1,0:T(8,128)S(1)} %get-tuple-element.81, ...), kind=kOutput, calls=%fused_computation.16 | convolution fusion | flops 2166358016 | bytes 19922944 | tf_op jit(solution)/shard_map/dot_general | solution.py:160
  285.8 7.6 %multiply_reduce_fusion.3 = (f32[1024]{0:T(1024)}, f32[512]{0:T(512)S(1)}, f32[512,1024]{1,0:T(8,128)S(1)}) fusion(f32[512,1024]{1,0:T(8,128)S(1)} %copy-done.8, f32[512]{0:T(512)S(1)} %fusion.25, f32[1024]{0:T(1024)S(1)} %copy-done.48, bf16[1024,4096]{1,0:T(8,128)(2,1)S(1)} %bitcast.199, bf16[512,1024]{1,0:T(8,128)(2,1)} %get-tuple-element.88, ...), kind=kOutput, calls=%fused_computation.50 | convolution fusion | flops 4314888704 | bytes 16789504 | tf_op jit(solution)/shard_map/dot_general | solution.py:160
  297.2 3.5 fusion.44.grad_ref
  300.7 12.8 %shard_map.342 = bf16[576,768]{1,0:T(8,128)(2,1)} custom-call(bf16[576,768]{1,0:T(8,128)(2,1)} %get-tuple-element.45.turned_ref, bf16[512,512]{1,0:T(8,128)(2,1)} %convolution_convert_fusion.6.grad_ref, f32[576,128]{1,0:T(8,128)} %get-tuple-element.98.cos_ref, f32[576,128]{1,0:T(8,128)} %get-tuple-element.97.sin_ref, s32[576,1]{1,0:T(8,128)} %broadcast_in_dim.56.seg_col_ref, ...), custom_call_target="tpu_custom_call" | custom-call | flops 20000000000 | bytes 2003456 | tf_op jit(solution)/shard_map/pallas_call | solution.py:1220
  313.5 3.9 fusion.45
  317.4 45.8 %shard_map.341 = (bf16[576,3352]{1,0:T(8,128)(2,1)}, f32[8,1792]{1,0:T(8,128)}, f32[8,1536]{1,0:T(8,128)}, f32[8,128]{1,0:T(8,128)}) custom-call(f32[576,3352]{1,0:T(8,128)} %fusion.35.proj_ref, f32[512,1536]{1,0:T(8,128)} %get-tuple-element.42.mix_ref, bf16[9,128,1536]{2,1,0:T(8,128)(2,1)} %get-tuple-element.43.states_ref, f32[512,1536]{1,0:T(8,128)} %fusion.44.grad_ref, ...), custom_call_target="tpu_custom_call" | custom-call | flops 40000000000 | bytes 17608704 | tf_op jit(solution)/shard_map/pallas_call | solution.py:1220
  363.2 9.6 %multiply_reduce_fusion = (f32[1024]{0:T(1024)S(1)}, f32[576]{0:T(1024)S(1)}, f32[576,1024]{1,0:T(8,128)S(1)}) fusion(f32[576]{0:T(1024)S(1)} %copy-done.57, bf16[512,1024]{1,0:T(8,128)(2,1)S(1)} %copy-done.4, bf16[64,1024]{1,0:T(8,128)(2,1)S(1)} %copy-done.33, f32[1024]{0:T(1024)S(1)} %copy-done.55, f32[576,1024]{1,0:T(8,128)} %fusion.45, ...), kind=kOutput, calls=%fused_computation.32 | convolution fusion | flops 3960666624 | bytes 16637440 | tf_op jit(solution)/shard_map/dot_general | solution.py:160
  378.0 10.1 %convolution_convert_fusion = bf16[1024,4096]{1,0:T(8,128)(2,1)} fusion(bf16[512,1024]{1,0:T(8,128)(2,1)S(1)} %copy-done.40, bf16[512,1024]{1,0:T(8,128)(2,1)} %get-tuple-element.86, bf16[512,1024]{1,0:T(8,128)(2,1)S(1)} %copy-done.39, bf16[512,1024]{1,0:T(8,128)(2,1)} %get-tuple-element.85, f32[512,1024]{1,0:T(8,128)S(1)} %copy-done.8, ...), kind=kOutput, calls=%fused_computation.2 | convolution fusion | flops 4317511680 | bytes 14686208 | tf_op jit(solution)/shard_map/dot_general | solution.py:166
  388.1 4.9 add_convert_fusion.8
  402.2 10.1 %convolution_convert_fusion.1 = bf16[1024,3352]{0,1:T(8,128)(2,1)} fusion(bf16[576,3352]{1,0:T(8,128)(2,1)} %get-tuple-element.44, f32[1024]{0:T(1024)} %reshape.1349, f32[576]{0:T(1024)} %fusion.21, bf16[512,1024]{1,0:T(8,128)(2,1)} %param.22, bf16[64,1024]{1,0:T(8,128)(2,1)S(1)} %copy-done.33), kind=kOutput, calls=%fused_computation.3 | convolution fusion | flops 3961741312 | bytes 11912448 | tf_op jit(solution)/shard_map/dot_general | solution.py:166
  412.3 10.1 %copy.90 = bf16[1024,3352]{1,0:T(8,128)(2,1)} copy(bf16[1024,3352]{0,1:T(8,128)(2,1)} %convolution_convert_fusion.1) | data formatting | bytes 13729792 | tf_op jit(solution)/shard_map/convert_element_type | solution.py:1430
  422.4 5.2 broadcast_select_fusion.1
  429.4 5.2 broadcast_select_fusion
  448.1 3.1 collective-permute-done.35
  452.1 4.6 collective-permute-done.36
  456.8 5.3 collective-permute-done.37
  470.7 4.2 collective-permute-done.57
  478.9 3.1 collective-permute-done.58
  484.6 4.0 collective-permute-done.59
  488.7 4.1 collective-permute-done.51
  492.9 5.5 collective-permute-done.60
  500.2 3.9 collective-permute-done.52
  504.2 5.8 collective-permute-done.61
  510.7 5.2 collective-permute-done.53
  524.6 14.7 %collective-permute-done.45 = bf16[4,1,1,96,1024]{4,3,2,1,0:T(8,128)(2,1)S(1)} collective-permute-done((bf16[4,1,1,96,1024]{4,3,2,1,0:T(8,128)(2,1)S(1)}, bf16[4,1,1,96,1024]{4,3,2,1,0:T(8,128)(2,1)S(1)}, u32[]{:S(2)}, u32[]{:S(2)}) %collective-permute-start.45) | collective-permute-done | bytes 786464 | tf_op jit(solution)/shard_map/ppermute | solution.py:663
  543.0 4.7 collective-permute-done.46
  547.9 7.1 %collective-permute-done.69 = bf16[4,1,1,128,1024]{4,3,2,1,0:T(8,128)(2,1)S(1)} collective-permute-done((bf16[4,1,1,128,1024]{4,3,2,1,0:T(8,128)(2,1)S(1)}, bf16[4,1,1,128,1024]{4,3,2,1,0:T(8,128)(2,1)S(1)}, u32[]{:S(2)}, u32[]{:S(2)}) %collective-permute-start.69) | collective-permute-done | bytes 1048608 | tf_op jit(solution)/shard_map/ppermute | solution.py:663
  561.9 8.8 %collective-permute-done.70 = bf16[4,1,1,128,512]{4,3,2,1,0:T(8,128)(2,1)S(1)} collective-permute-done((bf16[4,1,1,128,512]{4,3,2,1,0:T(8,128)(2,1)S(1)}, bf16[4,1,1,128,512]{4,3,2,1,0:T(8,128)(2,1)S(1)}, u32[]{:S(2)}, u32[]{:S(2)}) %collective-permute-start.70) | collective-permute-done | bytes 524320 | tf_op jit(solution)/shard_map/ppermute | solution.py:663
  576.1 6.0 collective-permute-done.71
  583.3 5.7 collective-permute-done.72
  589.3 20.7 %collective-permute-done.39 = bf16[4,2,1,64,1676]{4,3,2,1,0:T(8,128)(2,1)S(1)} collective-permute-done((bf16[4,2,1,64,1676]{4,3,2,1,0:T(8,128)(2,1)S(1)}, bf16[4,2,1,64,1676]{4,3,2,1,0:T(8,128)(2,1)S(1)}, u32[]{:S(2)}, u32[]{:S(2)}) %collective-permute-start.39) | collective-permute-done | bytes 1716256 | tf_op jit(solution)/shard_map/ppermute | solution.py:663
  612.4 34.8 %collective-permute-done.63 = bf16[4,2,1,64,2048]{4,3,2,1,0:T(8,128)(2,1)S(1)} collective-permute-done((bf16[4,2,1,64,2048]{4,3,2,1,0:T(8,128)(2,1)S(1)}, bf16[4,2,1,64,2048]{4,3,2,1,0:T(8,128)(2,1)S(1)}, u32[]{:S(2)}, u32[]{:S(2)}) %collective-permute-start.63) | collective-permute-done | bytes 2097184 | tf_op jit(solution)/shard_map/ppermute | solution.py:663
  651.5 14.8 %collective-permute-done.64 = bf16[4,1,1,64,2048]{4,3,2,1,0:T(8,128)(2,1)S(1)} collective-permute-done((bf16[4,1,1,64,2048]{4,3,2,1,0:T(8,128)(2,1)S(1)}, bf16[4,1,1,64,2048]{4,3,2,1,0:T(8,128)(2,1)S(1)}, u32[]{:S(2)}, u32[]{:S(2)}) %collective-permute-start.64) | collective-permute-done | bytes 1048608 | tf_op jit(solution)/shard_map/ppermute | solution.py:663
  667.4 10.5 %collective-permute-done.65 = bf16[1,1,1,64,2048]{4,3,2,1,0:T(8,128)(2,1)S(1)} collective-permute-done((bf16[1,1,1,64,2048]{4,3,2,1,0:T(8,128)(2,1)S(1)}, bf16[1,1,1,64,2048]{4,3,2,1,0:T(8,128)(2,1)S(1)}, u32[]{:S(2)}, u32[]{:S(2)}) %collective-permute-start.65) | collective-permute-done | bytes 262176 | tf_op jit(solution)/shard_map/ppermute | solution.py:663
  678.1 4.8 collective-permute-done.42
  683.0 3.2 collective-permute-done.66
  686.4 4.4 collective-permute-done.43
  691.6 2.9 collective-permute-done.67
  (480 shorter events, 189.9 us)
Async XLA Ops:
  5.9 30.7 %collective-permute-start.1 = (bf16[1,1,1,80,384]{4,3,2,1,0:T(8,128)(2,1)}, bf16[1,1,1,80,384]{4,3,2,1,0:T(8,128)(2,1)}, u32[]{:S(2)}, u32[]{:S(2)}) collective-permute-start(bf16[1,1,1,80,384]{4,3,2,1,0:T(8,128)(2,1)} %get-tuple-element.77), channel_id=1, source_target_pairs={{0,8},{2,10},{4,12},{6,14},{8,16},{10,18},{12,20},{14,22},{16,24},... | collective-permute-start | bytes 184328 | tf_op jit(solution)/shard_map/ppermute | solution.py:663
  10.5 32.3 %collective-permute-start = (bf16[64,1024]{1,0:T(8,128)(2,1)}, bf16[64,1024]{1,0:T(8,128)(2,1)S(1)}, u32[]{:S(2)}, u32[]{:S(2)}) collective-permute-start(bf16[64,1024]{1,0:T(8,128)(2,1)} %slice.344), channel_id=1, source_target_pairs={{0,1},{2,3},{4,5},{6,7},{8,9},{10,11},{12,13},{14,15},{16,17},{18,... | collective-permute-start | bytes 393224 | tf_op jit(solution)/shard_map/ppermute | solution.py:1295
  15.6 31.2 %collective-permute-start.7 = (bf16[1,1,1,128,512]{4,3,2,1,0:T(8,128)(2,1)}, bf16[1,1,1,128,512]{4,3,2,1,0:T(8,128)(2,1)}, u32[]{:S(2)}, u32[]{:S(2)}) collective-permute-start(bf16[1,1,1,128,512]{4,3,2,1,0:T(8,128)(2,1)} %maximum_bitcast_fusion.3), channel_id=1, source_target_pairs={{0,8},{2,10},{4,12},{6,14},{8,16},{10,18},{12,20},{14,22},{16,24},... | collective-permute-start | bytes 393224 | tf_op jit(solution)/shard_map/ppermute | solution.py:663
  17.2 38.2 %collective-permute-start.13 = (bf16[1,1,1,64,1676]{4,3,2,1,0:T(8,128)(2,1)}, bf16[1,1,1,64,1676]{4,3,2,1,0:T(8,128)(2,1)}, u32[]{:S(2)}, u32[]{:S(2)}) collective-permute-start(bf16[1,1,1,64,1676]{4,3,2,1,0:T(8,128)(2,1)} %bitcast.225), channel_id=1, source_target_pairs={{0,8},{2,10},{4,12},{6,14},{8,16},{10,18},{12,20},{14,22},{16,24},... | collective-permute-start | bytes 643592 | tf_op jit(solution)/shard_map/ppermute | solution.py:663
  20.5 36.8 %collective-permute-start.19 = (bf16[1,1,1,64,2048]{4,3,2,1,0:T(8,128)(2,1)}, bf16[1,1,1,64,2048]{4,3,2,1,0:T(8,128)(2,1)}, u32[]{:S(2)}, u32[]{:S(2)}) collective-permute-start(bf16[1,1,1,64,2048]{4,3,2,1,0:T(8,128)(2,1)} %maximum_bitcast_fusion.2), channel_id=1, source_target_pairs={{0,8},{2,10},{4,12},{6,14},{8,16},{10,18},{12,20},{14,22},{16,24},... | collective-permute-start | bytes 786440 | tf_op jit(solution)/shard_map/ppermute | solution.py:663
  36.6 6.2 collective-permute-start.2
  42.8 8.4 %collective-permute-start.25 = (bf16[1,1,1,128,512]{4,3,2,1,0:T(8,128)(2,1)}, bf16[1,1,1,128,512]{4,3,2,1,0:T(8,128)(2,1)S(1)}, u32[]{:S(2)}, u32[]{:S(2)}) collective-permute-start(bf16[1,1,1,128,512]{4,3,2,1,0:T(8,128)(2,1)} %bitcast.226), channel_id=1, source_target_pairs={{0,8},{2,10},{4,12},{6,14},{8,16},{10,18},{12,20},{14,22},{16,24},... | collective-permute-start | bytes 393224 | tf_op jit(solution)/shard_map/ppermute | solution.py:663
  42.8 9.7 %collective-permute-start.3 = (bf16[1,1,1,80,384]{4,3,2,1,0:T(8,128)(2,1)S(1)}, bf16[1,1,1,80,384]{4,3,2,1,0:T(8,128)(2,1)S(1)}, u32[]{:S(2)}, u32[]{:S(2)}) collective-permute-start(bf16[1,1,1,80,384]{4,3,2,1,0:T(8,128)(2,1)S(1)} %collective-permute-done.2), channel_id=1, source_target_pairs={{0,8},{2,10},{4,12},{6,14},{8,16},{10,18},{12,20},{14,22},{16,24},... | collective-permute-start | bytes 184328 | tf_op jit(solution)/shard_map/ppermute | solution.py:663
  46.9 8.3 %collective-permute-start.8 = (bf16[1,1,1,128,512]{4,3,2,1,0:T(8,128)(2,1)}, bf16[1,1,1,128,512]{4,3,2,1,0:T(8,128)(2,1)S(1)}, u32[]{:S(2)}, u32[]{:S(2)}) collective-permute-start(bf16[1,1,1,128,512]{4,3,2,1,0:T(8,128)(2,1)} %collective-permute-done.7), channel_id=1, source_target_pairs={{0,8},{2,10},{4,12},{6,14},{8,16},{10,18},{12,20},{14,22},{16,24},... | collective-permute-start | bytes 393224 | tf_op jit(solution)/shard_map/ppermute | solution.py:663
  51.2 8.2 %collective-permute-start.26 = (bf16[1,1,1,128,512]{4,3,2,1,0:T(8,128)(2,1)S(1)}, bf16[1,1,1,128,512]{4,3,2,1,0:T(8,128)(2,1)S(1)}, u32[]{:S(2)}, u32[]{:S(2)}) collective-permute-start(bf16[1,1,1,128,512]{4,3,2,1,0:T(8,128)(2,1)S(1)} %collective-permute-done.25), channel_id=1, source_target_pairs={{0,8},{2,10},{4,12},{6,14},{8,16},{10,18},{12,20},{14,22},{16,24},... | collective-permute-start | bytes 393224 | tf_op jit(solution)/shard_map/ppermute | solution.py:663
  55.2 8.3 %collective-permute-start.9 = (bf16[1,1,1,128,512]{4,3,2,1,0:T(8,128)(2,1)S(1)}, bf16[1,1,1,128,512]{4,3,2,1,0:T(8,128)(2,1)S(1)}, u32[]{:S(2)}, u32[]{:S(2)}) collective-permute-start(bf16[1,1,1,128,512]{4,3,2,1,0:T(8,128)(2,1)S(1)} %collective-permute-done.8), channel_id=1, source_target_pairs={{0,8},{2,10},{4,12},{6,14},{8,16},{10,18},{12,20},{14,22},{16,24},... | collective-permute-start | bytes 393224 | tf_op jit(solution)/shard_map/ppermute | solution.py:663
  55.3 20.1 %collective-permute-start.4 = (bf16[4,1,1,80,384]{4,3,0,2,1:T(8,128)(2,1)S(1)}, bf16[4,1,1,80,384]{4,3,0,2,1:T(8,128)(2,1)S(1)}, u32[]{:S(2)}, u32[]{:S(2)}) collective-permute-start(bf16[4,1,1,80,384]{4,3,0,2,1:T(8,128)(2,1)S(1)} %fusion.82), channel_id=1, source_target_pairs={{0,1},{1,0},{2,3},{3,2},{4,5},{5,4},{6,7},{7,6},{8,9},{9,8},{10,11... | collective-permute-start | bytes 737288 | tf_op jit(solution)/shard_map/ppermute | solution.py:663
  55.4 19.9 %collective-permute-start.14 = (bf16[1,1,1,64,1676]{4,3,2,1,0:T(8,128)(2,1)}, bf16[1,1,1,64,1676]{4,3,2,1,0:T(8,128)(2,1)S(1)}, u32[]{:S(2)}, u32[]{:S(2)}) collective-permute-start(bf16[1,1,1,64,1676]{4,3,2,1,0:T(8,128)(2,1)} %collective-permute-done.13), channel_id=1, source_target_pairs={{0,8},{2,10},{4,12},{6,14},{8,16},{10,18},{12,20},{14,22},{16,24},... | collective-permute-start | bytes 643592 | tf_op jit(solution)/shard_map/ppermute | solution.py:663
  57.3 19.9 %collective-permute-start.20 = (bf16[1,1,1,64,2048]{4,3,2,1,0:T(8,128)(2,1)}, bf16[1,1,1,64,2048]{4,3,2,1,0:T(8,128)(2,1)S(1)}, u32[]{:S(2)}, u32[]{:S(2)}) collective-permute-start(bf16[1,1,1,64,2048]{4,3,2,1,0:T(8,128)(2,1)} %collective-permute-done.19), channel_id=1, source_target_pairs={{0,8},{2,10},{4,12},{6,14},{8,16},{10,18},{12,20},{14,22},{16,24},... | collective-permute-start | bytes 786440 | tf_op jit(solution)/shard_map/ppermute | solution.py:663
  59.4 13.6 %collective-permute-start.27 = (bf16[1,1,1,128,512]{4,3,2,1,0:T(8,128)(2,1)S(1)}, bf16[1,1,1,128,512]{4,3,2,1,0:T(8,128)(2,1)S(1)}, u32[]{:S(2)}, u32[]{:S(2)}) collective-permute-start(bf16[1,1,1,128,512]{4,3,2,1,0:T(8,128)(2,1)S(1)} %collective-permute-done.26), channel_id=1, source_target_pairs={{0,8},{2,10},{4,12},{6,14},{8,16},{10,18},{12,20},{14,22},{16,24},... | collective-permute-start | bytes 393224 | tf_op jit(solution)/shard_map/ppermute | solution.py:663
  73.3 16.8 %collective-permute-start.10 = (bf16[4,1,1,128,512]{4,3,2,1,0:T(8,128)(2,1)S(1)}, bf16[4,1,1,128,512]{4,3,2,1,0:T(8,128)(2,1)S(1)}, u32[]{:S(2)}, u32[]{:S(2)}) collective-permute-start(bf16[4,1,1,128,512]{4,3,2,1,0:T(8,128)(2,1)S(1)} %constant_dynamic-slice_fusion.13), channel_id=1, source_target_pairs={{0,1},{1,0},{2,3},{3,2},{4,5},{5,4},{6,7},{7,6},{8,9},{9,8},{10,11... | collective-permute-start | bytes 1572872 | tf_op jit(solution)/shard_map/ppermute | solution.py:663
  73.3 21.3 %collective-permute-start.28 = (bf16[4,1,1,128,512]{4,3,0,2,1:T(8,128)(2,1)S(1)}, bf16[4,1,1,128,512]{4,3,0,2,1:T(8,128)(2,1)S(1)}, u32[]{:S(2)}, u32[]{:S(2)}) collective-permute-start(bf16[4,1,1,128,512]{4,3,0,2,1:T(8,128)(2,1)S(1)} %fusion.74), channel_id=1, source_target_pairs={{0,1},{1,0},{2,3},{3,2},{4,5},{5,4},{6,7},{7,6},{8,9},{9,8},{10,11... | collective-permute-start | bytes 1572872 | tf_op jit(solution)/shard_map/ppermute | solution.py:663
  75.4 7.8 %collective-permute-start.15 = (bf16[1,1,1,64,1676]{4,3,2,1,0:T(8,128)(2,1)S(1)}, bf16[1,1,1,64,1676]{4,3,2,1,0:T(8,128)(2,1)S(1)}, u32[]{:S(2)}, u32[]{:S(2)}) collective-permute-start(bf16[1,1,1,64,1676]{4,3,2,1,0:T(8,128)(2,1)S(1)} %collective-permute-done.14), channel_id=1, source_target_pairs={{0,8},{2,10},{4,12},{6,14},{8,16},{10,18},{12,20},{14,22},{16,24},... | collective-permute-start | bytes 643592 | tf_op jit(solution)/shard_map/ppermute | solution.py:663
  75.5 24.0 %collective-permute-start.5 = (bf16[4,1,1,80,768]{4,3,2,1,0:T(8,128)(2,1)S(1)}, bf16[4,1,1,80,768]{4,3,2,1,0:T(8,128)(2,1)S(1)}, u32[]{:S(2)}, u32[]{:S(2)}) collective-permute-start(bf16[4,1,1,80,768]{4,3,2,1,0:T(8,128)(2,1)S(1)} %fusion.13), channel_id=1, source_target_pairs={{0,4},{2,6},{4,0},{6,2},{8,12},{10,14},{12,8},{14,10},{16,20},{18,... | collective-permute-start | bytes 1474568 | tf_op jit(solution)/shard_map/ppermute | solution.py:663
  77.2 9.8 %collective-permute-start.21 = (bf16[1,1,1,64,2048]{4,3,2,1,0:T(8,128)(2,1)S(1)}, bf16[1,1,1,64,2048]{4,3,2,1,0:T(8,128)(2,1)S(1)}, u32[]{:S(2)}, u32[]{:S(2)}) collective-permute-start(bf16[1,1,1,64,2048]{4,3,2,1,0:T(8,128)(2,1)S(1)} %collective-permute-done.20), channel_id=1, source_target_pairs={{0,8},{2,10},{4,12},{6,14},{8,16},{10,18},{12,20},{14,22},{16,24},... | collective-permute-start | bytes 786440 | tf_op jit(solution)/shard_map/ppermute | solution.py:663
  85.4 23.4 %collective-permute-start.16 = (bf16[4,1,1,64,1676]{4,3,0,2,1:T(8,128)(2,1)S(1)}, bf16[4,1,1,64,1676]{4,3,0,2,1:T(8,128)(2,1)S(1)}, u32[]{:S(2)}, u32[]{:S(2)}) collective-permute-start(bf16[4,1,1,64,1676]{4,3,0,2,1:T(8,128)(2,1)S(1)} %fusion.79), channel_id=1, source_target_pairs={{0,4},{2,6},{4,0},{6,2},{8,12},{10,14},{12,8},{14,10},{16,20},{18,... | collective-permute-start | bytes 2574344 | tf_op jit(solution)/shard_map/ppermute | solution.py:663
  89.2 42.0 %collective-permute-start.22 = (bf16[4,1,1,64,2048]{4,3,0,2,1:T(8,128)(2,1)S(1)}, bf16[4,1,1,64,2048]{4,3,0,2,1:T(8,128)(2,1)S(1)}, u32[]{:S(2)}, u32[]{:S(2)}) collective-permute-start(bf16[4,1,1,64,2048]{4,3,0,2,1:T(8,128)(2,1)S(1)} %fusion.77), channel_id=1, source_target_pairs={{0,4},{2,6},{4,0},{6,2},{8,12},{10,14},{12,8},{14,10},{16,20},{18,... | collective-permute-start | bytes 3145736 | tf_op jit(solution)/shard_map/ppermute | solution.py:663
  91.3 62.5 %collective-permute-start.11 = (bf16[4,1,1,128,1024]{4,3,2,1,0:T(8,128)(2,1)}, bf16[4,1,1,128,1024]{4,3,2,1,0:T(8,128)(2,1)}, u32[]{:S(2)}, u32[]{:S(2)}) collective-permute-start(bf16[4,1,1,128,1024]{4,3,2,1,0:T(8,128)(2,1)} %maximum_select_fusion.14), channel_id=1, source_target_pairs={{0,4},{2,6},{4,0},{6,2},{8,12},{10,14},{12,8},{14,10},{16,20},{18,... | collective-permute-start | bytes 3145736 | tf_op jit(solution)/shard_map/ppermute | solution.py:663
  95.9 75.6 %collective-permute-start.29 = (bf16[4,1,1,128,1024]{4,3,2,1,0:T(8,128)(2,1)}, bf16[4,1,1,128,1024]{4,3,2,1,0:T(8,128)(2,1)}, u32[]{:S(2)}, u32[]{:S(2)}) collective-permute-start(bf16[4,1,1,128,1024]{4,3,2,1,0:T(8,128)(2,1)} %fusion.10), channel_id=1, source_target_pairs={{0,4},{2,6},{4,0},{6,2},{8,12},{10,14},{12,8},{14,10},{16,20},{18,... | collective-permute-start | bytes 3145736 | tf_op jit(solution)/shard_map/ppermute | solution.py:663
  99.6 35.7 %collective-permute-start.6 = (bf16[4,2,1,80,768]{4,3,2,1,0:T(8,128)(2,1)S(1)}, bf16[4,2,1,80,768]{4,3,2,1,0:T(8,128)(2,1)S(1)}, u32[]{:S(2)}, u32[]{:S(2)}) collective-permute-start(bf16[4,2,1,80,768]{4,3,2,1,0:T(8,128)(2,1)S(1)} %maximum_select_fusion.16), channel_id=1, source_target_pairs={{0,2},{2,0},{4,6},{6,4},{8,10},{10,8},{12,14},{14,12},{16,18},{18,... | collective-permute-start | bytes 2949128 | tf_op jit(solution)/shard_map/ppermute | solution.py:663
  109.2 47.9 %collective-permute-start.17 = (bf16[4,2,1,64,1676]{4,3,2,1,0:T(8,128)(2,1)S(1)}, bf16[4,2,1,64,1676]{4,3,2,1,0:T(8,128)(2,1)}, u32[]{:S(2)}, u32[]{:S(2)}) collective-permute-start(bf16[4,2,1,64,1676]{4,3,2,1,0:T(8,128)(2,1)S(1)} %maximum_select_fusion.12), channel_id=1, source_target_pairs={{0,1},{1,0},{2,3},{3,2},{4,5},{5,4},{6,7},{7,6},{8,9},{9,8},{10,11... | collective-permute-start | bytes 5148680 | tf_op jit(solution)/shard_map/ppermute | solution.py:663
  133.3 54.4 %collective-permute-start.23 = (bf16[4,2,1,64,2048]{4,3,2,1,0:T(8,128)(2,1)}, bf16[4,2,1,64,2048]{4,3,2,1,0:T(8,128)(2,1)}, u32[]{:S(2)}, u32[]{:S(2)}) collective-permute-start(bf16[4,2,1,64,2048]{4,3,2,1,0:T(8,128)(2,1)} %maximum_select_fusion.8), channel_id=1, source_target_pairs={{0,1},{1,0},{2,3},{3,2},{4,5},{5,4},{6,7},{7,6},{8,9},{9,8},{10,11... | collective-permute-start | bytes 6291464 | tf_op jit(solution)/shard_map/ppermute | solution.py:663
  157.1 35.8 %collective-permute-start.12 = (bf16[4,2,1,128,1024]{4,3,2,1,0:T(8,128)(2,1)}, bf16[4,2,1,128,1024]{4,3,2,1,0:T(8,128)(2,1)}, u32[]{:S(2)}, u32[]{:S(2)}) collective-permute-start(bf16[4,2,1,128,1024]{4,3,2,1,0:T(8,128)(2,1)} %maximum_select_fusion.6), channel_id=1, source_target_pairs={{0,2},{2,0},{4,6},{6,4},{8,10},{10,8},{12,14},{14,12},{16,18},{18,... | collective-permute-start | bytes 6291464 | tf_op jit(solution)/shard_map/ppermute | solution.py:663
  162.5 44.8 %collective-permute-start.18 = (bf16[4,2,1,64,3352]{4,3,2,1,0:T(8,128)(2,1)S(1)}, bf16[4,2,1,64,3352]{4,3,2,1,0:T(8,128)(2,1)}, u32[]{:S(2)}, u32[]{:S(2)}) collective-permute-start(bf16[4,2,1,64,3352]{4,3,2,1,0:T(8,128)(2,1)S(1)} %maximum_select_fusion.5), channel_id=1, source_target_pairs={{0,2},{2,0},{4,6},{6,4},{8,10},{10,8},{12,14},{14,12},{16,18},{18,... | collective-permute-start | bytes 10297352 | tf_op jit(solution)/shard_map/ppermute | solution.py:663
  175.4 26.1 %collective-permute-start.30 = (bf16[4,2,1,128,1024]{4,3,2,1,0:T(8,128)(2,1)}, bf16[4,2,1,128,1024]{4,3,2,1,0:T(8,128)(2,1)}, u32[]{:S(2)}, u32[]{:S(2)}) collective-permute-start(bf16[4,2,1,128,1024]{4,3,2,1,0:T(8,128)(2,1)} %maximum_select_fusion.9), channel_id=1, source_target_pairs={{0,2},{2,0},{4,6},{6,4},{8,10},{10,8},{12,14},{14,12},{16,18},{18,... | collective-permute-start | bytes 6291464 | tf_op jit(solution)/shard_map/ppermute | solution.py:663
  192.8 63.5 %collective-permute-start.24 = (bf16[4,2,1,64,4096]{4,3,2,1,0:T(8,128)(2,1)S(1)}, bf16[4,2,1,64,4096]{4,3,2,1,0:T(8,128)(2,1)}, u32[]{:S(2)}, u32[]{:S(2)}) collective-permute-start(bf16[4,2,1,64,4096]{4,3,2,1,0:T(8,128)(2,1)S(1)} %maximum_select_fusion.3), channel_id=1, source_target_pairs={{0,2},{2,0},{4,6},{6,4},{8,10},{10,8},{12,14},{14,12},{16,18},{18,... | collective-permute-start | bytes 12582920 | tf_op jit(solution)/shard_map/ppermute | solution.py:663
  393.0 89.9 %collective-permute-start.31 = (bf16[64,1024]{1,0:T(8,128)(2,1)}, bf16[64,1024]{1,0:T(8,128)(2,1)S(1)}, u32[]{:S(2)}, u32[]{:S(2)}) collective-permute-start(bf16[64,1024]{1,0:T(8,128)(2,1)} %slice.624), channel_id=1, source_target_pairs={{1,0},{3,2},{5,4},{7,6},{9,8},{11,10},{13,12},{15,14},{17,16},{19,... | collective-permute-start | bytes 393224 | tf_op jit(solution)/shard_map/ppermute | solution.py:1432
  401.7 36.1 %collective-permute-start.32 = (f32[4,2,1,2,464]{4,3,2,1,0:T(2,128)S(1)}, f32[4,2,1,2,464]{4,3,2,1,0:T(2,128)S(1)}, u32[]{:S(2)}, u32[]{:S(2)}) collective-permute-start(f32[4,2,1,2,464]{4,3,2,1,0:T(2,128)S(1)} %broadcast_select_fusion.19), channel_id=1, source_target_pairs={{0,2},{2,0},{4,6},{6,4},{8,10},{10,8},{12,14},{14,12},{16,18},{18,... | collective-permute-start | bytes 89096 | tf_op jit(solution)/shard_map/ppermute | solution.py:663
  427.6 129.9 %collective-permute-start.38 = (bf16[4,2,1,64,3352]{4,3,2,1,0:T(8,128)(2,1)}, bf16[4,2,1,64,3352]{4,3,2,1,0:T(8,128)(2,1)}, u32[]{:S(2)}, u32[]{:S(2)}) collective-permute-start(bf16[4,2,1,64,3352]{4,3,2,1,0:T(8,128)(2,1)} %broadcast_select_fusion.1), channel_id=1, source_target_pairs={{0,2},{2,0},{4,6},{6,4},{8,10},{10,8},{12,14},{14,12},{16,18},{18,... | collective-permute-start | bytes 10297352 | tf_op jit(solution)/shard_map/ppermute | solution.py:663
  429.0 87.1 %collective-permute-start.44 = (bf16[4,2,1,96,1024]{4,3,2,1,0:T(8,128)(2,1)}, bf16[4,2,1,96,1024]{4,3,2,1,0:T(8,128)(2,1)}, u32[]{:S(2)}, u32[]{:S(2)}) collective-permute-start(bf16[4,2,1,96,1024]{4,3,2,1,0:T(8,128)(2,1)} %broadcast_select_fusion.5), channel_id=1, source_target_pairs={{0,2},{2,0},{4,6},{6,4},{8,10},{10,8},{12,14},{14,12},{16,18},{18,... | collective-permute-start | bytes 4718600 | tf_op jit(solution)/shard_map/ppermute | solution.py:663
  443.9 32.1 %collective-permute-start.50 = (bf16[4,2,1,64,768]{4,3,2,1,0:T(8,128)(2,1)}, bf16[4,2,1,64,768]{4,3,2,1,0:T(8,128)(2,1)}, u32[]{:S(2)}, u32[]{:S(2)}) collective-permute-start(bf16[4,2,1,64,768]{4,3,2,1,0:T(8,128)(2,1)} %broadcast_select_fusion.9), channel_id=1, source_target_pairs={{0,2},{2,0},{4,6},{6,4},{8,10},{10,8},{12,14},{14,12},{16,18},{18,... | collective-permute-start | bytes 2359304 | tf_op jit(solution)/shard_map/ppermute | solution.py:663
  465.8 9.0 %collective-permute-start.57 = (bf16[4,2,1,32,512]{4,3,2,1,0:T(8,128)(2,1)}, bf16[4,2,1,32,512]{4,3,2,1,0:T(8,128)(2,1)S(1)}, u32[]{:S(2)}, u32[]{:S(2)}) collective-permute-start(bf16[4,2,1,32,512]{4,3,2,1,0:T(8,128)(2,1)} %broadcast_select_fusion.15), channel_id=1, source_target_pairs={{0,1},{1,0},{2,3},{3,2},{4,5},{5,4},{6,7},{7,6},{8,9},{9,8},{10,11... | collective-permute-start | bytes 786440 | tf_op jit(solution)/shard_map/ppermute | solution.py:663
  474.8 96.0 %collective-permute-start.62 = (bf16[4,2,1,64,4096]{4,3,2,1,0:T(8,128)(2,1)}, bf16[4,2,1,64,4096]{4,3,2,1,0:T(8,128)(2,1)S(1)}, u32[]{:S(2)}, u32[]{:S(2)}) collective-permute-start(bf16[4,2,1,64,4096]{4,3,2,1,0:T(8,128)(2,1)} %broadcast_select_fusion), channel_id=1, source_target_pairs={{0,2},{2,0},{4,6},{6,4},{8,10},{10,8},{12,14},{14,12},{16,18},{18,... | collective-permute-start | bytes 12582920 | tf_op jit(solution)/shard_map/ppermute | solution.py:663
  476.0 6.0 collective-permute-start.58
  482.0 10.7 %collective-permute-start.51 = (bf16[4,1,1,64,768]{4,3,2,1,0:T(8,128)(2,1)S(1)}, bf16[4,1,1,64,768]{4,3,2,1,0:T(8,128)(2,1)S(1)}, u32[]{:S(2)}, u32[]{:S(2)}) collective-permute-start(bf16[4,1,1,64,768]{4,3,2,1,0:T(8,128)(2,1)S(1)} %broadcast_select_fusion.13), channel_id=1, source_target_pairs={{0,4},{2,6},{4,0},{6,2},{8,12},{10,14},{12,8},{14,10},{16,20},{18,... | collective-permute-start | bytes 1179656 | tf_op jit(solution)/shard_map/ppermute | solution.py:663
  488.7 33.3 %collective-permute-start.68 = (bf16[4,2,1,128,1024]{4,3,2,1,0:T(8,128)(2,1)S(1)}, bf16[4,2,1,128,1024]{4,3,2,1,0:T(8,128)(2,1)S(1)}, u32[]{:S(2)}, u32[]{:S(2)}) collective-permute-start(bf16[4,2,1,128,1024]{4,3,2,1,0:T(8,128)(2,1)S(1)} %copy-done.27), channel_id=1, source_target_pairs={{0,2},{2,0},{4,6},{6,4},{8,10},{10,8},{12,14},{14,12},{16,18},{18,... | collective-permute-start | bytes 6291464 | tf_op jit(solution)/shard_map/ppermute | solution.py:663
  504.1 5.9 collective-permute-start.61
  516.0 5.9 collective-permute-start.54
  518.8 20.5 %collective-permute-start.45 = (bf16[4,1,1,96,1024]{4,3,2,1,0:T(8,128)(2,1)S(1)}, bf16[4,1,1,96,1024]{4,3,2,1,0:T(8,128)(2,1)S(1)}, u32[]{:S(2)}, u32[]{:S(2)}) collective-permute-start(bf16[4,1,1,96,1024]{4,3,2,1,0:T(8,128)(2,1)S(1)} %broadcast_select_fusion.10), channel_id=1, source_target_pairs={{0,4},{2,6},{4,0},{6,2},{8,12},{10,14},{12,8},{14,10},{16,20},{18,... | collective-permute-start | bytes 2359304 | tf_op jit(solution)/shard_map/ppermute | solution.py:663
  521.9 19.7 %collective-permute-start.55 = (bf16[1,1,1,64,384]{4,3,2,1,0:T(8,128)(2,1)S(1)}, bf16[1,1,1,64,384]{4,3,2,1,0:T(8,128)(2,1)S(1)}, u32[]{:S(2)}, u32[]{:S(2)}) collective-permute-start(bf16[1,1,1,64,384]{4,3,2,1,0:T(8,128)(2,1)S(1)} %add_convert_fusion.27), channel_id=1, source_target_pairs={{0,8},{2,10},{4,12},{6,14},{8,16},{10,18},{12,20},{14,22},{16,24},... | collective-permute-start | bytes 147464 | tf_op jit(solution)/shard_map/ppermute | solution.py:663
  523.7 31.3 %collective-permute-start.69 = (bf16[4,1,1,128,1024]{4,3,2,1,0:T(8,128)(2,1)S(1)}, bf16[4,1,1,128,1024]{4,3,2,1,0:T(8,128)(2,1)S(1)}, u32[]{:S(2)}, u32[]{:S(2)}) collective-permute-start(bf16[4,1,1,128,1024]{4,3,2,1,0:T(8,128)(2,1)S(1)} %broadcast_select_fusion.6), channel_id=1, source_target_pairs={{0,4},{2,6},{4,0},{6,2},{8,12},{10,14},{12,8},{14,10},{16,20},{18,... | collective-permute-start | bytes 3145736 | tf_op jit(solution)/shard_map/ppermute | solution.py:663
  539.8 7.8 %collective-permute-start.46 = (bf16[4,1,1,96,512]{4,3,2,1,0:T(8,128)(2,1)S(1)}, bf16[4,1,1,96,512]{4,3,2,1,0:T(8,128)(2,1)S(1)}, u32[]{:S(2)}, u32[]{:S(2)}) collective-permute-start(bf16[4,1,1,96,512]{4,3,2,1,0:T(8,128)(2,1)S(1)} %broadcast_select_fusion.14), channel_id=1, source_target_pairs={{0,1},{1,0},{2,3},{3,2},{4,5},{5,4},{6,7},{7,6},{8,9},{9,8},{10,11... | collective-permute-start | bytes 1179656 | tf_op jit(solution)/shard_map/ppermute | solution.py:663
  547.8 27.5 %collective-permute-start.47 = (bf16[1,1,1,96,512]{4,3,2,1,0:T(8,128)(2,1)S(1)}, bf16[1,1,1,96,512]{4,3,2,1,0:T(8,128)(2,1)S(1)}, u32[]{:S(2)}, u32[]{:S(2)}) collective-permute-start(bf16[1,1,1,96,512]{4,3,2,1,0:T(8,128)(2,1)S(1)} %constant_dynamic-slice_fusion.4), channel_id=1, source_target_pairs={{0,8},{2,10},{4,12},{6,14},{8,16},{10,18},{12,20},{14,22},{16,24},... | collective-permute-start | bytes 294920 | tf_op jit(solution)/shard_map/ppermute | solution.py:663
  555.7 14.9 %collective-permute-start.70 = (bf16[4,1,1,128,512]{4,3,2,1,0:T(8,128)(2,1)S(1)}, bf16[4,1,1,128,512]{4,3,2,1,0:T(8,128)(2,1)S(1)}, u32[]{:S(2)}, u32[]{:S(2)}) collective-permute-start(bf16[4,1,1,128,512]{4,3,2,1,0:T(8,128)(2,1)S(1)} %broadcast_select_fusion.11), channel_id=1, source_target_pairs={{0,1},{1,0},{2,3},{3,2},{4,5},{5,4},{6,7},{7,6},{8,9},{9,8},{10,11... | collective-permute-start | bytes 1572872 | tf_op jit(solution)/shard_map/ppermute | solution.py:663
  561.0 49.0 %collective-permute-start.39 = (bf16[4,2,1,64,1676]{4,3,2,1,0:T(8,128)(2,1)S(1)}, bf16[4,2,1,64,1676]{4,3,2,1,0:T(8,128)(2,1)S(1)}, u32[]{:S(2)}, u32[]{:S(2)}) collective-permute-start(bf16[4,2,1,64,1676]{4,3,2,1,0:T(8,128)(2,1)S(1)} %broadcast_select_fusion.4), channel_id=1, source_target_pairs={{0,1},{1,0},{2,3},{3,2},{4,5},{5,4},{6,7},{7,6},{8,9},{9,8},{10,11... | collective-permute-start | bytes 5148680 | tf_op jit(solution)/shard_map/ppermute | solution.py:663
  573.5 73.7 %collective-permute-start.63 = (bf16[4,2,1,64,2048]{4,3,2,1,0:T(8,128)(2,1)S(1)}, bf16[4,2,1,64,2048]{4,3,2,1,0:T(8,128)(2,1)S(1)}, u32[]{:S(2)}, u32[]{:S(2)}) collective-permute-start(bf16[4,2,1,64,2048]{4,3,2,1,0:T(8,128)(2,1)S(1)} %broadcast_select_fusion.3), channel_id=1, source_target_pairs={{0,1},{1,0},{2,3},{3,2},{4,5},{5,4},{6,7},{7,6},{8,9},{9,8},{10,11... | collective-permute-start | bytes 6291464 | tf_op jit(solution)/shard_map/ppermute | solution.py:663
  575.3 6.8 collective-permute-start.71
  575.4 7.8 %collective-permute-start.48 = (bf16[1,1,1,96,512]{4,3,2,1,0:T(8,128)(2,1)S(1)}, bf16[1,1,1,96,512]{4,3,2,1,0:T(8,128)(2,1)S(1)}, u32[]{:S(2)}, u32[]{:S(2)}) collective-permute-start(bf16[1,1,1,96,512]{4,3,2,1,0:T(8,128)(2,1)S(1)} %add_convert_fusion.26), channel_id=1, source_target_pairs={{0,8},{2,10},{4,12},{6,14},{8,16},{10,18},{12,20},{14,22},{16,24},... | collective-permute-start | bytes 294920 | tf_op jit(solution)/shard_map/ppermute | solution.py:663
  582.2 6.8 collective-permute-start.72
  583.2 66.4 %collective-permute-start.49 = (bf16[1,1,1,96,512]{4,3,2,1,0:T(8,128)(2,1)S(1)}, bf16[1,1,1,96,512]{4,3,2,1,0:T(8,128)(2,1)S(1)}, u32[]{:S(2)}, u32[]{:S(2)}) collective-permute-start(bf16[1,1,1,96,512]{4,3,2,1,0:T(8,128)(2,1)S(1)} %add_convert_fusion.25), channel_id=1, source_target_pairs={{0,8},{2,10},{4,12},{6,14},{8,16},{10,18},{12,20},{14,22},{16,24},... | collective-permute-start | bytes 294920 | tf_op jit(solution)/shard_map/ppermute | solution.py:663
  589.0 61.3 %collective-permute-start.73 = (bf16[1,1,1,128,512]{4,3,2,1,0:T(8,128)(2,1)S(1)}, bf16[1,1,1,128,512]{4,3,2,1,0:T(8,128)(2,1)S(1)}, u32[]{:S(2)}, u32[]{:S(2)}) collective-permute-start(bf16[1,1,1,128,512]{4,3,2,1,0:T(8,128)(2,1)S(1)} %add_convert_fusion.22), channel_id=1, source_target_pairs={{0,8},{2,10},{4,12},{6,14},{8,16},{10,18},{12,20},{14,22},{16,24},... | collective-permute-start | bytes 393224 | tf_op jit(solution)/shard_map/ppermute | solution.py:663
  611.5 39.5 %collective-permute-start.40 = (bf16[4,1,1,64,1676]{4,3,2,1,0:T(8,128)(2,1)S(1)}, bf16[4,1,1,64,1676]{4,3,2,1,0:T(8,128)(2,1)S(1)}, u32[]{:S(2)}, u32[]{:S(2)}) collective-permute-start(bf16[4,1,1,64,1676]{4,3,2,1,0:T(8,128)(2,1)S(1)} %broadcast_select_fusion.8), channel_id=1, source_target_pairs={{0,4},{2,6},{4,0},{6,2},{8,12},{10,14},{12,8},{14,10},{16,20},{18,... | collective-permute-start | bytes 2574344 | tf_op jit(solution)/shard_map/ppermute | solution.py:663
  648.7 17.5 %collective-permute-start.64 = (bf16[4,1,1,64,2048]{4,3,2,1,0:T(8,128)(2,1)S(1)}, bf16[4,1,1,64,2048]{4,3,2,1,0:T(8,128)(2,1)S(1)}, u32[]{:S(2)}, u32[]{:S(2)}) collective-permute-start(bf16[4,1,1,64,2048]{4,3,2,1,0:T(8,128)(2,1)S(1)} %broadcast_select_fusion.7), channel_id=1, source_target_pairs={{0,4},{2,6},{4,0},{6,2},{8,12},{10,14},{12,8},{14,10},{16,20},{18,... | collective-permute-start | bytes 3145736 | tf_op jit(solution)/shard_map/ppermute | solution.py:663
  651.4 15.5 %collective-permute-start.41 = (bf16[1,1,1,64,1676]{4,3,2,1,0:T(8,128)(2,1)S(1)}, bf16[1,1,1,64,1676]{4,3,2,1,0:T(8,128)(2,1)S(1)}, u32[]{:S(2)}, u32[]{:S(2)}) collective-permute-start(bf16[1,1,1,64,1676]{4,3,2,1,0:T(8,128)(2,1)S(1)} %constant_dynamic-slice_fusion.5), channel_id=1, source_target_pairs={{0,8},{2,10},{4,12},{6,14},{8,16},{10,18},{12,20},{14,22},{16,24},... | collective-permute-start | bytes 643592 | tf_op jit(solution)/shard_map/ppermute | solution.py:663
  666.9 11.1 %collective-permute-start.65 = (bf16[1,1,1,64,2048]{4,3,2,1,0:T(8,128)(2,1)S(1)}, bf16[1,1,1,64,2048]{4,3,2,1,0:T(8,128)(2,1)S(1)}, u32[]{:S(2)}, u32[]{:S(2)}) collective-permute-start(bf16[1,1,1,64,2048]{4,3,2,1,0:T(8,128)(2,1)S(1)} %constant_dynamic-slice_fusion.1), channel_id=1, source_target_pairs={{0,8},{2,10},{4,12},{6,14},{8,16},{10,18},{12,20},{14,22},{16,24},... | collective-permute-start | bytes 786440 | tf_op jit(solution)/shard_map/ppermute | solution.py:663
  667.0 15.9 %collective-permute-start.42 = (bf16[1,1,1,64,1676]{4,3,2,1,0:T(8,128)(2,1)S(1)}, bf16[1,1,1,64,1676]{4,3,2,1,0:T(8,128)(2,1)S(1)}, u32[]{:S(2)}, u32[]{:S(2)}) collective-permute-start(bf16[1,1,1,64,1676]{4,3,2,1,0:T(8,128)(2,1)S(1)} %add_convert_fusion.20), channel_id=1, source_target_pairs={{0,8},{2,10},{4,12},{6,14},{8,16},{10,18},{12,20},{14,22},{16,24},... | collective-permute-start | bytes 643592 | tf_op jit(solution)/shard_map/ppermute | solution.py:663
  678.0 8.2 %collective-permute-start.66 = (bf16[1,1,1,64,2048]{4,3,2,1,0:T(8,128)(2,1)S(1)}, bf16[1,1,1,64,2048]{4,3,2,1,0:T(8,128)(2,1)S(1)}, u32[]{:S(2)}, u32[]{:S(2)}) collective-permute-start(bf16[1,1,1,64,2048]{4,3,2,1,0:T(8,128)(2,1)S(1)} %add_convert_fusion.17), channel_id=1, source_target_pairs={{0,8},{2,10},{4,12},{6,14},{8,16},{10,18},{12,20},{14,22},{16,24},... | collective-permute-start | bytes 786440 | tf_op jit(solution)/shard_map/ppermute | solution.py:663
  682.9 7.9 %collective-permute-start.43 = (bf16[1,1,1,64,1676]{4,3,2,1,0:T(8,128)(2,1)S(1)}, bf16[1,1,1,64,1676]{4,3,2,1,0:T(8,128)(2,1)S(1)}, u32[]{:S(2)}, u32[]{:S(2)}) collective-permute-start(bf16[1,1,1,64,1676]{4,3,2,1,0:T(8,128)(2,1)S(1)} %add_convert_fusion.19), channel_id=1, source_target_pairs={{0,8},{2,10},{4,12},{6,14},{8,16},{10,18},{12,20},{14,22},{16,24},... | collective-permute-start | bytes 643592 | tf_op jit(solution)/shard_map/ppermute | solution.py:663
  686.3 8.2 %collective-permute-start.67 = (bf16[1,1,1,64,2048]{4,3,2,1,0:T(8,128)(2,1)S(1)}, bf16[1,1,1,64,2048]{4,3,2,1,0:T(8,128)(2,1)S(1)}, u32[]{:S(2)}, u32[]{:S(2)}) collective-permute-start(bf16[1,1,1,64,2048]{4,3,2,1,0:T(8,128)(2,1)S(1)} %add_convert_fusion.16), channel_id=1, source_target_pairs={{0,8},{2,10},{4,12},{6,14},{8,16},{10,18},{12,20},{14,22},{16,24},... | collective-permute-start | bytes 786440 | tf_op jit(solution)/shard_map/ppermute | solution.py:663
  (79 other events, 775.2 us)

commit v2 on v1

--- a/solution.py
+++ b/solution.py
@@ -1,7 +1,10 @@
+import functools
+
 import jax
 import jax.numpy as jnp
 from jax import lax
 from jax.experimental import pallas as pl
+from jax.experimental.layout import Layout, with_layout_constraint
 from jax.experimental.pallas import tpu as pltpu
 from jax.sharding import PartitionSpec as P
 
@@ -654,12 +657,12 @@
     )
 
 
-def ring(value, axis, stride, size):
+def shift(value, axis, stride, size, by=1):
     count = lax.axis_size(axis)
     pairs = []
     for place in range(count):
         own = place // stride % size
-        pairs.append((place, place + ((own + 1) % size - own) * stride))
+        pairs.append((place, place + ((own + by) % size - own) * stride))
     return lax.ppermute(value, axis, pairs)
 
 
@@ -682,11 +685,12 @@
     )
 
 
-def gather_stage(value, axis, stride, size, dim):
-    parts = [value]
-    for _ in range(size - 1):
-        parts.append(ring(parts[-1], axis, stride, size))
-    return in_order(parts, own_place(axis, stride, size), dim)
+def send_all(value, axis, stride, size):
+    return [value] + [shift(value, axis, stride, size, by) for by in range(1, size)]
+
+
+def join(*values):
+    return lax.optimization_barrier(values)
 
 
 def dp_factors():
@@ -696,19 +700,81 @@
     return core, row, count // (core * row)
 
 
-def gather_weight(piece, seq_last):
+def gather_far(piece, direct):
     core, row, far = dp_factors()
-    rows, columns = piece.shape
-    value = piece.reshape(1, 1, 1, rows, columns)
-    value = gather_stage(value, "dp", core * row, far, 0)
-    if seq_last:
-        value = gather_stage(value, "dp", core, row, 1)
-        value = gather_stage(value, "seq", 1, lax.axis_size("seq"), 4)
-    else:
-        value = gather_stage(value, "seq", 1, lax.axis_size("seq"), 4)
-        value = gather_stage(value, "dp", core, row, 1)
-    value = gather_stage(value, "dp", 1, core, 2)
-    return value.reshape(far * row * core, rows, value.shape[-1])
+    place = ("dp", core * row, far)
+    value = piece.reshape(1, 1, 1, 1, *piece.shape)
+    parts = [value]
+    for by in range(1, far):
+        parts.append(shift(value, *place, by) if direct else shift(parts[-1], *place))
+    return in_order(parts, own_place(*place), 1)
+
+
+def start_rings(values, places):
+    core, row, far = dp_factors()
+    stages = {"row": ("dp", core, row), "seq": ("seq", 1, lax.axis_size("seq"))}
+    parts = []
+    for value, place in zip(values, places, strict=True):
+        parts.append(send_all(value, *stages[place]))
+    return parts
+
+
+def finish_rings(parts, places):
+    core, row, far = dp_factors()
+    stages = {"row": ("dp", core, row, 2), "seq": ("seq", 1, lax.axis_size("seq"), 0)}
+    values = []
+    for part, place in zip(parts, places, strict=True):
+        axis, stride, size, dim = stages[place]
+        values.append(in_order(part, own_place(axis, stride, size), dim))
+    return values
+
+
+NEAR = ("row", "seq")
+LAST = ("seq", "row")
+
+
+def exchange_cores(parts):
+    return [(part, shift(part, "dp", 1, 2)) for part in parts]
+
+
+def place_pieces(plan, count, core_ref, *refs):
+    sources, outs = refs[:count], refs[count:]
+    core = core_ref[0]
+    for half, columns, out, out_rows in plan:
+        width = columns.stop - columns.start
+        for s in range(sources[0].shape[0]):
+            for other in range(2):
+                index = 1 - core if other else core
+                outs[out][0, 0, index, out_rows, s * width : (s + 1) * width] = sources[
+                    2 * half + other
+                ][s, 0, 0, 0, :, columns]
+
+
+def assemble(pairs, plan, outs):
+    sources = [value for pair in pairs for value in pair]
+    seq, far, row = sources[0].shape[:3]
+    core = own_place("dp", 1, 2).astype(jnp.int32).reshape(1)
+    size = 4 * sum(value.size for value in sources)
+    results = pl.pallas_call(
+        functools.partial(place_pieces, plan, len(sources)),
+        grid=(far, row),
+        out_shape=[
+            jax.ShapeDtypeStruct((far, row, 2, rows, seq * width), jnp.bfloat16)
+            for rows, width in outs
+        ],
+        in_specs=[pl.BlockSpec(memory_space=pltpu.SMEM)]
+        + [
+            pl.BlockSpec((seq, 1, 1, *value.shape[3:]), lambda f, r: (0, f, r, 0, 0, 0))
+            for value in sources
+        ],
+        out_specs=[
+            pl.BlockSpec((1, 1, 2, rows, seq * width), lambda f, r: (f, r, 0, 0, 0))
+            for rows, width in outs
+        ],
+        compiler_params=pltpu.CompilerParams(vmem_limit_bytes=32 * 1024 * 1024),
+        cost_estimate=pl.CostEstimate(flops=0, bytes_accessed=size, transcendentals=0),
+    )(core, *sources)
+    return [value.reshape(-1, value.shape[-1]) for value in results]
 
 
 def pick(value, index, size, dim):
@@ -722,54 +788,95 @@
     return lax.dynamic_slice_in_dim(value, index * width, width, dim)
 
 
-def scatter_stage(value, axis, stride, size, dim):
-    own = own_place(axis, stride, size)
-    moving = pick(value, (own + size - 1) % size, size, dim).astype(jnp.bfloat16)
-    for step in range(2, size + 1):
-        moving = ring(moving, axis, stride, size)
-        mine = pick(value, (own + size - step) % size, size, dim)
-        total = mine.astype(jnp.float32) + moving.astype(jnp.float32)
-        moving = total.astype(jnp.bfloat16)
-    return total
-
-
-def scatter_weight(grad, seq_first):
-    core, row, far = dp_factors()
-    rows = grad.shape[0] // (core * row * far)
-    value = grad.reshape(far, row, core, rows, grad.shape[1])
-    value = scatter_stage(value, "dp", 1, core, 2).astype(jnp.bfloat16)
-    if seq_first:
-        value = scatter_stage(value, "seq", 1, lax.axis_size("seq"), 4).astype(jnp.bfloat16)
-        value = scatter_stage(value, "dp", core, row, 1).astype(jnp.bfloat16)
-    else:
-        value = scatter_stage(value, "dp", core, row, 1).astype(jnp.bfloat16)
-        value = scatter_stage(value, "seq", 1, lax.axis_size("seq"), 4).astype(jnp.bfloat16)
-    value = scatter_stage(value, "dp", core * row, far, 0)
-    return value.reshape(rows, value.shape[-1])
-
-
-def scatter_small(parts):
-    core, row, far = dp_factors()
-    seq = lax.axis_size("seq")
-    value = parts.reshape(far, row, core, seq, parts.shape[-1])
-    for axis, stride, size, dim in (
-        ("dp", 1, core, 2),
-        ("seq", 1, seq, 3),
-        ("dp", core, row, 1),
-        ("dp", core * row, far, 0),
-    ):
+class Scatter:
+    def __init__(self, value, names, kind=jnp.bfloat16):
+        core, row, far = dp_factors()
+        stages = {
+            "core": ("dp", 1, core, 2),
+            "row": ("dp", core, row, 1),
+            "far": ("dp", core * row, far, 0),
+            "seq": ("seq", 1, lax.axis_size("seq"), 4),
+        }
+        self.steps = [stages[name] for name in names]
+        self.value, self.kind, self.left, self.moving = value.astype(kind), kind, 0, None
+
+    def start(self, direct=False):
+        axis, stride, size, dim = self.steps[0]
         own = own_place(axis, stride, size)
-        moving = pick(value, (own + size - 1) % size, size, dim)
-        for step in range(2, size + 1):
-            moving = ring(moving, axis, stride, size) + pick(
-                value, (own + size - step) % size, size, dim
-            )
-        value = moving
-    return value.reshape(-1)
+        if direct:
+            self.left = 1
+            self.moving = [
+                shift(pick(self.value, (own + by) % size, size, dim), axis, stride, size, by)
+                for by in range(1, size)
+            ]
+            return
+        if self.left == 0:
+            self.left = size - 1
+            self.moving = [pick(self.value, (own + size - 1) % size, size, dim)]
+        self.moving = [shift(self.moving[0], axis, stride, size)]
+
+    def finish(self):
+        axis, stride, size, dim = self.steps[0]
+        self.left -= 1
+        own = own_place(axis, stride, size)
+        total = pick(self.value, (own + self.left) % size, size, dim).astype(jnp.float32)
+        for value in self.moving:
+            total = total + value.astype(jnp.float32)
+        if self.left > 0:
+            self.moving = [total.astype(self.kind)]
+        else:
+            self.steps.pop(0)
+            self.value = total.astype(self.kind) if self.steps else total
+
+
+class Total:
+    def __init__(self, value):
+        core, row, far = dp_factors()
+        self.steps = [
+            ("dp", 1, core),
+            ("dp", core, row),
+            ("seq", 1, lax.axis_size("seq")),
+            ("dp", core * row, far),
+        ]
+        self.value = value
+
+    def start(self):
+        self.moving = send_all(self.value, *self.steps.pop(0))[1:]
+
+    def finish(self):
+        for value in self.moving:
+            self.value = self.value + value
+
+
+def meet(chains, *values):
+    moving = [chain.moving for chain in chains]
+    moving, values = join(moving, values)
+    for chain, value in zip(chains, moving, strict=True):
+        chain.moving = value
+        chain.finish()
+    return values
+
+
+def start_all(chains):
+    for chain in chains:
+        chain.start()
+
+
+def settle(chains, *values):
+    sums, values = join([chain.value for chain in chains], values)
+    for chain, value in zip(chains, sums, strict=True):
+        chain.value = value
+    return values
+
+
+SEQ_FIRST = ("core", "seq", "row", "far")
+ROW_FIRST = ("core", "row", "seq", "far")
 
 
 CHUNK = 64
 PAIR = 128
+FRONT = HEADS // KV_HEADS * HEAD_DIM + 2 * HEAD_DIM
+SPLIT = (INNER + CHANNELS + SSM_HEADS) // 2
 
 
 def dot_high(left, right):
@@ -818,21 +925,24 @@
     return scores / jnp.sum(scores, axis=1, keepdims=True)
 
 
-def attention_forward(part_ref, cos_ref, sin_ref, seg_col_ref, seg_row_ref, turned_ref, out_ref):
-    count, row_count = part_ref.shape[0], out_ref.shape[0]
+def attention_forward(*refs):
+    parts, refs = refs[: 3 * KV_HEADS], refs[3 * KV_HEADS :]
+    cos_ref, sin_ref, seg_col_ref, seg_row_ref, turned_ref, out_ref = refs
+    count, row_count = turned_ref.shape[0], out_ref.shape[0]
     halo = count - row_count
     block = min(row_count, 128)
     cosine, sine = cos_ref[...], sin_ref[...]
     seg_row = seg_row_ref[...]
     group = HEADS // KV_HEADS * HEAD_DIM
     for kv_head in range(KV_HEADS):
+        part_refs = parts[3 * kv_head : 3 * kv_head + 3]
         base = kv_head * (group + 2 * HEAD_DIM)
-        for at in range(base, base + group, PAIR):
-            turned_ref[:, at : at + PAIR] = turn(part_ref[:, at : at + PAIR], cosine, sine).astype(
-                jnp.bfloat16
-            )
+        for at in range(0, group, PAIR):
+            turned_ref[:, base + at : base + at + PAIR] = turn(
+                part_refs[at // PAIR][...], cosine, sine
+            ).astype(jnp.bfloat16)
         at = base + group
-        both = part_ref[:, at : at + PAIR]
+        both = part_refs[2][...]
         both = jnp.where(first_lanes(count), turn(both, cosine, sine), both).astype(jnp.bfloat16)
         turned_ref[:, at : at + PAIR] = both
         keys, values = twice(both.astype(jnp.float32))
@@ -925,12 +1035,23 @@
         out_ref[:halo, base : base + group] = jnp.zeros((halo, group), jnp.bfloat16)
 
 
-def load_conv(proj_ref, conv_ref):
-    count = proj_ref.shape[0]
+def column_halves(ref):
+    half = ref.shape[1] // 2
+    return ref.at[:, :half], ref.at[:, half:]
+
+
+def load_conv(first_ref, second_ref, conv_ref, split):
+    count = first_ref.shape[0]
+    early = split - INNER
     conv_ref[:8] = jnp.zeros((8, CHANNELS), jnp.float32)
-    conv_ref[8 : count + 8] = (
-        proj_ref[:, INNER : INNER + CHANNELS].astype(jnp.bfloat16).astype(jnp.float32)
-    )
+    channels = jnp.concatenate(
+        [
+            first_ref[:, FRONT + INNER : FRONT + split],
+            second_ref[:, FRONT : FRONT + CHANNELS - early],
+        ],
+        axis=1,
+    )
+    conv_ref[8 : count + 8] = channels.astype(jnp.bfloat16).astype(jnp.float32)
 
 
 def conv_chunk(conv_ref, seg_ref, taps_ref, base):
@@ -945,8 +1066,9 @@
     return total, segs
 
 
-def steps_of(proj_ref, heads_ref, base):
-    raw = proj_ref[pl.ds(base, CHUNK), INNER + CHANNELS :] + heads_ref[0:1, :SSM_HEADS]
+def steps_of(second_ref, heads_ref, base):
+    raw = second_ref[pl.ds(base, CHUNK), FRONT + SPLIT - SSM_HEADS : FRONT + SPLIT]
+    raw = raw + heads_ref[0:1, :SSM_HEADS]
     step = jnp.maximum(raw, 0.0) + jnp.log1p(jnp.exp(-jnp.abs(raw)))
     rate = -step * heads_ref[1:2, :SSM_HEADS]
     early = lax.broadcasted_iota(jnp.int32, (CHUNK, CHUNK), 0)
@@ -994,9 +1116,10 @@
     proj_ref, taps_ref, heads_ref, wide_ref, seg_ref, seg_row_ref,
     out_ref, mix_ref, states_ref, conv_ref, state_ref, gated_ref,
 ):
-    count, row_count = proj_ref.shape[0], out_ref.shape[0]
+    first_ref, second_ref = column_halves(proj_ref)
+    count, row_count = first_ref.shape[0], out_ref.shape[0]
     low = jnp.bfloat16
-    load_conv(proj_ref, conv_ref)
+    load_conv(first_ref, second_ref, conv_ref, SPLIT)
     state_ref[...] = jnp.zeros_like(state_ref)
     low_half = first_lanes(CHUNK)
 
@@ -1007,7 +1130,7 @@
         mixed = (total * jax.nn.sigmoid(total)).astype(low)
         inner = mixed[:, :INNER].astype(jnp.float32)
         state_in, state_out = mixed[:, INNER : INNER + STATE], mixed[:, INNER + STATE :]
-        _, step, _, cumul, across = steps_of(proj_ref, heads_ref, base)
+        _, step, _, cumul, across = steps_of(second_ref, heads_ref, base)
         allowed, entry, tail, carry = chunk_masks(segs, seg_row_ref[pl.ds(c, 1), :])
         shared = dot_right_t(state_out, jnp.concatenate([state_in, state_in]))
         shared = jnp.where(allowed, shared, 0.0)
@@ -1033,7 +1156,9 @@
             )
             fresh.append((stepped * (jnp.exp(end - sums) * tail)).astype(low))
             kept.append(jnp.exp(end) * carry)
-            gate = proj_ref[pl.ds(base, CHUNK), lanes]
+            gate = first_ref[
+                pl.ds(base, CHUNK), FRONT + k * PAIR : FRONT + (k + 1) * PAIR
+            ]
             gated = mix * gate * jax.nn.sigmoid(gate)
             mix_ref[pl.ds(store, CHUNK), lanes] = mix
             gated_ref[:, lanes] = gated
@@ -1049,18 +1174,18 @@
 
 
 def mixer_backward(
-    proj_ref, mix_ref, states_ref, grad_ref, taps_ref, heads_ref, wide_ref, seg_ref, seg_row_ref,
-    out_ref, taps_out_ref, wide_out_ref, heads_out_ref,
+    proj_ref, mix_ref, states_ref, grad_ref, attention_ref, taps_ref, heads_ref, wide_ref, seg_ref, seg_row_ref,
+    both_ref, sums_ref,
     conv_ref, pre_ref, adjoint_ref, mixgrad_ref, innergrad_ref,
 ):
-    count, row_count = proj_ref.shape[0], mix_ref.shape[0]
+    first_ref, second_ref = column_halves(proj_ref)
+    out_ref, other_ref = column_halves(both_ref)
+    count, row_count = first_ref.shape[0], mix_ref.shape[0]
     low = jnp.bfloat16
-    load_conv(proj_ref, conv_ref)
+    load_conv(first_ref, second_ref, conv_ref, SPLIT)
     adjoint_ref[...] = jnp.zeros_like(adjoint_ref)
     pre_ref[...] = jnp.zeros_like(pre_ref)
-    taps_out_ref[...] = jnp.zeros_like(taps_out_ref)
-    wide_out_ref[...] = jnp.zeros_like(wide_out_ref)
-    heads_out_ref[...] = jnp.zeros_like(heads_out_ref)
+    sums_ref[...] = jnp.zeros_like(sums_ref)
     low_half = first_lanes(CHUNK)
     chunks = count // CHUNK
 
@@ -1070,7 +1195,7 @@
         store = pl.multiple_of(jnp.maximum(c - 1, 0) * CHUNK, CHUNK)
         real = (c > 0).astype(jnp.float32)
 
-        gate = proj_ref[pl.ds(base, CHUNK), :INNER]
+        gate = first_ref[pl.ds(base, CHUNK), FRONT : FRONT + INNER]
         mix = mix_ref[pl.ds(store, CHUNK), :]
         norm_grad = grad_ref[pl.ds(store, CHUNK), :].astype(jnp.float32) * real
         sig = jax.nn.sigmoid(gate)
@@ -1078,14 +1203,12 @@
         gated = mix * silu
         norm = lax.rsqrt(jnp.mean(gated * gated, axis=1, keepdims=True) + EPS)
         scaled = norm_grad * wide_ref[1:2, :]
-        wide_out_ref[1:2, :] += jnp.sum(norm_grad * gated * norm, axis=0, keepdims=True)
+        sums_ref[5:6, :INNER] += jnp.sum(norm_grad * gated * norm, axis=0, keepdims=True)
         pull = jnp.mean(gated * scaled, axis=1, keepdims=True) * (norm * norm * norm)
         gated_grad = norm * scaled - gated * pull
         mix_grad = gated_grad * silu
         mixgrad_ref[...] = mix_grad
-        out_ref[pl.ds(base, CHUNK), :INNER] = (
-            gated_grad * mix * (sig * (1.0 + gate * (1.0 - sig)))
-        ).astype(low)
+        gate_grad = (gated_grad * mix * (sig * (1.0 + gate * (1.0 - sig)))).astype(low)
 
         total, segs = conv_chunk(conv_ref, seg_ref, taps_ref, base)
         sig = jax.nn.sigmoid(total)
@@ -1093,8 +1216,8 @@
         slope = sig * (1.0 + total * (1.0 - sig))
         inner = mixed[:, :INNER].astype(jnp.float32)
         state_in, state_out = mixed[:, INNER : INNER + STATE], mixed[:, INNER + STATE :]
-        wide_out_ref[0:1, :] += jnp.sum(mix_grad * inner, axis=0, keepdims=True)
-        raw, step, rate, cumul, across = steps_of(proj_ref, heads_ref, base)
+        sums_ref[6:7, :INNER] += jnp.sum(mix_grad * inner, axis=0, keepdims=True)
+        raw, step, rate, cumul, across = steps_of(second_ref, heads_ref, base)
         allowed, entry, tail, carry = chunk_masks(segs, seg_row_ref[pl.ds(c, 1), :])
         twice_in = jnp.concatenate([state_in, state_in])
         shared = jnp.where(allowed, dot_right_t(state_out, twice_in), 0.0)
@@ -1184,18 +1307,17 @@
         late = lax.broadcasted_iota(jnp.int32, (CHUNK, CHUNK), 1)
         rate_grad = dot_high((late >= early).astype(jnp.float32), sum_grad)
         raw_grad = (step_grad - rate_grad * heads_ref[1:2, :SSM_HEADS]) * jax.nn.sigmoid(raw)
-        heads_out_ref[0:1, :SSM_HEADS] += jnp.sum(raw_grad, axis=0, keepdims=True)
-        heads_out_ref[1:2, :SSM_HEADS] += jnp.sum(rate_grad * rate, axis=0, keepdims=True)
-        out_ref[pl.ds(base, CHUNK), INNER + CHANNELS :] = raw_grad.astype(low)
+        sums_ref[7:8, :SSM_HEADS] += jnp.sum(raw_grad, axis=0, keepdims=True)
+        sums_ref[8:9, :SSM_HEADS] += jnp.sum(rate_grad * rate, axis=0, keepdims=True)
 
         pre = jnp.concatenate([innergrad_ref[...], in_grad, out_grad], axis=1) * slope
-        taps_out_ref[CONV : CONV + 1, :] += jnp.sum(pre, axis=0, keepdims=True)
+        sums_ref[CONV : CONV + 1, :] += jnp.sum(pre, axis=0, keepdims=True)
         rows = conv_ref[pl.ds(base, CHUNK + 8), :]
         own = segs[8:]
         for offset in range(CONV):
             at = 8 - (CONV - 1) + offset
             same = segs[at : at + CHUNK] == own
-            taps_out_ref[offset : offset + 1, :] += jnp.sum(
+            sums_ref[offset : offset + 1, :] += jnp.sum(
                 jnp.where(same, pre * rows[at : at + CHUNK], 0.0), axis=0, keepdims=True
             )
         later = jnp.concatenate([pre, pre_ref[...]])
@@ -1207,20 +1329,40 @@
             conv_grad = conv_grad + jnp.where(
                 same, later[at : at + CHUNK] * taps_ref[offset : offset + 1], 0.0
             )
-        out_ref[pl.ds(base, CHUNK), INNER : INNER + CHANNELS] = conv_grad.astype(low)
+        conv_grad = conv_grad.astype(low)
+        early = SPLIT - INNER
+        rest = jnp.zeros((CHUNK, out_ref.shape[1] - FRONT - SPLIT), low)
+        out_ref[pl.ds(base, CHUNK), :] = jnp.concatenate(
+            [attention_ref[pl.ds(base, CHUNK), :FRONT], gate_grad, conv_grad[:, :early], rest],
+            axis=1,
+        )
+        other_ref[pl.ds(base, CHUNK), :] = jnp.concatenate(
+            [
+                attention_ref[pl.ds(base, CHUNK), FRONT:],
+                conv_grad[:, early:],
+                raw_grad.astype(low),
+                rest,
+            ],
+            axis=1,
+        )
         pre_ref[...] = pre[:8]
         return 0
 
     lax.fori_loop(0, chunks, body, 0)
 
 
-def call(kernel, outs, scratch, flops, *args):
+def call(kernel, outs, scratch, flops, *args, blocks=()):
     size = sum(a.size * a.dtype.itemsize for a in args)
     whole = pl.BlockSpec(memory_space=pltpu.VMEM)
+    specs = [
+        pl.BlockSpec((args[0].shape[0], PAIR), functools.partial(lambda at, _: (0, at), at))
+        for at in blocks
+    ]
     return pl.pallas_call(
         kernel,
+        grid=(1,) if blocks else (),
         out_shape=[jax.ShapeDtypeStruct(shape, kind) for shape, kind in outs],
-        in_specs=[whole] * len(args),
+        in_specs=specs + [whole] * (len(args) - len(blocks)),
         out_specs=[whole] * len(outs),
         scratch_shapes=[pltpu.VMEM(shape, jnp.float32) for shape in scratch],
         compiler_params=pltpu.CompilerParams(vmem_limit_bytes=56 * 1024 * 1024),
@@ -1260,14 +1402,52 @@
     small = jnp.concatenate(
         [input_gain, conv_weight.reshape(-1), conv_bias, mixer_gain, hidden_gain]
     )
-    per_row = w_query.shape[1] + w_key.shape[1] + w_value.shape[1]
-    small = jnp.pad(small, (0, 16 * per_row - small.shape[0])).reshape(16, per_row)
-    qkv_piece = jnp.concatenate([w_query, w_key, w_value], axis=1)
-    qkv_rows = qkv_piece.shape[0]
-    qkv = gather_weight(jnp.concatenate([qkv_piece, small]), False)
-    smalls = (
-        qkv[:, qkv_rows:].reshape(dp_count, 16, 2, per_row).transpose(0, 2, 1, 3)
-    ).reshape(2 * dp_count, 16 * per_row)
+    rows = w_query.shape[0]
+    small = jnp.pad(small, (0, -small.shape[0] % rows)).reshape(rows, -1)
+    small_width = small.shape[1]
+    half_q, half_k = w_query.shape[1], w_key.shape[1]
+    front = half_q + 2 * half_k
+    split = mixer_in.shape[1]
+    first_piece = jnp.concatenate([w_query, w_key, w_value, mixer_in, small], axis=1)
+    first_piece = jnp.pad(first_piece, ((0, 0), (0, -first_piece.shape[1] % 128)))
+    first_width = first_piece.shape[1]
+    half_ff, half_width = w_gate.shape[1], mixer_out.shape[1]
+    out_piece = jnp.concatenate([mixer_out, w_output])
+    second_piece = jnp.concatenate(
+        [w_gate, w_up]
+        + [
+            value[at : at + rows]
+            for value in (out_piece, w_down)
+            for at in range(0, value.shape[0], rows)
+        ],
+        axis=1,
+    )
+    first_far = gather_far(first_piece, True)
+    both = slice(0, rows // 2), slice(rows // 2, rows)
+
+    def halves(value):
+        return [value[:, :, :, :, half] for half in both]
+
+    first_near = finish_rings(start_rings(halves(first_far), NEAR), NEAR)
+    second_piece, first_near = join(second_piece, first_near)
+    second_far = gather_far(second_piece, False)
+    first_last = finish_rings(start_rings(first_near, LAST), LAST)
+    (weights_one,) = assemble(
+        exchange_cores(first_last),
+        [(half, slice(0, first_width), 0, both[half]) for half in range(2)],
+        [(rows, first_width)],
+    )
+    second_far, weights_one = join(second_far, weights_one)
+    second_near = start_rings(halves(second_far), NEAR)
+
+    smalls = jnp.stack(
+        [
+            weights_one[:, at + front + split : at + front + split + small_width]
+            for at in (0, first_width)
+        ]
+    )
+    smalls = smalls.reshape(2, dp_count, -1)
+    smalls = smalls.transpose(1, 0, 2).reshape(2 * dp_count, -1)
     sizes = [
         input_gain.shape[0],
         conv_weight.size,
@@ -1282,14 +1462,23 @@
     ]
     full_input_gain, full_conv_weight, full_conv_bias, full_mixer_gain, full_hidden_gain = gains
     full_conv_weight = full_conv_weight.reshape(-1, CONV)
-    qkv = qkv[:, :qkv_rows].reshape(width, 2 * per_row)
-    half_q, half_k = w_query.shape[1], w_key.shape[1]
-    full_mixer_in = gather_weight(mixer_in, True).reshape(width, -1)
-    outs = gather_weight(jnp.concatenate([mixer_out, w_output]), False)
-    full_mixer_out = outs[:, : mixer_out.shape[0]].reshape(-1, width)
-    full_output = outs[:, mixer_out.shape[0] :].reshape(-1, width)
-    gate_up = gather_weight(jnp.concatenate([w_gate, w_up], axis=1), True).reshape(width, -1)
-    full_down = gather_weight(w_down, False).reshape(-1, width)
+
+    half_rows = rows // 2
+
+    def half_sums(grad):
+        return [
+            Scatter(grad[:, :, :, :half_rows], SEQ_FIRST),
+            Scatter(grad[:, :, :, half_rows:], ROW_FIRST),
+        ]
+
+    def row_major(value):
+        return with_layout_constraint(value, Layout(tuple(range(value.ndim))))
+
+    def weight_grad(left, right):
+        core, row, far = dp_factors()
+        grad = row_major(dot_left_t(left, right).astype(low))
+        return grad.reshape(far, row, core, -1, right.shape[1])
+
 
     seg_all = segments[0]
     tail = lax.ppermute(tokens[row_count - halo :], "seq", [(0, 1)])
@@ -1310,21 +1499,38 @@
     angle = places.astype(f32)[:, None] * (THETA ** (-(lane % half).astype(f32) / half))[None, :]
     cosine = jnp.cos(angle)
     sine = jnp.sin(angle) * jnp.where(lane % HEAD_DIM < half, -1.0, 1.0)[None, :]
+    projected = row_major(dot_plain(normed_low, weights_one))
+    second_near, projected = join(second_near, projected)
+    second_near = finish_rings(second_near, NEAR)
+    base_out = 2 * half_ff
+    base_down = base_out + 2 * half_width
+    second_near, projected = join(
+        [
+            [value[..., :base_down] for value in second_near],
+            [value[..., base_down:] for value in second_near],
+        ],
+        projected,
+    )
+    second_last = start_rings(second_near[0], LAST)
+    blocks = [at + k for at in (0, first_width // PAIR) for k in range(front // PAIR)]
     turned, attended_low = call(
         attention_forward,
-        [((count, 2 * per_row), low), ((row_count, HEADS * HEAD_DIM), low)],
+        [((count, 2 * front), low), ((row_count, HEADS * HEAD_DIM), low)],
         [],
-        10**10,
-        dot_plain(normed_low, qkv),
+        10**9,
+        *[projected] * len(blocks),
         cosine,
         sine,
         seg_col,
         seg_row,
-    )
-
-    projected = dot_plain(normed_low, full_mixer_in)
+        blocks=blocks,
+    )
+    projected, attended_low = join(projected, attended_low)
+
     chunks = count // CHUNK
-    seg_conv = jnp.concatenate([jnp.full((8,), -1, jnp.int32), seg_ext, jnp.full((8,), -9, jnp.int32)])
+    seg_conv = jnp.concatenate(
+        [jnp.full((8,), -1, jnp.int32), seg_ext, jnp.full((8,), -9, jnp.int32)]
+    )
     seg_conv = seg_conv[:, None]
     seg_chunks = jnp.concatenate([seg_ext.reshape(chunks, CHUNK)] * 2, axis=1)
     taps = jnp.concatenate([full_conv_weight.T, full_conv_bias[None]])
@@ -1338,7 +1544,7 @@
             ((chunks, STATE, INNER), low),
         ],
         [(count + 8, CHANNELS), (STATE, INNER), (CHUNK, INNER)],
-        2 * 10**10,
+        10**9,
         projected,
         taps,
         heads,
@@ -1346,6 +1552,32 @@
         seg_conv,
         seg_chunks,
     )
+    second_last, mixed_low = join(second_last, mixed_low)
+    second_last = finish_rings(second_last, LAST)
+    second_near[1], second_last = join(second_near[1], second_last)
+    third_last = start_rings(second_near[1], LAST)
+    pieces, down_pieces = [], []
+    for half in range(2):
+        pieces.append((half, slice(0, base_out), 0, both[half]))
+        for k in range(2):
+            at = k * rows + half * (rows // 2)
+            columns = slice(k * half_width, (k + 1) * half_width)
+            down_pieces.append((half, columns, 0, slice(at, at + rows // 2)))
+            columns = slice(base_out + k * half_width, base_out + (k + 1) * half_width)
+            if at < mixer_out.shape[0]:
+                pieces.append((half, columns, 1, slice(at, at + rows // 2)))
+            else:
+                at -= mixer_out.shape[0]
+                pieces.append((half, columns, 2, slice(at, at + rows // 2)))
+    gate_up, full_mixer_out, full_output = assemble(
+        exchange_cores(second_last),
+        pieces,
+        [
+            (rows, base_out),
+            (mixer_out.shape[0], half_width),
+            (w_output.shape[0], half_width),
+        ],
+    )
     hidden_mid = (
         hidden_ext[halo:]
         + dot_plain(attended_low, full_output)
@@ -1353,56 +1585,79 @@
     )
     normed_two, norm_two_pull = jax.vjp(rms_scale, hidden_mid, full_hidden_gain)
     normed_two_low = normed_two.astype(low)
+    third_last, normed_two_low = join(third_last, normed_two_low)
+    third_cores = exchange_cores(finish_rings(third_last, LAST))
     gate_up_part = dot_plain(normed_two_low, gate_up)
-    half_ff = w_gate.shape[1]
-    gate_part = two_halves(gate_up_part, 0, half_ff)
-    up_part = two_halves(gate_up_part, 1, half_ff)
-    sigmoid_gate = jax.nn.sigmoid(gate_part)
-    activated_low = (gate_part * sigmoid_gate * up_part).astype(low)
+    ffn = []
+    for k in range(2):
+        gate_part, up_part = (
+            gate_up_part[:, at : at + half_ff]
+            for at in (2 * k * half_ff, (2 * k + 1) * half_ff)
+        )
+        sigmoid_gate = jax.nn.sigmoid(gate_part)
+        ffn.append((gate_part, up_part, sigmoid_gate))
+    (full_down,) = assemble(third_cores, down_pieces, [(w_down.shape[0], half_width)])
+    activated_low = jnp.concatenate([(g * s * u).astype(low) for g, u, s in ffn], axis=1)
     output = (hidden_mid + dot_plain(activated_low, full_down)).astype(low)
 
+    grad_down = weight_grad(activated_low, cotangent)
+    down = Scatter(grad_down, ROW_FIRST)
+    down.start()
     act_grad = dot_right_t(cotangent, full_down)
-    grad_down = scatter_weight(dot_left_t(activated_low, cotangent).astype(low), False)
-    gate_grad_low, up_grad_low = ffn_backward_grads(act_grad, gate_part, up_part, sigmoid_gate)
-    gate_up_grad = jnp.concatenate(
-        [
-            gate_grad_low[:, :half_ff],
-            up_grad_low[:, :half_ff],
-            gate_grad_low[:, half_ff:],
-            up_grad_low[:, half_ff:],
-        ],
-        axis=1,
-    )
-    grad_gate_up = scatter_weight(dot_left_t(normed_two_low, gate_up_grad).astype(low), True)
-    normed_two_grad = dot_right_t(gate_up_grad, gate_up)
+    gate_up_grad = []
+    for k in range(2):
+        gate_grad, up_grad = ffn_backward_grads(
+            act_grad[:, k * half_ff : (k + 1) * half_ff], *ffn[k]
+        )
+        gate_up_grad += [gate_grad, up_grad]
+    gate_up_grad = jnp.concatenate(gate_up_grad, axis=1)
+    (gate_up_grad,) = meet([down], gate_up_grad)
+    down.start()
+    grad_gate_up = weight_grad(normed_two_low, gate_up_grad)
+    grad_gate_up, gate_up_grad = join(grad_gate_up, gate_up_grad)
+    ffn_sums = half_sums(grad_gate_up)
+    start_all(ffn_sums)
+    normed_two_grad = row_major(
+        dot_right_t(gate_up_grad, gate_up)
+    )
     hidden_part, hidden_gain_grad = norm_two_pull(normed_two_grad)
     hidden_grad = cotangent.astype(jnp.float32) + hidden_part
     branch_low = hidden_grad.astype(low)
-    grad_mixer_out = scatter_weight(dot_left_t(mixed_low, branch_low).astype(low), False)
-    grad_output = scatter_weight(dot_left_t(attended_low, branch_low).astype(low), True)
-
+    (branch_low,) = meet(ffn_sums, branch_low)
+    start_all(ffn_sums)
+
+    grad_outs = jnp.concatenate(
+        [
+            weight_grad(mixed_low, branch_low),
+            weight_grad(attended_low, branch_low),
+        ],
+        axis=3,
+    )
+    outs = Scatter(grad_outs, ROW_FIRST)
+    outs.start()
+    attended_grad = dot_right_t(branch_low, full_output).astype(low)
+    norm_grad = row_major(dot_right_t(branch_low, full_mixer_out))
     (qkv_grad,) = call(
         attention_backward,
-        [((count, 2 * per_row), low)],
+        [((count, 2 * front), low)],
         [(count, PAIR), (count, PAIR)],
-        2 * 10**10,
+        10**9,
         turned,
-        dot_right_t(branch_low, full_output).astype(low),
+        attended_grad,
         cosine,
         sine,
         seg_col,
         seg_row,
     )
-    grad_qkv = scatter_weight(dot_left_t(normed_low, qkv_grad).astype(low), False)
-
-    norm_grad = dot_right_t(branch_low, full_mixer_out)
-    proj_grad_low, taps_grad, wide_grad, heads_grad = call(
+    others = [*ffn_sums, down, outs]
+    qkv_grad, norm_grad = meet(others, qkv_grad, norm_grad)
+    (qkv_grad,) = settle(others, qkv_grad)
+    start_all(others)
+    proj_grad, small_sums = call(
         mixer_backward,
         [
-            ((count, INNER + CHANNELS + SSM_HEADS), low),
-            ((8, CHANNELS), f32),
-            ((8, INNER), f32),
-            ((8, PAIR), f32),
+            ((count, 2 * first_width), low),
+            ((16, CHANNELS), f32),
         ],
         [
             (count + 8, CHANNELS),
@@ -1411,74 +1666,90 @@
             (CHUNK, INNER),
             (CHUNK, INNER),
         ],
-        4 * 10**10,
+        10**9,
         projected,
         mix,
         states,
         norm_grad,
+        qkv_grad,
         taps,
         heads,
         wide,
         seg_conv,
         seg_chunks,
     )
-    conv_weight_grad, conv_bias_grad = taps_grad[:CONV].T, taps_grad[CONV]
-    mixer_gain_grad = wide_grad[1]
-    skip_grad = jnp.sum(wide_grad[0].reshape(SSM_HEADS, SSM_DIM), axis=1)
-    bias_grad, decay_grad = heads_grad[0, :SSM_HEADS], heads_grad[1, :SSM_HEADS]
-    normed_grad = dot_right_t(proj_grad_low, full_mixer_in) + dot_right_t(qkv_grad, qkv)
-    grad_mixer_in = scatter_weight(dot_left_t(normed_low, proj_grad_low).astype(low), True)
+    (proj_grad,) = meet(others, proj_grad)
+    (proj_grad,) = settle(others, proj_grad)
+    start_all(others)
+    grad_first = weight_grad(normed_low, proj_grad)
+    grad_first, proj_grad = meet(others, grad_first, proj_grad)
+    first = half_sums(grad_first)
+    start_all([*first, *others])
+    normed_grad = row_major(dot_right_t(proj_grad, weights_one))
+    normed_grad, small_sums, hidden_gain_grad = meet(
+        [*first, *others], normed_grad, small_sums, hidden_gain_grad
+    )
+    normed_grad, small_sums, hidden_gain_grad = settle(
+        first, normed_grad, small_sums, hidden_gain_grad
+    )
+    start_all([*first, *others])
     input_part, input_gain_grad = norm_pull(normed_grad)
     returned = lax.ppermute(input_part[:halo].astype(low), "seq", [(1, 0)]).astype(jnp.float32)
     token_grad = hidden_grad + input_part[halo:]
-    token_grad = token_grad.at[row_count - halo :].add(returned)
-
-    blocks = 2 * dp_count
-    shared_sums = jnp.concatenate([bias_grad, decay_grad, skip_grad])
-    small_grads = jnp.concatenate(
-        [
-            input_gain_grad.reshape(blocks, -1),
-            conv_weight_grad.reshape(blocks, -1),
-            conv_bias_grad.reshape(blocks, -1),
-            mixer_gain_grad.reshape(blocks, -1),
-            hidden_gain_grad.reshape(blocks, -1),
-            jnp.broadcast_to(shared_sums[None], (blocks, 3 * SSM_HEADS)),
-        ],
-        axis=1,
-    )
-    sums = scatter_small(small_grads)
-    small_out = [sums[places_at[k] : places_at[k + 1]] for k in range(5)]
-    heads_out = sums[places_at[5] :].reshape(3, SSM_HEADS)
+    token_grad = token_grad + jnp.pad(returned, ((row_count - halo, 0), (0, 0)))
+
+    gain_rows = jnp.stack([hidden_gain_grad, input_gain_grad])
+    small = Total(small_sums + jnp.pad(gain_rows, ((9, 5), (0, CHANNELS - width))))
+    meet(others)
+    start_all([outs])
+    small.start()
+    meet([*first, small, outs])
+    first.append(small)
+    start_all(first)
+    meet(first)
+    start_all(first)
+    meet(first)
+    start_all(first)
+    meet(first)
+    first.pop()
+    start_all(first)
+    meet(first)
+    grad_down = down.value.reshape(-1, half_width)
+    grad_gate_up = jnp.concatenate(
+        [chain.value.reshape(half_rows, -1) for chain in ffn_sums]
+    )
+    grad_outs = outs.value.reshape(-1, half_width)
+    grad_mixer_out = grad_outs[: mixer_out.shape[0]]
+    grad_output = grad_outs[mixer_out.shape[0] :]
+    grad_first = jnp.concatenate([chain.value.reshape(half_rows, first_width) for chain in first[:2]])
+    sums = small.value
+    place = lax.axis_index("dp") * 2 + seq_rank
+
+    def own_part(row, size):
+        return lax.dynamic_slice(sums, (row, place * size), (1, size)).reshape(-1)
+
+    own_taps = lax.dynamic_slice(sums, (0, place * sizes[2]), (CONV, sizes[2]))
+    skip_grad = jnp.sum(sums[6, :INNER].reshape(SSM_HEADS, SSM_DIM), axis=1)
     return (
         output,
         token_grad,
-        small_out[0],
-        grad_mixer_in,
-        small_out[1].reshape(-1, CONV),
-        small_out[2],
-        heads_out[0],
-        heads_out[1],
-        heads_out[2],
-        small_out[3],
+        own_part(10, sizes[0]),
+        grad_first[:, front : front + split],
+        own_taps.T,
+        own_part(CONV, sizes[2]),
+        sums[7, :SSM_HEADS],
+        sums[8, :SSM_HEADS],
+        skip_grad,
+        own_part(5, sizes[3]),
         grad_mixer_out,
-        grad_qkv[:, :half_q],
-        grad_qkv[:, half_q : half_q + half_k],
-        grad_qkv[:, half_q + half_k :],
+        grad_first[:, :half_q],
+        grad_first[:, half_q : half_q + half_k],
+        grad_first[:, half_q + half_k : front],
         grad_output,
-        small_out[4],
+        own_part(9, sizes[4]),
         grad_gate_up[:, :half_ff],
         grad_gate_up[:, half_ff:],
         grad_down,
-    )
-
-
-def two_halves(value, which, half):
-    return jnp.concatenate(
-        [
-            value[:, which * half : which * half + half],
-            value[:, (2 + which) * half : (3 + which) * half],
-        ],
-        axis=1,
     )
 
 

time: 701 us -> 498 us (0.71)
  waiting for transfers between devices: 268 us -> 132 us
  other arithmetic: 121 us -> 73.5 us
  local copies, waits for them, and re-layouts: 75.6 us -> 41.4 us
  matrix products: 88 us -> 66.1 us
  starting transfers between devices: 53.6 us -> 70.8 us
  Pallas kernels: 87.1 us -> 103 us
    ppermute x72 -> x64, waiting for transfers between devices: 268 us -> 132 us  [shift(): return lax.ppermute(value, axis, pairs)]
    select_n x15 -> x10, other arithmetic: 53.5 us -> 7.96 us  [in_order(): jnp.where(own == 0, jnp.concatenate(parts, axis=dim), jnp.concatenate(par...]
    ppermute x72 -> x64, starting transfers between devices: 48.8 us -> 66.1 us  [shift(): return lax.ppermute(value, axis, pairs)]
    pallas_call x4 -> x7, Pallas kernels: 87.1 us -> 103 us  [the longest x4 90.6 us: call(): pl.pallas_call(kernel, grid=(1,) if blocks else (), out_shape=[jax.ShapeD...]
    dot_general x6 -> x5, matrix products: 33.9 us -> 23.7 us  [dot_right_t(): lax.dot_general(left, right, (((1,), (1,)), ((), ())), preferred_element_...]
    convert_element_type x1 -> x0, local copies, waits for them, and re-layouts: 10.1 us -> none  [shards_halo(): dot_left_t(normed_low, proj_grad_low).astype(low)]
    convert_element_type x31 -> x30, other arithmetic: 18.6 us -> 28.4 us  [the longest x16 24 us: finish(): self.value = total.astype(self.kind) if self.steps else total]
    slice x16 -> x11, local copies, waits for them, and re-layouts: 14.6 us -> 5.02 us  [the longest x2 1.67 us: shards_halo(): value[..., base_down:]]
  transfers between devices with their start and end apart: 74 -> 66, of which waited for: 43 -> 34; matrix products, arithmetic and copies ran while one was open for 28% -> 24% of each run, Pallas kernels for 4% -> 21%
where the time goes in v2:
time: 498 us; the launch traced here: 489 us
  waiting for transfers between devices  132 us (27%)
  Pallas kernels  103 us (21%)
  other arithmetic  73.5 us (15%)
  starting transfers between devices  70.8 us (14%)
  matrix products  66.1 us (13%)
  local copies, waits for them, and re-layouts  41.4 us (8%)
    ppermute x64, waiting for transfers between devices, shift(): return lax.ppermute(value, axis, pairs)  132 us
    pallas_call x4, Pallas kernels, call(): pl.pallas_call(kernel, grid=(1,) if blocks else (), out_shape=[jax.ShapeD...  90.6 us
    ppermute x64, starting transfers between devices, shift(): return lax.ppermute(value, axis, pairs)  66.1 us
    convert_element_type x16, other arithmetic, finish(): self.value = total.astype(self.kind) if self.steps else total  24 us
    dot_general x5, matrix products, dot_right_t(): lax.dot_general(left, right, (((1,), (1,)), ((), ())), preferred_element_...  23.7 us
    dot_general x5, matrix products, dot_plain(): return jnp.dot(left, right, preferred_element_type=jnp.float32)  22.3 us
    unnamed x163, local copies, waits for them, and re-layouts  20.2 us
    dot_general x5, matrix products, dot_left_t(): lax.dot_general(left, right, (((0,), (0,)), ((), ())), preferred_element_...  20.1 us
  transfers between devices with their start and end apart: 66, of which 34 were waited for; matrix products, arithmetic and copies ran while one was open for 24% of the time, Pallas kernels for 21%

profile of v2, /device:TPU:0, one launch (start us, length us, event | category | flops | bytes accessed | tf_op | source)
XLA Modules:
  0.0 488.9 jit_solution(5417721277481962153)
XLA Ops:
  1.6 2.8 concatenate.282
  5.7 3.1 collective-permute-start.3
  8.7 2.6 collective-permute-start.2
  13.6 3.4 collective-permute-start
  22.9 3.8 collective-permute-done.1
  26.7 2.8 collective-permute-done.2
  34.3 10.0 %collective-permute-done.5 = bf16[1,4,1,1,32,2176]{5,4,3,2,1,0:T(8,128)(2,1)S(1)} collective-permute-done((bf16[1,4,1,1,32,2176]{5,4,3,2,1,0:T(8,128)(2,1)S(1)}, bf16[1,4,1,1,32,2176]{5,4,3,2,1,0:T(8,128)(2,1)S(1)}, u32[]{:S(2)}, u32[]{:S(2)}) %collective-permute-start.5) | collective-permute-done | bytes 557088 | tf_op jit(solution)/shard_map/ppermute | solution.py:666
  46.4 6.6 %collective-permute-start.6 = (bf16[1,1,1,1,64,4096]{5,4,3,2,1,0:T(8,128)(2,1)}, bf16[1,1,1,1,64,4096]{5,4,3,2,1,0:T(8,128)(2,1)}, u32[]{:S(2)}, u32[]{:S(2)}) collective-permute-start(bf16[1,1,1,1,64,4096]{5,4,3,2,1,0:T(8,128)(2,1)} %bitcast.1), channel_id=1, source_target_pairs={{0,8},{2,10},{4,12},{6,14},{8,16},{10,18},{12,20},{14,22},{16,24},... | collective-permute-start | bytes 1572872 | tf_op jit(solution)/shard_map/ppermute | solution.py:666
  56.0 7.6 %collective-permute-done.6 = bf16[1,1,1,1,64,4096]{5,4,3,2,1,0:T(8,128)(2,1)} collective-permute-done((bf16[1,1,1,1,64,4096]{5,4,3,2,1,0:T(8,128)(2,1)}, bf16[1,1,1,1,64,4096]{5,4,3,2,1,0:T(8,128)(2,1)}, u32[]{:S(2)}, u32[]{:S(2)}) %collective-permute-start.6) | collective-permute-done | bytes 524320 | tf_op jit(solution)/shard_map/ppermute | solution.py:666
  63.6 2.5 collective-permute-start.7
  67.1 10.2 %collective-permute-done.7 = bf16[1,1,1,1,64,4096]{5,4,3,2,1,0:T(8,128)(2,1)S(1)} collective-permute-done((bf16[1,1,1,1,64,4096]{5,4,3,2,1,0:T(8,128)(2,1)}, bf16[1,1,1,1,64,4096]{5,4,3,2,1,0:T(8,128)(2,1)S(1)}, u32[]{:S(2)}, u32[]{:S(2)}) %collective-permute-start.7) | collective-permute-done | bytes 524320 | tf_op jit(solution)/shard_map/ppermute | solution.py:666
  80.4 9.5 %collective-permute-done.8 = bf16[1,1,1,1,64,4096]{5,4,3,2,1,0:T(8,128)(2,1)S(1)} collective-permute-done((bf16[1,1,1,1,64,4096]{5,4,3,2,1,0:T(8,128)(2,1)S(1)}, bf16[1,1,1,1,64,4096]{5,4,3,2,1,0:T(8,128)(2,1)S(1)}, u32[]{:S(2)}, u32[]{:S(2)}) %collective-permute-start.8) | collective-permute-done | bytes 524320 | tf_op jit(solution)/shard_map/ppermute | solution.py:666
  96.6 2.5 copy-done
  103.3 11.6 %fusion.5.refs_0_.refs_1_.refs_2_.refs_3_.refs_4_.refs_5_.proj_ref = f32[576,4352]{1,0:T(8,128)} fusion(bf16[1024,4352]{1,0:T(8,128)(2,1)} %bitcast.92, f32[1024]{0:T(1024)S(1)} %reshape.804, f32[576]{0:T(1024)S(1)} %fusion.14, bf16[512,1024]{1,0:T(8,128)(2,1)S(1)} %copy-done.13, bf16[64,1024]{1,0:T(8,128)(2,1)S(1)} %collective-permute-done), kind=kOutput, calls=%fused_computation.96 | convolution fusion | flops 5137956864 | bytes 20125952 | tf_op jit(solution)/shard_map/dot_general | solution.py:159
  114.9 6.6 %collective-permute-done.14 = bf16[1,4,1,1,32,4096]{5,4,3,2,1,0:T(8,128)(2,1)S(1)} collective-permute-done((bf16[1,4,1,1,32,4096]{5,4,3,2,1,0:T(8,128)(2,1)S(1)}, bf16[1,4,1,1,32,4096]{5,4,3,2,1,0:T(8,128)(2,1)S(1)}, u32[]{:S(2)}, u32[]{:S(2)}) %collective-permute-start.14) | collective-permute-done | bytes 1048608 | tf_op jit(solution)/shard_map/ppermute | solution.py:666
  131.5 2.1 fusion.6
  137.6 8.9 %shard_map.340 = (bf16[576,768]{1,0:T(8,128)(2,1)}, bf16[512,512]{1,0:T(8,128)(2,1)}) custom-call(f32[576,4352]{1,0:T(8,128)} %fusion.5.refs_0_.refs_1_.refs_2_.refs_3_.refs_4_.refs_5_.proj_ref, f32[576,4352]{1,0:T(8,128)} %fusion.5.refs_0_.refs_1_.refs_2_.refs_3_.refs_4_.refs_5_.proj_ref, ...), custom_call_target="tpu_custom_call" | custom-call | flops 1000000000 | bytes 60756480 | tf_op jit(solution)/shard_map/pallas_call | solution.py:1361
  146.5 23.2 %shard_map.341 = (bf16[512,1536]{1,0:T(8,128)(2,1)}, f32[512,1536]{1,0:T(8,128)}, bf16[9,128,1536]{2,1,0:T(8,128)(2,1)}) custom-call(f32[576,4352]{1,0:T(8,128)} %fusion.5.refs_0_.refs_1_.refs_2_.refs_3_.refs_4_.refs_5_.proj_ref, f32[5,1792]{1,0:T(8,128)} %maximum_convert_fusion.taps_ref, f32[2,24]{1,0:T(2,128)} %pad_maximum_fusion.10.heads_ref, ...), custom_call_target="tpu_custom_call" | custom-call | flops 1000000000 | bytes 10082304 | tf_op jit(solution)/shard_map/pallas_call | solution.py:1361
  169.7 2.2 maximum_select_fusion.refs_0_
  172.1 3.8 maximum_select_fusion.1.refs_2_
  176.4 2.9 fusion.24
  181.6 4.6 collective-permute-done.17.refs_1_
  186.4 9.7 %shard_map.342 = (bf16[4,2,2,64,4096]{4,3,2,1,0:T(8,128)(2,1)}, bf16[4,2,2,96,1024]{4,3,2,1,0:T(8,128)(2,1)S(1)}, bf16[4,2,2,32,1024]{4,3,2,1,0:T(8,128)(2,1)S(1)}) custom-call(s32[1]{0:T(128)} %bitcast.2.core_ref, bf16[2,4,2,1,32,3072]{5,4,3,2,1,0:T(8,128)(2,1)S(1)} %maximum_select_fusion.refs_0_, ...), custom_call_target="tpu_custom_call" | custom-call | bytes 25165824 | tf_op jit(solution)/shard_map/pallas_call | solution.py:758
  196.9 2.4 copy-done.35
  199.3 2.0 multiply_reduce_fusion.5
  203.8 4.6 fusion.29
  209.6 2.4 convolution_bitcast_fusion
  212.0 3.7 multiply_convert_fusion.4
  215.7 2.4 convolution_convert_fusion.3
  221.1 2.3 pad_maximum_fusion
  225.2 3.1 add_convert_fusion.3
  230.5 4.8 convolution_convert_fusion.1
  235.3 2.2 broadcast_select_fusion.2
  238.0 7.7 %multiply_reduce_fusion.3 = (f32[1024]{0:T(1024)S(1)}, f32[512]{0:T(512)S(1)}, f32[512,1024]{1,0:T(8,128)S(1)}) fusion(f32[512,1024]{1,0:T(8,128)S(1)} %get-tuple-element.244, f32[512]{0:T(512)S(1)} %fusion.16, f32[1024]{0:T(1024)S(1)} %reshape.806, bf16[512,4096]{1,0:T(8,128)(2,1)S(1)} %pad_maximum_fusion, bf16[1024,4096]{1,0:T(8,128)(2,1)} %bitcast.119), kind=kOutput, calls=%fused_computation.39 | convolution fusion | flops 4298111488 | bytes 16789504 | tf_op jit(solution)/shard_map/dot_general | solution.py:163
  250.8 2.4 broadcast_select_fusion.4
  253.5 3.8 add_convert_fusion.4
  262.7 2.9 convolution_convert_fusion.5.grad_ref
  265.5 12.8 %shard_map.344.attention_ref = bf16[576,768]{1,0:T(8,128)(2,1)} custom-call(bf16[576,768]{1,0:T(8,128)(2,1)} %get-tuple-element.172.turned_ref, bf16[512,512]{1,0:T(8,128)(2,1)} %convolution_convert_fusion.5.grad_ref, f32[576,128]{1,0:T(8,128)} %get-tuple-element.276.refs_6_.cos_ref, f32[576,128]{1,0:T(8,128)} %get-tuple-element.275.refs_7_.sin_ref, ...), custom_call_target="tpu_custom_call" | custom-call | flops 1000000000 | bytes 2003456 | tf_op jit(solution)/shard_map/pallas_call | solution.py:1361
  278.4 3.5 fusion.30.grad_ref
  281.9 3.3 collective-permute-done.26
  286.6 3.0 add_convert_fusion.2
  289.7 2.0 add_convert_fusion.9
  291.7 2.1 add_convert_fusion.10
  303.5 3.4 add_convert_fusion.12
  306.8 45.7 %shard_map.345 = (bf16[576,4352]{1,0:T(8,128)(2,1)}, f32[16,1792]{1,0:T(8,128)}) custom-call(f32[576,4352]{1,0:T(8,128)} %fusion.5.refs_0_.refs_1_.refs_2_.refs_3_.refs_4_.refs_5_.proj_ref, f32[512,1536]{1,0:T(8,128)} %get-tuple-element.182.mix_ref, bf16[9,128,1536]{2,1,0:T(8,128)(2,1)} %get-tuple-element.183.states_ref, f32[512,1536]{1,0:T(8,128)} %fusion.30.grad_ref, ...), custom_call_target="tpu_custom_call" | custom-call | flops 1000000000 | bytes 20797440 | tf_op jit(solution)/shard_map/pallas_call | solution.py:1361
  353.5 1.9 add_convert_fusion.8
  360.0 10.3 %convolution_convert_fusion = bf16[1024,4352]{1,0:T(8,128)(2,1)S(1)} fusion(bf16[576,4352]{1,0:T(8,128)(2,1)} %get-tuple-element.202, f32[1024]{0:T(1024)S(1)} %reshape.804, f32[576]{0:T(1024)S(1)} %fusion.14, bf16[512,1024]{1,0:T(8,128)(2,1)S(1)} %copy-done.14, bf16[64,1024]{1,0:T(8,128)(2,1)S(1)} %collective-permute-done), kind=kOutput, calls=%fused_computation | convolution fusion | flops 5142413312 | bytes 15112448 | tf_op jit(solution)/shard_map/dot_general | solution.py:169
  371.0 4.0 collective-permute-start.43
  375.0 2.3 broadcast_select_fusion
  380.0 7.3 %fusion.31 = f32[576,1024]{1,0:T(8,128)S(1)} fusion(bf16[576,4352]{1,0:T(8,128)(2,1)} %get-tuple-element.202, bf16[1024,4352]{1,0:T(8,128)(2,1)S(1)} %bitcast.95), kind=kOutput, calls=%fused_computation.213 | convolution fusion | flops 5133828096 | bytes 16285696 | tf_op jit(solution)/shard_map/dot_general | solution.py:163
  394.6 4.3 collective-permute-start.48
  399.8 2.3 collective-permute-done.51
  410.4 2.0 fusion.2
  414.0 3.1 collective-permute-done.52
  417.1 13.2 %collective-permute-done.46 = bf16[4,1,1,32,4352]{4,3,2,1,0:T(8,128)(2,1)S(1)} collective-permute-done((bf16[4,1,1,32,4352]{4,3,2,1,0:T(8,128)(2,1)S(1)}, bf16[4,1,1,32,4352]{4,3,2,1,0:T(8,128)(2,1)S(1)}, u32[]{:S(2)}, u32[]{:S(2)}) %collective-permute-start.46) | collective-permute-done | bytes 1114144 | tf_op jit(solution)/shard_map/ppermute | solution.py:666
  430.3 2.8 collective-permute-done.45
  437.8 12.5 %collective-permute-done.55 = f32[16,1792]{1,0:T(8,128)S(1)} collective-permute-done((f32[16,1792]{1,0:T(8,128)S(1)}, f32[16,1792]{1,0:T(8,128)S(1)}, u32[]{:S(2)}, u32[]{:S(2)}) %collective-permute-start.55) | collective-permute-done | bytes 114720 | tf_op jit(solution)/shard_map/ppermute | solution.py:666
  452.3 3.3 collective-permute-done.58
  455.6 3.4 collective-permute-done.57
  459.0 3.0 collective-permute-done.56
  462.2 1.9 collective-permute-start.61
  465.8 1.9 collective-permute-start.59
  469.1 6.5 %collective-permute-done.62 = f32[16,1792]{1,0:T(8,128)S(1)} collective-permute-done((f32[16,1792]{1,0:T(8,128)S(1)}, f32[16,1792]{1,0:T(8,128)S(1)}, u32[]{:S(2)}, u32[]{:S(2)}) %collective-permute-start.62) | collective-permute-done | bytes 114720 | tf_op jit(solution)/shard_map/ppermute | solution.py:666
  479.7 5.2 %collective-permute-done.65 = bf16[1,1,1,32,2176]{4,3,2,1,0:T(8,128)(2,1)S(1)} collective-permute-done((bf16[1,1,1,32,2176]{4,3,2,1,0:T(8,128)(2,1)S(1)}, bf16[1,1,1,32,2176]{4,3,2,1,0:T(8,128)(2,1)S(1)}, u32[]{:S(2)}, u32[]{:S(2)}) %collective-permute-start.65) | collective-permute-done | bytes 139296 | tf_op jit(solution)/shard_map/ppermute | solution.py:666
  (412 shorter events, 129.2 us)
Async XLA Ops:
  5.7 23.9 %collective-permute-start.3 = (bf16[1,1,1,1,64,2176]{5,4,3,2,1,0:T(8,128)(2,1)S(1)}, bf16[1,1,1,1,64,2176]{5,4,3,2,1,0:T(8,128)(2,1)S(1)}, u32[]{:S(2)}, u32[]{:S(2)}) collective-permute-start(bf16[1,1,1,1,64,2176]{5,4,3,2,1,0:T(8,128)(2,1)S(1)} %pad_bitcast_fusion), channel_id=1, source_target_pairs={{0,8},{2,10},{4,12},{6,14},{8,16},{10,18},{12,20},{14,22},{16,24},... | collective-permute-start | bytes 835592 | tf_op jit(solution)/shard_map/ppermute | solution.py:666
  8.7 20.8 %collective-permute-start.2 = (bf16[1,1,1,1,64,2176]{5,4,3,2,1,0:T(8,128)(2,1)S(1)}, bf16[1,1,1,1,64,2176]{5,4,3,2,1,0:T(8,128)(2,1)S(1)}, u32[]{:S(2)}, u32[]{:S(2)}) collective-permute-start(bf16[1,1,1,1,64,2176]{5,4,3,2,1,0:T(8,128)(2,1)S(1)} %pad_bitcast_fusion), channel_id=1, source_target_pairs={{0,16},{2,18},{4,20},{6,22},{8,24},{10,26},{12,28},{14,30},{16,0},... | collective-permute-start | bytes 835592 | tf_op jit(solution)/shard_map/ppermute | solution.py:666
  11.3 15.3 %collective-permute-start.1 = (bf16[1,1,1,1,64,2176]{5,4,3,2,1,0:T(8,128)(2,1)S(1)}, bf16[1,1,1,1,64,2176]{5,4,3,2,1,0:T(8,128)(2,1)S(1)}, u32[]{:S(2)}, u32[]{:S(2)}) collective-permute-start(bf16[1,1,1,1,64,2176]{5,4,3,2,1,0:T(8,128)(2,1)S(1)} %pad_bitcast_fusion), channel_id=1, source_target_pairs={{0,24},{2,26},{4,28},{6,30},{8,0},{10,2},{12,4},{14,6},{16,8},{18,... | collective-permute-start | bytes 835592 | tf_op jit(solution)/shard_map/ppermute | solution.py:666
  13.6 39.7 %collective-permute-start = (bf16[64,1024]{1,0:T(8,128)(2,1)S(1)}, bf16[64,1024]{1,0:T(8,128)(2,1)S(1)}, u32[]{:S(2)}, u32[]{:S(2)}) collective-permute-start(bf16[64,1024]{1,0:T(8,128)(2,1)S(1)} %slice.298), channel_id=1, source_target_pairs={{0,1},{2,3},{4,5},{6,7},{8,9},{10,11},{12,13},{14,15},{16,17},{18,... | collective-permute-start | bytes 393224 | tf_op jit(solution)/shard_map/ppermute | solution.py:1484
  29.8 14.5 %collective-permute-start.5 = (bf16[1,4,1,1,32,2176]{5,4,3,2,1,0:T(8,128)(2,1)S(1)}, bf16[1,4,1,1,32,2176]{5,4,3,2,1,0:T(8,128)(2,1)S(1)}, u32[]{:S(2)}, u32[]{:S(2)}) collective-permute-start(bf16[1,4,1,1,32,2176]{5,4,3,2,1,0:T(8,128)(2,1)S(1)} %get-tuple-element.261), channel_id=1, source_target_pairs={{0,1},{1,0},{2,3},{3,2},{4,5},{5,4},{6,7},{7,6},{8,9},{9,8},{10,11... | collective-permute-start | bytes 1671176 | tf_op jit(solution)/shard_map/ppermute | solution.py:666
  32.1 14.2 %collective-permute-start.4 = (bf16[1,4,1,1,32,2176]{5,4,3,2,1,0:T(8,128)(2,1)S(1)}, bf16[1,4,1,1,32,2176]{5,4,3,2,1,0:T(8,128)(2,1)S(1)}, u32[]{:S(2)}, u32[]{:S(2)}) collective-permute-start(bf16[1,4,1,1,32,2176]{5,4,3,2,1,0:T(8,128)(2,1)S(1)} %get-tuple-element.262), channel_id=1, source_target_pairs={{0,4},{2,6},{4,0},{6,2},{8,12},{10,14},{12,8},{14,10},{16,20},{18,... | collective-permute-start | bytes 1671176 | tf_op jit(solution)/shard_map/ppermute | solution.py:666
  46.4 17.1 %collective-permute-start.6 = (bf16[1,1,1,1,64,4096]{5,4,3,2,1,0:T(8,128)(2,1)}, bf16[1,1,1,1,64,4096]{5,4,3,2,1,0:T(8,128)(2,1)}, u32[]{:S(2)}, u32[]{:S(2)}) collective-permute-start(bf16[1,1,1,1,64,4096]{5,4,3,2,1,0:T(8,128)(2,1)} %bitcast.1), channel_id=1, source_target_pairs={{0,8},{2,10},{4,12},{6,14},{8,16},{10,18},{12,20},{14,22},{16,24},... | collective-permute-start | bytes 1572872 | tf_op jit(solution)/shard_map/ppermute | solution.py:666
  53.6 25.1 %collective-permute-start.11 = (bf16[2,4,1,1,32,2176]{5,4,3,2,1,0:T(8,128)(2,1)S(1)}, bf16[2,4,1,1,32,2176]{5,4,3,2,1,0:T(8,128)(2,1)S(1)}, u32[]{:S(2)}, u32[]{:S(2)}) collective-permute-start(bf16[2,4,1,1,32,2176]{5,4,3,2,1,0:T(8,128)(2,1)S(1)} %maximum_select_fusion.7), channel_id=1, source_target_pairs={{0,4},{2,6},{4,0},{6,2},{8,12},{10,14},{12,8},{14,10},{16,20},{18,... | collective-permute-start | bytes 3342344 | tf_op jit(solution)/shard_map/ppermute | solution.py:666
  55.2 24.8 %collective-permute-start.9 = (bf16[1,4,2,1,32,2176]{5,4,3,2,1,0:T(8,128)(2,1)S(1)}, bf16[1,4,2,1,32,2176]{5,4,3,2,1,0:T(8,128)(2,1)S(1)}, u32[]{:S(2)}, u32[]{:S(2)}) collective-permute-start(bf16[1,4,2,1,32,2176]{5,4,3,2,1,0:T(8,128)(2,1)S(1)} %maximum_select_fusion.6), channel_id=1, source_target_pairs={{0,1},{1,0},{2,3},{3,2},{4,5},{5,4},{6,7},{7,6},{8,9},{9,8},{10,11... | collective-permute-start | bytes 3342344 | tf_op jit(solution)/shard_map/ppermute | solution.py:666
  63.6 13.8 %collective-permute-start.7 = (bf16[1,1,1,1,64,4096]{5,4,3,2,1,0:T(8,128)(2,1)}, bf16[1,1,1,1,64,4096]{5,4,3,2,1,0:T(8,128)(2,1)S(1)}, u32[]{:S(2)}, u32[]{:S(2)}) collective-permute-start(bf16[1,1,1,1,64,4096]{5,4,3,2,1,0:T(8,128)(2,1)} %collective-permute-done.6), channel_id=1, source_target_pairs={{0,8},{2,10},{4,12},{6,14},{8,16},{10,18},{12,20},{14,22},{16,24},... | collective-permute-start | bytes 1572872 | tf_op jit(solution)/shard_map/ppermute | solution.py:666
  77.3 12.6 %collective-permute-start.8 = (bf16[1,1,1,1,64,4096]{5,4,3,2,1,0:T(8,128)(2,1)S(1)}, bf16[1,1,1,1,64,4096]{5,4,3,2,1,0:T(8,128)(2,1)S(1)}, u32[]{:S(2)}, u32[]{:S(2)}) collective-permute-start(bf16[1,1,1,1,64,4096]{5,4,3,2,1,0:T(8,128)(2,1)S(1)} %collective-permute-done.7), channel_id=1, source_target_pairs={{0,8},{2,10},{4,12},{6,14},{8,16},{10,18},{12,20},{14,22},{16,24},... | collective-permute-start | bytes 1572872 | tf_op jit(solution)/shard_map/ppermute | solution.py:666
  79.0 14.6 %collective-permute-start.12 = (bf16[2,4,2,1,32,2176]{5,4,3,2,1,0:T(8,128)(2,1)S(1)}, bf16[2,4,2,1,32,2176]{5,4,3,2,1,0:T(8,128)(2,1)S(1)}, u32[]{:S(2)}, u32[]{:S(2)}) collective-permute-start(bf16[2,4,2,1,32,2176]{5,4,3,2,1,0:T(8,128)(2,1)S(1)} %maximum_select_fusion.3.refs_2_), channel_id=1, source_target_pairs={{0,2},{2,0},{4,6},{6,4},{8,10},{10,8},{12,14},{14,12},{16,18},{18,... | collective-permute-start | bytes 6684680 | tf_op jit(solution)/shard_map/ppermute | solution.py:666
  80.4 13.3 %collective-permute-start.10 = (bf16[2,4,2,1,32,2176]{5,4,3,2,1,0:T(8,128)(2,1)S(1)}, bf16[2,4,2,1,32,2176]{5,4,3,2,1,0:T(8,128)(2,1)S(1)}, u32[]{:S(2)}, u32[]{:S(2)}) collective-permute-start(bf16[2,4,2,1,32,2176]{5,4,3,2,1,0:T(8,128)(2,1)S(1)} %maximum_select_fusion.2.refs_0_), channel_id=1, source_target_pairs={{0,2},{2,0},{4,6},{6,4},{8,10},{10,8},{12,14},{14,12},{16,18},{18,... | collective-permute-start | bytes 6684680 | tf_op jit(solution)/shard_map/ppermute | solution.py:666
  100.3 21.2 %collective-permute-start.14 = (bf16[1,4,1,1,32,4096]{5,4,3,2,1,0:T(8,128)(2,1)S(1)}, bf16[1,4,1,1,32,4096]{5,4,3,2,1,0:T(8,128)(2,1)S(1)}, u32[]{:S(2)}, u32[]{:S(2)}) collective-permute-start(bf16[1,4,1,1,32,4096]{5,4,3,2,1,0:T(8,128)(2,1)S(1)} %get-tuple-element.136), channel_id=1, source_target_pairs={{0,1},{1,0},{2,3},{3,2},{4,5},{5,4},{6,7},{7,6},{8,9},{9,8},{10,11... | collective-permute-start | bytes 3145736 | tf_op jit(solution)/shard_map/ppermute | solution.py:666
  101.8 21.3 %collective-permute-start.13 = (bf16[1,4,1,1,32,4096]{5,4,3,2,1,0:T(8,128)(2,1)}, bf16[1,4,1,1,32,4096]{5,4,3,2,1,0:T(8,128)(2,1)S(1)}, u32[]{:S(2)}, u32[]{:S(2)}) collective-permute-start(bf16[1,4,1,1,32,4096]{5,4,3,2,1,0:T(8,128)(2,1)} %get-tuple-element.134), channel_id=1, source_target_pairs={{0,4},{2,6},{4,0},{6,2},{8,12},{10,14},{12,8},{14,10},{16,20},{18,... | collective-permute-start | bytes 3145736 | tf_op jit(solution)/shard_map/ppermute | solution.py:666
  125.8 43.9 %collective-permute-start.15 = (bf16[1,4,2,1,32,3072]{5,4,3,2,1,0:T(8,128)(2,1)S(1)}, bf16[1,4,2,1,32,3072]{5,4,3,2,1,0:T(8,128)(2,1)}, u32[]{:S(2)}, u32[]{:S(2)}) collective-permute-start(bf16[1,4,2,1,32,3072]{5,4,3,2,1,0:T(8,128)(2,1)S(1)} %slice.382), channel_id=1, source_target_pairs={{0,1},{1,0},{2,3},{3,2},{4,5},{5,4},{6,7},{7,6},{8,9},{9,8},{10,11... | collective-permute-start | bytes 4718600 | tf_op jit(solution)/shard_map/ppermute | solution.py:666
  126.2 43.5 %collective-permute-start.16 = (bf16[2,4,1,1,32,3072]{5,4,3,2,1,0:T(8,128)(2,1)S(1)}, bf16[2,4,1,1,32,3072]{5,4,3,2,1,0:T(8,128)(2,1)}, u32[]{:S(2)}, u32[]{:S(2)}) collective-permute-start(bf16[2,4,1,1,32,3072]{5,4,3,2,1,0:T(8,128)(2,1)S(1)} %slice.383), channel_id=1, source_target_pairs={{0,4},{2,6},{4,0},{6,2},{8,12},{10,14},{12,8},{14,10},{16,20},{18,... | collective-permute-start | bytes 4718600 | tf_op jit(solution)/shard_map/ppermute | solution.py:666
  175.9 10.3 %collective-permute-start.17 = (bf16[2,4,2,1,32,3072]{5,4,3,2,1,0:T(8,128)(2,1)S(1)}, bf16[2,4,2,1,32,3072]{5,4,3,2,1,0:T(8,128)(2,1)}, u32[]{:S(2)}, u32[]{:S(2)}) collective-permute-start(bf16[2,4,2,1,32,3072]{5,4,3,2,1,0:T(8,128)(2,1)S(1)} %maximum_select_fusion.refs_0_), channel_id=1, source_target_pairs={{0,2},{2,0},{4,6},{6,4},{8,10},{10,8},{12,14},{14,12},{16,18},{18,... | collective-permute-start | bytes 9437192 | tf_op jit(solution)/shard_map/ppermute | solution.py:666
  175.9 10.5 %collective-permute-start.18 = (bf16[2,4,2,1,32,3072]{5,4,3,2,1,0:T(8,128)(2,1)}, bf16[2,4,2,1,32,3072]{5,4,3,2,1,0:T(8,128)(2,1)}, u32[]{:S(2)}, u32[]{:S(2)}) collective-permute-start(bf16[2,4,2,1,32,3072]{5,4,3,2,1,0:T(8,128)(2,1)} %maximum_select_fusion.1.refs_2_), channel_id=1, source_target_pairs={{0,2},{2,0},{4,6},{6,4},{8,10},{10,8},{12,14},{14,12},{16,18},{18,... | collective-permute-start | bytes 9437192 | tf_op jit(solution)/shard_map/ppermute | solution.py:666
  179.5 22.2 %collective-permute-start.19 = (bf16[1,4,2,1,32,1024]{5,4,3,2,1,0:T(8,128)(2,1)}, bf16[1,4,2,1,32,1024]{5,4,3,2,1,0:T(8,128)(2,1)S(1)}, u32[]{:S(2)}, u32[]{:S(2)}) collective-permute-start(bf16[1,4,2,1,32,1024]{5,4,3,2,1,0:T(8,128)(2,1)} %slice.384), channel_id=1, source_target_pairs={{0,1},{1,0},{2,3},{3,2},{4,5},{5,4},{6,7},{7,6},{8,9},{9,8},{10,11... | collective-permute-start | bytes 1572872 | tf_op jit(solution)/shard_map/ppermute | solution.py:666
  181.1 20.6 %collective-permute-start.20 = (bf16[2,4,1,1,32,1024]{5,4,3,2,1,0:T(8,128)(2,1)}, bf16[2,4,1,1,32,1024]{5,4,3,2,1,0:T(8,128)(2,1)S(1)}, u32[]{:S(2)}, u32[]{:S(2)}) collective-permute-start(bf16[2,4,1,1,32,1024]{5,4,3,2,1,0:T(8,128)(2,1)} %slice.385), channel_id=1, source_target_pairs={{0,4},{2,6},{4,0},{6,2},{8,12},{10,14},{12,8},{14,10},{16,20},{18,... | collective-permute-start | bytes 1572872 | tf_op jit(solution)/shard_map/ppermute | solution.py:666
  202.9 5.4 %collective-permute-start.22 = (bf16[2,4,2,1,32,1024]{5,4,3,2,1,0:T(8,128)(2,1)S(1)}, bf16[2,4,2,1,32,1024]{5,4,3,2,1,0:T(8,128)(2,1)S(1)}, u32[]{:S(2)}, u32[]{:S(2)}) collective-permute-start(bf16[2,4,2,1,32,1024]{5,4,3,2,1,0:T(8,128)(2,1)S(1)} %maximum_select_fusion.9.refs_2_), channel_id=1, source_target_pairs={{0,2},{2,0},{4,6},{6,4},{8,10},{10,8},{12,14},{14,12},{16,18},{18,... | collective-permute-start | bytes 3145736 | tf_op jit(solution)/shard_map/ppermute | solution.py:666
  230.0 51.9 %collective-permute-start.28 = (bf16[4,1,1,128,1024]{4,3,2,1,0:T(8,128)(2,1)}, bf16[4,1,1,128,1024]{4,3,2,1,0:T(8,128)(2,1)}, u32[]{:S(2)}, u32[]{:S(2)}) collective-permute-start(bf16[4,1,1,128,1024]{4,3,2,1,0:T(8,128)(2,1)} %broadcast_select_fusion.9), channel_id=1, source_target_pairs={{0,4},{2,6},{4,0},{6,2},{8,12},{10,14},{12,8},{14,10},{16,20},{18,... | collective-permute-start | bytes 3145736 | tf_op jit(solution)/shard_map/ppermute | solution.py:666
  237.5 9.6 %collective-permute-start.25 = (bf16[4,2,1,32,4096]{4,3,2,1,0:T(8,128)(2,1)}, bf16[4,2,1,32,4096]{4,3,2,1,0:T(8,128)(2,1)}, u32[]{:S(2)}, u32[]{:S(2)}) collective-permute-start(bf16[4,2,1,32,4096]{4,3,2,1,0:T(8,128)(2,1)} %get-tuple-element.257), channel_id=1, source_target_pairs={{0,2},{2,0},{4,6},{6,4},{8,10},{10,8},{12,14},{14,12},{16,18},{18,... | collective-permute-start | bytes 6291464 | tf_op jit(solution)/shard_map/ppermute | solution.py:666
  237.7 9.4 %collective-permute-start.24 = (bf16[4,2,1,32,4096]{4,3,2,1,0:T(8,128)(2,1)}, bf16[4,2,1,32,4096]{4,3,2,1,0:T(8,128)(2,1)}, u32[]{:S(2)}, u32[]{:S(2)}) collective-permute-start(bf16[4,2,1,32,4096]{4,3,2,1,0:T(8,128)(2,1)} %get-tuple-element.258), channel_id=1, source_target_pairs={{0,2},{2,0},{4,6},{6,4},{8,10},{10,8},{12,14},{14,12},{16,18},{18,... | collective-permute-start | bytes 6291464 | tf_op jit(solution)/shard_map/ppermute | solution.py:666
  253.2 33.4 %collective-permute-start.29 = (bf16[4,2,1,128,1024]{4,3,2,1,0:T(8,128)(2,1)}, bf16[4,2,1,128,1024]{4,3,2,1,0:T(8,128)(2,1)}, u32[]{:S(2)}, u32[]{:S(2)}) collective-permute-start(bf16[4,2,1,128,1024]{4,3,2,1,0:T(8,128)(2,1)} %broadcast_select_fusion.4), channel_id=1, source_target_pairs={{0,2},{2,0},{4,6},{6,4},{8,10},{10,8},{12,14},{14,12},{16,18},{18,... | collective-permute-start | bytes 6291464 | tf_op jit(solution)/shard_map/ppermute | solution.py:666
  259.6 25.6 %collective-permute-start.26 = (bf16[4,2,1,32,2048]{4,3,2,1,0:T(8,128)(2,1)}, bf16[4,2,1,32,2048]{4,3,2,1,0:T(8,128)(2,1)}, u32[]{:S(2)}, u32[]{:S(2)}) collective-permute-start(bf16[4,2,1,32,2048]{4,3,2,1,0:T(8,128)(2,1)} %broadcast_select_fusion.11), channel_id=1, source_target_pairs={{0,1},{1,0},{2,3},{3,2},{4,5},{5,4},{6,7},{7,6},{8,9},{9,8},{10,11... | collective-permute-start | bytes 3145736 | tf_op jit(solution)/shard_map/ppermute | solution.py:666
  261.3 25.3 %collective-permute-start.27 = (bf16[4,1,1,32,4096]{4,3,2,1,0:T(8,128)(2,1)}, bf16[4,1,1,32,4096]{4,3,2,1,0:T(8,128)(2,1)}, u32[]{:S(2)}, u32[]{:S(2)}) collective-permute-start(bf16[4,1,1,32,4096]{4,3,2,1,0:T(8,128)(2,1)} %broadcast_select_fusion.10), channel_id=1, source_target_pairs={{0,4},{2,6},{4,0},{6,2},{8,12},{10,14},{12,8},{14,10},{16,20},{18,... | collective-permute-start | bytes 3145736 | tf_op jit(solution)/shard_map/ppermute | solution.py:666
  297.4 55.1 %collective-permute-start.32 = (bf16[4,1,1,128,512]{4,3,2,1,0:T(8,128)(2,1)}, bf16[4,1,1,128,512]{4,3,2,1,0:T(8,128)(2,1)}, u32[]{:S(2)}, u32[]{:S(2)}) collective-permute-start(bf16[4,1,1,128,512]{4,3,2,1,0:T(8,128)(2,1)} %broadcast_select_fusion.15), channel_id=1, source_target_pairs={{0,1},{1,0},{2,3},{3,2},{4,5},{5,4},{6,7},{7,6},{8,9},{9,8},{10,11... | collective-permute-start | bytes 1572872 | tf_op jit(solution)/shard_map/ppermute | solution.py:666
  297.8 54.7 %collective-permute-start.31 = (bf16[4,1,1,32,2048]{4,3,2,1,0:T(8,128)(2,1)}, bf16[4,1,1,32,2048]{4,3,2,1,0:T(8,128)(2,1)S(1)}, u32[]{:S(2)}, u32[]{:S(2)}) collective-permute-start(bf16[4,1,1,32,2048]{4,3,2,1,0:T(8,128)(2,1)} %broadcast_select_fusion.16), channel_id=1, source_target_pairs={{0,1},{1,0},{2,3},{3,2},{4,5},{5,4},{6,7},{7,6},{8,9},{9,8},{10,11... | collective-permute-start | bytes 1572872 | tf_op jit(solution)/shard_map/ppermute | solution.py:666
  300.6 52.0 %collective-permute-start.33 = (bf16[4,1,1,128,1024]{4,3,2,1,0:T(8,128)(2,1)}, bf16[4,1,1,128,1024]{4,3,2,1,0:T(8,128)(2,1)S(1)}, u32[]{:S(2)}, u32[]{:S(2)}) collective-permute-start(bf16[4,1,1,128,1024]{4,3,2,1,0:T(8,128)(2,1)} %broadcast_select_fusion.8), channel_id=1, source_target_pairs={{0,4},{2,6},{4,0},{6,2},{8,12},{10,14},{12,8},{14,10},{16,20},{18,... | collective-permute-start | bytes 3145736 | tf_op jit(solution)/shard_map/ppermute | solution.py:666
  302.9 49.6 %collective-permute-start.30 = (bf16[4,1,1,32,2048]{4,3,2,1,0:T(8,128)(2,1)}, bf16[4,1,1,32,2048]{4,3,2,1,0:T(8,128)(2,1)}, u32[]{:S(2)}, u32[]{:S(2)}) collective-permute-start(bf16[4,1,1,32,2048]{4,3,2,1,0:T(8,128)(2,1)} %broadcast_select_fusion.17), channel_id=1, source_target_pairs={{0,4},{2,6},{4,0},{6,2},{8,12},{10,14},{12,8},{14,10},{16,20},{18,... | collective-permute-start | bytes 1572872 | tf_op jit(solution)/shard_map/ppermute | solution.py:666
  358.6 11.7 %collective-permute-start.36 = (bf16[1,1,1,128,512]{4,3,2,1,0:T(8,128)(2,1)S(1)}, bf16[1,1,1,128,512]{4,3,2,1,0:T(8,128)(2,1)S(1)}, u32[]{:S(2)}, u32[]{:S(2)}) collective-permute-start(bf16[1,1,1,128,512]{4,3,2,1,0:T(8,128)(2,1)S(1)} %constant_dynamic-slice_fusion.5), channel_id=1, source_target_pairs={{0,8},{2,10},{4,12},{6,14},{8,16},{10,18},{12,20},{14,22},{16,24},... | collective-permute-start | bytes 393224 | tf_op jit(solution)/shard_map/ppermute | solution.py:666
  358.7 11.6 %collective-permute-start.35 = (bf16[1,1,1,32,2048]{4,3,2,1,0:T(8,128)(2,1)S(1)}, bf16[1,1,1,32,2048]{4,3,2,1,0:T(8,128)(2,1)S(1)}, u32[]{:S(2)}, u32[]{:S(2)}) collective-permute-start(bf16[1,1,1,32,2048]{4,3,2,1,0:T(8,128)(2,1)S(1)} %constant_dynamic-slice_fusion.6), channel_id=1, source_target_pairs={{0,8},{2,10},{4,12},{6,14},{8,16},{10,18},{12,20},{14,22},{16,24},... | collective-permute-start | bytes 393224 | tf_op jit(solution)/shard_map/ppermute | solution.py:666
  358.8 11.6 %collective-permute-start.34 = (bf16[1,1,1,32,2048]{4,3,2,1,0:T(8,128)(2,1)S(1)}, bf16[1,1,1,32,2048]{4,3,2,1,0:T(8,128)(2,1)S(1)}, u32[]{:S(2)}, u32[]{:S(2)}) collective-permute-start(bf16[1,1,1,32,2048]{4,3,2,1,0:T(8,128)(2,1)S(1)} %constant_dynamic-slice_fusion.7), channel_id=1, source_target_pairs={{0,8},{2,10},{4,12},{6,14},{8,16},{10,18},{12,20},{14,22},{16,24},... | collective-permute-start | bytes 393224 | tf_op jit(solution)/shard_map/ppermute | solution.py:666
  359.6 11.2 %collective-permute-start.37 = (bf16[4,1,1,128,512]{4,3,2,1,0:T(8,128)(2,1)S(1)}, bf16[4,1,1,128,512]{4,3,2,1,0:T(8,128)(2,1)S(1)}, u32[]{:S(2)}, u32[]{:S(2)}) collective-permute-start(bf16[4,1,1,128,512]{4,3,2,1,0:T(8,128)(2,1)S(1)} %broadcast_select_fusion.14), channel_id=1, source_target_pairs={{0,1},{1,0},{2,3},{3,2},{4,5},{5,4},{6,7},{7,6},{8,9},{9,8},{10,11... | collective-permute-start | bytes 1572872 | tf_op jit(solution)/shard_map/ppermute | solution.py:666
  371.0 7.7 %collective-permute-start.43 = (bf16[1,1,1,128,512]{4,3,2,1,0:T(8,128)(2,1)S(1)}, bf16[1,1,1,128,512]{4,3,2,1,0:T(8,128)(2,1)S(1)}, u32[]{:S(2)}, u32[]{:S(2)}) collective-permute-start(bf16[1,1,1,128,512]{4,3,2,1,0:T(8,128)(2,1)S(1)} %constant_dynamic-slice_fusion.4), channel_id=1, source_target_pairs={{0,8},{2,10},{4,12},{6,14},{8,16},{10,18},{12,20},{14,22},{16,24},... | collective-permute-start | bytes 393224 | tf_op jit(solution)/shard_map/ppermute | solution.py:666
  377.3 13.5 %collective-permute-start.39 = (bf16[4,2,1,32,4352]{4,3,2,1,0:T(8,128)(2,1)}, bf16[4,2,1,32,4352]{4,3,2,1,0:T(8,128)(2,1)S(1)}, u32[]{:S(2)}, u32[]{:S(2)}) collective-permute-start(bf16[4,2,1,32,4352]{4,3,2,1,0:T(8,128)(2,1)} %get-tuple-element.251), channel_id=1, source_target_pairs={{0,2},{2,0},{4,6},{6,4},{8,10},{10,8},{12,14},{14,12},{16,18},{18,... | collective-permute-start | bytes 6684680 | tf_op jit(solution)/shard_map/ppermute | solution.py:666
  377.3 13.5 %collective-permute-start.38 = (bf16[4,2,1,32,4352]{4,3,2,1,0:T(8,128)(2,1)}, bf16[4,2,1,32,4352]{4,3,2,1,0:T(8,128)(2,1)S(1)}, u32[]{:S(2)}, u32[]{:S(2)}) collective-permute-start(bf16[4,2,1,32,4352]{4,3,2,1,0:T(8,128)(2,1)} %get-tuple-element.252), channel_id=1, source_target_pairs={{0,2},{2,0},{4,6},{6,4},{8,10},{10,8},{12,14},{14,12},{16,18},{18,... | collective-permute-start | bytes 6684680 | tf_op jit(solution)/shard_map/ppermute | solution.py:666
  378.0 9.4 %collective-permute-start.42 = (bf16[1,1,1,128,512]{4,3,2,1,0:T(8,128)(2,1)S(1)}, bf16[1,1,1,128,512]{4,3,2,1,0:T(8,128)(2,1)S(1)}, u32[]{:S(2)}, u32[]{:S(2)}) collective-permute-start(bf16[1,1,1,128,512]{4,3,2,1,0:T(8,128)(2,1)S(1)} %add_convert_fusion.28), channel_id=1, source_target_pairs={{0,8},{2,10},{4,12},{6,14},{8,16},{10,18},{12,20},{14,22},{16,24},... | collective-permute-start | bytes 393224 | tf_op jit(solution)/shard_map/ppermute | solution.py:666
  378.4 10.6 %collective-permute-start.41 = (bf16[1,1,1,32,2048]{4,3,2,1,0:T(8,128)(2,1)S(1)}, bf16[1,1,1,32,2048]{4,3,2,1,0:T(8,128)(2,1)S(1)}, u32[]{:S(2)}, u32[]{:S(2)}) collective-permute-start(bf16[1,1,1,32,2048]{4,3,2,1,0:T(8,128)(2,1)S(1)} %add_convert_fusion.29), channel_id=1, source_target_pairs={{0,8},{2,10},{4,12},{6,14},{8,16},{10,18},{12,20},{14,22},{16,24},... | collective-permute-start | bytes 393224 | tf_op jit(solution)/shard_map/ppermute | solution.py:666
  378.7 12.1 %collective-permute-start.40 = (bf16[1,1,1,32,2048]{4,3,2,1,0:T(8,128)(2,1)S(1)}, bf16[1,1,1,32,2048]{4,3,2,1,0:T(8,128)(2,1)S(1)}, u32[]{:S(2)}, u32[]{:S(2)}) collective-permute-start(bf16[1,1,1,32,2048]{4,3,2,1,0:T(8,128)(2,1)S(1)} %add_convert_fusion.30), channel_id=1, source_target_pairs={{0,8},{2,10},{4,12},{6,14},{8,16},{10,18},{12,20},{14,22},{16,24},... | collective-permute-start | bytes 393224 | tf_op jit(solution)/shard_map/ppermute | solution.py:666
  393.5 20.5 %collective-permute-start.47 = (f32[16,1792]{1,0:T(8,128)S(1)}, f32[16,1792]{1,0:T(8,128)S(1)}, u32[]{:S(2)}, u32[]{:S(2)}) collective-permute-start(f32[16,1792]{1,0:T(8,128)S(1)} %fusion.8), channel_id=1, source_target_pairs={{0,2},{2,0},{4,6},{6,4},{8,10},{10,8},{12,14},{14,12},{16,18},{18,... | collective-permute-start | bytes 344072 | tf_op jit(solution)/shard_map/ppermute | solution.py:666
  393.9 8.2 %collective-permute-start.51 = (bf16[1,1,1,128,512]{4,3,2,1,0:T(8,128)(2,1)S(1)}, bf16[1,1,1,128,512]{4,3,2,1,0:T(8,128)(2,1)S(1)}, u32[]{:S(2)}, u32[]{:S(2)}) collective-permute-start(bf16[1,1,1,128,512]{4,3,2,1,0:T(8,128)(2,1)S(1)} %add_convert_fusion.24), channel_id=1, source_target_pairs={{0,8},{2,10},{4,12},{6,14},{8,16},{10,18},{12,20},{14,22},{16,24},... | collective-permute-start | bytes 393224 | tf_op jit(solution)/shard_map/ppermute | solution.py:666
  394.0 10.9 %collective-permute-start.49 = (bf16[1,1,1,32,2048]{4,3,2,1,0:T(8,128)(2,1)S(1)}, bf16[1,1,1,32,2048]{4,3,2,1,0:T(8,128)(2,1)S(1)}, u32[]{:S(2)}, u32[]{:S(2)}) collective-permute-start(bf16[1,1,1,32,2048]{4,3,2,1,0:T(8,128)(2,1)S(1)} %add_convert_fusion.26), channel_id=1, source_target_pairs={{0,8},{2,10},{4,12},{6,14},{8,16},{10,18},{12,20},{14,22},{16,24},... | collective-permute-start | bytes 393224 | tf_op jit(solution)/shard_map/ppermute | solution.py:666
  394.1 13.7 %collective-permute-start.50 = (bf16[1,1,1,128,512]{4,3,2,1,0:T(8,128)(2,1)S(1)}, bf16[1,1,1,128,512]{4,3,2,1,0:T(8,128)(2,1)S(1)}, u32[]{:S(2)}, u32[]{:S(2)}) collective-permute-start(bf16[1,1,1,128,512]{4,3,2,1,0:T(8,128)(2,1)S(1)} %add_convert_fusion.25), channel_id=1, source_target_pairs={{0,8},{2,10},{4,12},{6,14},{8,16},{10,18},{12,20},{14,22},{16,24},... | collective-permute-start | bytes 393224 | tf_op jit(solution)/shard_map/ppermute | solution.py:666
  394.6 15.3 %collective-permute-start.48 = (bf16[1,1,1,32,2048]{4,3,2,1,0:T(8,128)(2,1)S(1)}, bf16[1,1,1,32,2048]{4,3,2,1,0:T(8,128)(2,1)S(1)}, u32[]{:S(2)}, u32[]{:S(2)}) collective-permute-start(bf16[1,1,1,32,2048]{4,3,2,1,0:T(8,128)(2,1)S(1)} %add_convert_fusion.27), channel_id=1, source_target_pairs={{0,8},{2,10},{4,12},{6,14},{8,16},{10,18},{12,20},{14,22},{16,24},... | collective-permute-start | bytes 393224 | tf_op jit(solution)/shard_map/ppermute | solution.py:666
  402.1 8.2 %collective-permute-start.44 = (bf16[64,1024]{1,0:T(8,128)(2,1)S(1)}, bf16[64,1024]{1,0:T(8,128)(2,1)S(1)}, u32[]{:S(2)}, u32[]{:S(2)}) collective-permute-start(bf16[64,1024]{1,0:T(8,128)(2,1)S(1)} %slice.567), channel_id=1, source_target_pairs={{1,0},{3,2},{5,4},{7,6},{9,8},{11,10},{13,12},{15,14},{17,16},{19,... | collective-permute-start | bytes 393224 | tf_op jit(solution)/shard_map/ppermute | solution.py:1697
  404.9 25.3 %collective-permute-start.46 = (bf16[4,1,1,32,4352]{4,3,2,1,0:T(8,128)(2,1)S(1)}, bf16[4,1,1,32,4352]{4,3,2,1,0:T(8,128)(2,1)S(1)}, u32[]{:S(2)}, u32[]{:S(2)}) collective-permute-start(bf16[4,1,1,32,4352]{4,3,2,1,0:T(8,128)(2,1)S(1)} %broadcast_select_fusion.6), channel_id=1, source_target_pairs={{0,4},{2,6},{4,0},{6,2},{8,12},{10,14},{12,8},{14,10},{16,20},{18,... | collective-permute-start | bytes 3342344 | tf_op jit(solution)/shard_map/ppermute | solution.py:666
  407.7 25.3 %collective-permute-start.45 = (bf16[4,2,1,32,2176]{4,3,2,1,0:T(8,128)(2,1)S(1)}, bf16[4,2,1,32,2176]{4,3,2,1,0:T(8,128)(2,1)S(1)}, u32[]{:S(2)}, u32[]{:S(2)}) collective-permute-start(bf16[4,2,1,32,2176]{4,3,2,1,0:T(8,128)(2,1)S(1)} %broadcast_select_fusion.7), channel_id=1, source_target_pairs={{0,1},{1,0},{2,3},{3,2},{4,5},{5,4},{6,7},{7,6},{8,9},{9,8},{10,11... | collective-permute-start | bytes 3342344 | tf_op jit(solution)/shard_map/ppermute | solution.py:666
  410.0 7.0 %collective-permute-start.52 = (bf16[1,1,1,128,512]{4,3,2,1,0:T(8,128)(2,1)S(1)}, bf16[1,1,1,128,512]{4,3,2,1,0:T(8,128)(2,1)S(1)}, u32[]{:S(2)}, u32[]{:S(2)}) collective-permute-start(bf16[1,1,1,128,512]{4,3,2,1,0:T(8,128)(2,1)S(1)} %add_convert_fusion.23), channel_id=1, source_target_pairs={{0,8},{2,10},{4,12},{6,14},{8,16},{10,18},{12,20},{14,22},{16,24},... | collective-permute-start | bytes 393224 | tf_op jit(solution)/shard_map/ppermute | solution.py:666
  434.1 16.2 %collective-permute-start.54 = (bf16[4,1,1,32,2176]{4,3,2,1,0:T(8,128)(2,1)S(1)}, bf16[4,1,1,32,2176]{4,3,2,1,0:T(8,128)(2,1)S(1)}, u32[]{:S(2)}, u32[]{:S(2)}) collective-permute-start(bf16[4,1,1,32,2176]{4,3,2,1,0:T(8,128)(2,1)S(1)} %broadcast_select_fusion.12), channel_id=1, source_target_pairs={{0,1},{1,0},{2,3},{3,2},{4,5},{5,4},{6,7},{7,6},{8,9},{9,8},{10,11... | collective-permute-start | bytes 1671176 | tf_op jit(solution)/shard_map/ppermute | solution.py:666
  435.6 14.7 %collective-permute-start.53 = (bf16[4,1,1,32,2176]{4,3,2,1,0:T(8,128)(2,1)S(1)}, bf16[4,1,1,32,2176]{4,3,2,1,0:T(8,128)(2,1)S(1)}, u32[]{:S(2)}, u32[]{:S(2)}) collective-permute-start(bf16[4,1,1,32,2176]{4,3,2,1,0:T(8,128)(2,1)S(1)} %broadcast_select_fusion.13), channel_id=1, source_target_pairs={{0,4},{2,6},{4,0},{6,2},{8,12},{10,14},{12,8},{14,10},{16,20},{18,... | collective-permute-start | bytes 1671176 | tf_op jit(solution)/shard_map/ppermute | solution.py:666
  437.1 13.1 %collective-permute-start.55 = (f32[16,1792]{1,0:T(8,128)S(1)}, f32[16,1792]{1,0:T(8,128)S(1)}, u32[]{:S(2)}, u32[]{:S(2)}) collective-permute-start(f32[16,1792]{1,0:T(8,128)S(1)} %fusion.58), channel_id=1, source_target_pairs={{0,4},{2,6},{4,0},{6,2},{8,12},{10,14},{12,8},{14,10},{16,20},{18,... | collective-permute-start | bytes 344072 | tf_op jit(solution)/shard_map/ppermute | solution.py:666
  450.8 4.9 collective-permute-start.58
  451.4 7.6 %collective-permute-start.57 = (bf16[1,1,1,32,2176]{4,3,2,1,0:T(8,128)(2,1)S(1)}, bf16[1,1,1,32,2176]{4,3,2,1,0:T(8,128)(2,1)S(1)}, u32[]{:S(2)}, u32[]{:S(2)}) collective-permute-start(bf16[1,1,1,32,2176]{4,3,2,1,0:T(8,128)(2,1)S(1)} %constant_dynamic-slice_fusion.2), channel_id=1, source_target_pairs={{0,8},{2,10},{4,12},{6,14},{8,16},{10,18},{12,20},{14,22},{16,24},... | collective-permute-start | bytes 417800 | tf_op jit(solution)/shard_map/ppermute | solution.py:666
  451.5 10.5 %collective-permute-start.56 = (bf16[1,1,1,32,2176]{4,3,2,1,0:T(8,128)(2,1)S(1)}, bf16[1,1,1,32,2176]{4,3,2,1,0:T(8,128)(2,1)S(1)}, u32[]{:S(2)}, u32[]{:S(2)}) collective-permute-start(bf16[1,1,1,32,2176]{4,3,2,1,0:T(8,128)(2,1)S(1)} %constant_dynamic-slice_fusion.3), channel_id=1, source_target_pairs={{0,8},{2,10},{4,12},{6,14},{8,16},{10,18},{12,20},{14,22},{16,24},... | collective-permute-start | bytes 417800 | tf_op jit(solution)/shard_map/ppermute | solution.py:666
  462.0 7.1 %collective-permute-start.63 = (f32[16,1792]{1,0:T(8,128)S(1)}, f32[16,1792]{1,0:T(8,128)S(1)}, u32[]{:S(2)}, u32[]{:S(2)}) collective-permute-start(f32[16,1792]{1,0:T(8,128)S(1)} %add.560), channel_id=1, source_target_pairs={{0,24},{2,26},{4,28},{6,30},{8,0},{10,2},{12,4},{14,6},{16,8},{18,... | collective-permute-start | bytes 344072 | tf_op jit(solution)/shard_map/ppermute | solution.py:666
  462.1 13.5 %collective-permute-start.62 = (f32[16,1792]{1,0:T(8,128)S(1)}, f32[16,1792]{1,0:T(8,128)S(1)}, u32[]{:S(2)}, u32[]{:S(2)}) collective-permute-start(f32[16,1792]{1,0:T(8,128)S(1)} %add.560), channel_id=1, source_target_pairs={{0,16},{2,18},{4,20},{6,22},{8,24},{10,26},{12,28},{14,30},{16,0},... | collective-permute-start | bytes 344072 | tf_op jit(solution)/shard_map/ppermute | solution.py:666
  462.2 13.4 %collective-permute-start.61 = (f32[16,1792]{1,0:T(8,128)S(1)}, f32[16,1792]{1,0:T(8,128)S(1)}, u32[]{:S(2)}, u32[]{:S(2)}) collective-permute-start(f32[16,1792]{1,0:T(8,128)S(1)} %add.560), channel_id=1, source_target_pairs={{0,8},{2,10},{4,12},{6,14},{8,16},{10,18},{12,20},{14,22},{16,24},... | collective-permute-start | bytes 344072 | tf_op jit(solution)/shard_map/ppermute | solution.py:666
  464.2 11.4 %collective-permute-start.60 = (bf16[1,1,1,32,2176]{4,3,2,1,0:T(8,128)(2,1)S(1)}, bf16[1,1,1,32,2176]{4,3,2,1,0:T(8,128)(2,1)S(1)}, u32[]{:S(2)}, u32[]{:S(2)}) collective-permute-start(bf16[1,1,1,32,2176]{4,3,2,1,0:T(8,128)(2,1)S(1)} %add_convert_fusion.21), channel_id=1, source_target_pairs={{0,8},{2,10},{4,12},{6,14},{8,16},{10,18},{12,20},{14,22},{16,24},... | collective-permute-start | bytes 417800 | tf_op jit(solution)/shard_map/ppermute | solution.py:666
  465.8 9.8 %collective-permute-start.59 = (bf16[1,1,1,32,2176]{4,3,2,1,0:T(8,128)(2,1)S(1)}, bf16[1,1,1,32,2176]{4,3,2,1,0:T(8,128)(2,1)S(1)}, u32[]{:S(2)}, u32[]{:S(2)}) collective-permute-start(bf16[1,1,1,32,2176]{4,3,2,1,0:T(8,128)(2,1)S(1)} %add_convert_fusion.22), channel_id=1, source_target_pairs={{0,8},{2,10},{4,12},{6,14},{8,16},{10,18},{12,20},{14,22},{16,24},... | collective-permute-start | bytes 417800 | tf_op jit(solution)/shard_map/ppermute | solution.py:666
  477.5 7.5 %collective-permute-start.65 = (bf16[1,1,1,32,2176]{4,3,2,1,0:T(8,128)(2,1)S(1)}, bf16[1,1,1,32,2176]{4,3,2,1,0:T(8,128)(2,1)S(1)}, u32[]{:S(2)}, u32[]{:S(2)}) collective-permute-start(bf16[1,1,1,32,2176]{4,3,2,1,0:T(8,128)(2,1)S(1)} %add_convert_fusion.19), channel_id=1, source_target_pairs={{0,8},{2,10},{4,12},{6,14},{8,16},{10,18},{12,20},{14,22},{16,24},... | collective-permute-start | bytes 417800 | tf_op jit(solution)/shard_map/ppermute | solution.py:666
  477.5 8.9 %collective-permute-start.64 = (bf16[1,1,1,32,2176]{4,3,2,1,0:T(8,128)(2,1)S(1)}, bf16[1,1,1,32,2176]{4,3,2,1,0:T(8,128)(2,1)S(1)}, u32[]{:S(2)}, u32[]{:S(2)}) collective-permute-start(bf16[1,1,1,32,2176]{4,3,2,1,0:T(8,128)(2,1)S(1)} %add_convert_fusion.20), channel_id=1, source_target_pairs={{0,8},{2,10},{4,12},{6,14},{8,16},{10,18},{12,20},{14,22},{16,24},... | collective-permute-start | bytes 417800 | tf_op jit(solution)/shard_map/ppermute | solution.py:666
  (74 other events, 598.5 us)

commit v3 on v2

--- a/solution.py
+++ b/solution.py
@@ -834,9 +834,9 @@
         core, row, far = dp_factors()
         self.steps = [
             ("dp", 1, core),
+            ("dp", core * row, far),
             ("dp", core, row),
             ("seq", 1, lax.axis_size("seq")),
-            ("dp", core * row, far),
         ]
         self.value = value
 
@@ -1684,15 +1684,15 @@
     grad_first = weight_grad(normed_low, proj_grad)
     grad_first, proj_grad = meet(others, grad_first, proj_grad)
     first = half_sums(grad_first)
-    start_all([*first, *others])
+    start_all(first)
     normed_grad = row_major(dot_right_t(proj_grad, weights_one))
     normed_grad, small_sums, hidden_gain_grad = meet(
-        [*first, *others], normed_grad, small_sums, hidden_gain_grad
+        first, normed_grad, small_sums, hidden_gain_grad
     )
     normed_grad, small_sums, hidden_gain_grad = settle(
         first, normed_grad, small_sums, hidden_gain_grad
     )
-    start_all([*first, *others])
+    start_all(first)
     input_part, input_gain_grad = norm_pull(normed_grad)
     returned = lax.ppermute(input_part[:halo].astype(low), "seq", [(1, 0)]).astype(jnp.float32)
     token_grad = hidden_grad + input_part[halo:]
@@ -1700,20 +1700,22 @@
 
     gain_rows = jnp.stack([hidden_gain_grad, input_gain_grad])
     small = Total(small_sums + jnp.pad(gain_rows, ((9, 5), (0, CHANNELS - width))))
-    meet(others)
-    start_all([outs])
     small.start()
-    meet([*first, small, outs])
-    first.append(small)
-    start_all(first)
-    meet(first)
-    start_all(first)
-    meet(first)
-    start_all(first)
-    meet(first)
-    first.pop()
-    start_all(first)
-    meet(first)
+    meet([small])
+    rings = others[:3]
+    moving, outs.value, small.value = join(
+        [chain.moving for chain in rings], outs.value, small.value
+    )
+    for chain, value in zip(rings, moving, strict=True):
+        chain.moving = value
+    start_all([small, *others])
+    meet([*first, small, *others])
+    start_all([*first, small, *others])
+    meet([*first, small, *others])
+    last = Scatter(jnp.concatenate([chain.value for chain in first], axis=3), ("far",))
+    last.start(direct=True)
+    start_all([small, outs])
+    meet([last, small, outs])
     grad_down = down.value.reshape(-1, half_width)
     grad_gate_up = jnp.concatenate(
         [chain.value.reshape(half_rows, -1) for chain in ffn_sums]
@@ -1721,7 +1723,7 @@
     grad_outs = outs.value.reshape(-1, half_width)
     grad_mixer_out = grad_outs[: mixer_out.shape[0]]
     grad_output = grad_outs[mixer_out.shape[0] :]
-    grad_first = jnp.concatenate([chain.value.reshape(half_rows, first_width) for chain in first[:2]])
+    grad_first = last.value.reshape(rows, first_width)
     sums = small.value
     place = lax.axis_index("dp") * 2 + seq_rank
 

time: 498 us -> 478 us (0.960)
  waiting for transfers between devices: 132 us -> 107 us
  starting transfers between devices: 70.8 us -> 76.7 us
    ppermute x64 -> x61, waiting for transfers between devices: 132 us -> 107 us  [shift(): return lax.ppermute(value, axis, pairs)]
    ppermute x64 -> x61, starting transfers between devices: 66.1 us -> 72 us  [shift(): return lax.ppermute(value, axis, pairs)]
    unnamed x163 -> x159, local copies, waits for them, and re-layouts: 20.2 us -> 20 us
  transfers between devices with their start and end apart: 66 -> 63, of which waited for: 34 -> 32; matrix products, arithmetic and copies ran while one was open for 24% -> 24% of each run, Pallas kernels for 21% -> 21%
where the time goes in v3:
time: 478 us; the launch traced here: 469 us
  waiting for transfers between devices  107 us (22%)
  Pallas kernels  103 us (22%)
  starting transfers between devices  76.7 us (16%)
  other arithmetic  71.4 us (15%)
  matrix products  66.1 us (14%)
  local copies, waits for them, and re-layouts  43.3 us (9%)
    ppermute x61, waiting for transfers between devices, shift(): return lax.ppermute(value, axis, pairs)  107 us
    pallas_call x4, Pallas kernels, call(): pl.pallas_call(kernel, grid=(1,) if blocks else (), out_shape=[jax.ShapeD...  90.7 us
    ppermute x61, starting transfers between devices, shift(): return lax.ppermute(value, axis, pairs)  72 us
    convert_element_type x16, other arithmetic, finish(): self.value = total.astype(self.kind) if self.steps else total  23.8 us
    dot_general x5, matrix products, dot_right_t(): lax.dot_general(left, right, (((1,), (1,)), ((), ())), preferred_element_...  23.7 us
    dot_general x5, matrix products, dot_plain(): return jnp.dot(left, right, preferred_element_type=jnp.float32)  22.3 us
    dot_general x5, matrix products, dot_left_t(): lax.dot_general(left, right, (((0,), (0,)), ((), ())), preferred_element_...  20.1 us
    unnamed x159, local copies, waits for them, and re-layouts  20 us
  transfers between devices with their start and end apart: 63, of which 32 were waited for; matrix products, arithmetic and copies ran while one was open for 24% of the time, Pallas kernels for 21%

profile of v3, /device:TPU:0, one launch (start us, length us, event | category | flops | bytes accessed | tf_op | source)
XLA Modules:
  0.0 469.5 jit_solution(8388397693785587903)
XLA Ops:
  1.6 2.8 concatenate.282
  5.7 3.1 collective-permute-start.3
  8.7 2.6 collective-permute-start.2
  13.6 3.4 collective-permute-start
  22.9 3.8 collective-permute-done.1
  26.7 2.8 collective-permute-done.2
  34.3 10.0 %collective-permute-done.5 = bf16[1,4,1,1,32,2176]{5,4,3,2,1,0:T(8,128)(2,1)S(1)} collective-permute-done((bf16[1,4,1,1,32,2176]{5,4,3,2,1,0:T(8,128)(2,1)S(1)}, bf16[1,4,1,1,32,2176]{5,4,3,2,1,0:T(8,128)(2,1)S(1)}, u32[]{:S(2)}, u32[]{:S(2)}) %collective-permute-start.5) | collective-permute-done | bytes 557088 | tf_op jit(solution)/shard_map/ppermute | solution.py:666
  46.4 6.6 %collective-permute-start.6 = (bf16[1,1,1,1,64,4096]{5,4,3,2,1,0:T(8,128)(2,1)}, bf16[1,1,1,1,64,4096]{5,4,3,2,1,0:T(8,128)(2,1)}, u32[]{:S(2)}, u32[]{:S(2)}) collective-permute-start(bf16[1,1,1,1,64,4096]{5,4,3,2,1,0:T(8,128)(2,1)} %bitcast.1), channel_id=1, source_target_pairs={{0,8},{2,10},{4,12},{6,14},{8,16},{10,18},{12,20},{14,22},{16,24},... | collective-permute-start | bytes 1572872 | tf_op jit(solution)/shard_map/ppermute | solution.py:666
  56.0 7.6 %collective-permute-done.6 = bf16[1,1,1,1,64,4096]{5,4,3,2,1,0:T(8,128)(2,1)} collective-permute-done((bf16[1,1,1,1,64,4096]{5,4,3,2,1,0:T(8,128)(2,1)}, bf16[1,1,1,1,64,4096]{5,4,3,2,1,0:T(8,128)(2,1)}, u32[]{:S(2)}, u32[]{:S(2)}) %collective-permute-start.6) | collective-permute-done | bytes 524320 | tf_op jit(solution)/shard_map/ppermute | solution.py:666
  63.6 2.5 collective-permute-start.7
  67.1 10.2 %collective-permute-done.7 = bf16[1,1,1,1,64,4096]{5,4,3,2,1,0:T(8,128)(2,1)S(1)} collective-permute-done((bf16[1,1,1,1,64,4096]{5,4,3,2,1,0:T(8,128)(2,1)}, bf16[1,1,1,1,64,4096]{5,4,3,2,1,0:T(8,128)(2,1)S(1)}, u32[]{:S(2)}, u32[]{:S(2)}) %collective-permute-start.7) | collective-permute-done | bytes 524320 | tf_op jit(solution)/shard_map/ppermute | solution.py:666
  80.4 9.5 %collective-permute-done.8 = bf16[1,1,1,1,64,4096]{5,4,3,2,1,0:T(8,128)(2,1)S(1)} collective-permute-done((bf16[1,1,1,1,64,4096]{5,4,3,2,1,0:T(8,128)(2,1)S(1)}, bf16[1,1,1,1,64,4096]{5,4,3,2,1,0:T(8,128)(2,1)S(1)}, u32[]{:S(2)}, u32[]{:S(2)}) %collective-permute-start.8) | collective-permute-done | bytes 524320 | tf_op jit(solution)/shard_map/ppermute | solution.py:666
  96.6 2.6 copy-done
  103.3 11.6 %fusion.4.refs_0_.refs_1_.refs_2_.refs_3_.refs_4_.refs_5_.proj_ref = f32[576,4352]{1,0:T(8,128)} fusion(bf16[1024,4352]{1,0:T(8,128)(2,1)} %bitcast.90, f32[1024]{0:T(1024)S(1)} %reshape.800, f32[576]{0:T(1024)S(1)} %fusion.15, bf16[512,1024]{1,0:T(8,128)(2,1)S(1)} %copy-done.13, bf16[64,1024]{1,0:T(8,128)(2,1)S(1)} %collective-permute-done), kind=kOutput, calls=%fused_computation.98 | convolution fusion | flops 5137956864 | bytes 20125952 | tf_op jit(solution)/shard_map/dot_general | solution.py:159
  114.9 6.6 %collective-permute-done.14 = bf16[1,4,1,1,32,4096]{5,4,3,2,1,0:T(8,128)(2,1)S(1)} collective-permute-done((bf16[1,4,1,1,32,4096]{5,4,3,2,1,0:T(8,128)(2,1)S(1)}, bf16[1,4,1,1,32,4096]{5,4,3,2,1,0:T(8,128)(2,1)S(1)}, u32[]{:S(2)}, u32[]{:S(2)}) %collective-permute-start.14) | collective-permute-done | bytes 1048608 | tf_op jit(solution)/shard_map/ppermute | solution.py:666
  131.6 2.1 fusion.5
  137.6 8.9 %shard_map.340 = (bf16[576,768]{1,0:T(8,128)(2,1)}, bf16[512,512]{1,0:T(8,128)(2,1)}) custom-call(f32[576,4352]{1,0:T(8,128)} %fusion.4.refs_0_.refs_1_.refs_2_.refs_3_.refs_4_.refs_5_.proj_ref, f32[576,4352]{1,0:T(8,128)} %fusion.4.refs_0_.refs_1_.refs_2_.refs_3_.refs_4_.refs_5_.proj_ref, ...), custom_call_target="tpu_custom_call" | custom-call | flops 1000000000 | bytes 60756480 | tf_op jit(solution)/shard_map/pallas_call | solution.py:1361
  146.5 23.2 %shard_map.341 = (bf16[512,1536]{1,0:T(8,128)(2,1)}, f32[512,1536]{1,0:T(8,128)}, bf16[9,128,1536]{2,1,0:T(8,128)(2,1)}) custom-call(f32[576,4352]{1,0:T(8,128)} %fusion.4.refs_0_.refs_1_.refs_2_.refs_3_.refs_4_.refs_5_.proj_ref, f32[5,1792]{1,0:T(8,128)} %maximum_convert_fusion.taps_ref, f32[2,24]{1,0:T(2,128)} %pad_maximum_fusion.9.heads_ref, ...), custom_call_target="tpu_custom_call" | custom-call | flops 1000000000 | bytes 10082304 | tf_op jit(solution)/shard_map/pallas_call | solution.py:1361
  169.8 2.4 maximum_select_fusion.refs_0_
  172.2 3.7 maximum_select_fusion.1.refs_2_
  176.3 2.9 fusion.25
  181.5 4.5 collective-permute-done.17.refs_1_
  186.3 9.5 %shard_map.342 = (bf16[4,2,2,64,4096]{4,3,2,1,0:T(8,128)(2,1)}, bf16[4,2,2,96,1024]{4,3,2,1,0:T(8,128)(2,1)S(1)}, bf16[4,2,2,32,1024]{4,3,2,1,0:T(8,128)(2,1)S(1)}) custom-call(s32[1]{0:T(128)} %bitcast.2.core_ref, bf16[2,4,2,1,32,3072]{5,4,3,2,1,0:T(8,128)(2,1)S(1)} %maximum_select_fusion.refs_0_, ...), custom_call_target="tpu_custom_call" | custom-call | bytes 25165824 | tf_op jit(solution)/shard_map/pallas_call | solution.py:758
  196.6 2.4 copy-done.35
  199.0 2.0 multiply_reduce_fusion.5
  203.5 4.6 fusion.31
  209.3 2.4 convolution_bitcast_fusion
  211.7 3.7 multiply_convert_fusion.4
  215.4 2.4 convolution_convert_fusion.3
  220.8 2.6 pad_maximum_fusion
  224.9 3.1 add_convert_fusion.3
  230.2 4.8 %convolution_convert_fusion.1 = bf16[1024,4096]{1,0:T(8,128)(2,1)S(1)} fusion(bf16[512,1024]{1,0:T(8,128)(2,1)S(1)} %copy-done.48, bf16[512,4096]{1,0:T(8,128)(2,1)S(1)} %pad_maximum_fusion), kind=kOutput, calls=%fused_computation.1 | convolution fusion | flops 4299161600 | bytes 13631488 | tf_op jit(solution)/shard_map/dot_general | solution.py:169
  235.0 2.2 broadcast_select_fusion.2
  237.8 7.7 %multiply_reduce_fusion.3 = (f32[1024]{0:T(1024)S(1)}, f32[512]{0:T(512)S(1)}, f32[512,1024]{1,0:T(8,128)S(1)}) fusion(f32[512,1024]{1,0:T(8,128)S(1)} %get-tuple-element.246, f32[512]{0:T(512)S(1)} %fusion.17, f32[1024]{0:T(1024)S(1)} %reshape.802, bf16[512,4096]{1,0:T(8,128)(2,1)S(1)} %pad_maximum_fusion, bf16[1024,4096]{1,0:T(8,128)(2,1)} %bitcast.117), kind=kOutput, calls=%fused_computation.39 | convolution fusion | flops 4298111488 | bytes 16789504 | tf_op jit(solution)/shard_map/dot_general | solution.py:163
  250.5 2.4 broadcast_select_fusion.4
  253.2 3.8 add_convert_fusion.4
  262.4 2.9 convolution_convert_fusion.5.grad_ref
  265.3 12.8 %shard_map.344.attention_ref = bf16[576,768]{1,0:T(8,128)(2,1)} custom-call(bf16[576,768]{1,0:T(8,128)(2,1)} %get-tuple-element.173.turned_ref, bf16[512,512]{1,0:T(8,128)(2,1)} %convolution_convert_fusion.5.grad_ref, f32[576,128]{1,0:T(8,128)} %get-tuple-element.281.refs_6_.cos_ref, f32[576,128]{1,0:T(8,128)} %get-tuple-element.280.refs_7_.sin_ref, ...), custom_call_target="tpu_custom_call" | custom-call | flops 1000000000 | bytes 2003456 | tf_op jit(solution)/shard_map/pallas_call | solution.py:1361
  278.1 3.5 fusion.32.grad_ref
  281.6 3.3 collective-permute-done.26
  286.3 3.0 add_convert_fusion.2
  289.4 2.0 add_convert_fusion.9
  291.4 2.1 add_convert_fusion.10
  303.1 3.4 add_convert_fusion.12
  306.5 45.7 %shard_map.345 = (bf16[576,4352]{1,0:T(8,128)(2,1)}, f32[16,1792]{1,0:T(8,128)}) custom-call(f32[576,4352]{1,0:T(8,128)} %fusion.4.refs_0_.refs_1_.refs_2_.refs_3_.refs_4_.refs_5_.proj_ref, f32[512,1536]{1,0:T(8,128)} %get-tuple-element.183.mix_ref, bf16[9,128,1536]{2,1,0:T(8,128)(2,1)} %get-tuple-element.184.states_ref, f32[512,1536]{1,0:T(8,128)} %fusion.32.grad_ref, ...), custom_call_target="tpu_custom_call" | custom-call | flops 1000000000 | bytes 20797440 | tf_op jit(solution)/shard_map/pallas_call | solution.py:1361
  359.5 10.3 %convolution_convert_fusion = bf16[1024,4352]{1,0:T(8,128)(2,1)S(1)} fusion(bf16[576,4352]{1,0:T(8,128)(2,1)} %get-tuple-element.199, f32[1024]{0:T(1024)S(1)} %reshape.800, f32[576]{0:T(1024)S(1)} %fusion.15, bf16[512,1024]{1,0:T(8,128)(2,1)S(1)} %copy-done.14, bf16[64,1024]{1,0:T(8,128)(2,1)S(1)} %collective-permute-done), kind=kOutput, calls=%fused_computation | convolution fusion | flops 5142413312 | bytes 15112448 | tf_op jit(solution)/shard_map/dot_general | solution.py:169
  370.5 2.4 broadcast_select_fusion
  373.5 7.3 %fusion.33 = f32[576,1024]{1,0:T(8,128)S(1)} fusion(bf16[576,4352]{1,0:T(8,128)(2,1)} %get-tuple-element.199, bf16[1024,4352]{1,0:T(8,128)(2,1)S(1)} %bitcast.93), kind=kOutput, calls=%fused_computation.209 | convolution fusion | flops 5133828096 | bytes 16285696 | tf_op jit(solution)/shard_map/dot_general | solution.py:163
  386.7 3.2 collective-permute-start.46
  389.8 2.5 collective-permute-start.45
  394.1 10.5 %collective-permute-start.50 = (bf16[1,1,1,128,512]{4,3,2,1,0:T(8,128)(2,1)S(1)}, bf16[1,1,1,128,512]{4,3,2,1,0:T(8,128)(2,1)S(1)}, u32[]{:S(2)}, u32[]{:S(2)}) collective-permute-start(bf16[1,1,1,128,512]{4,3,2,1,0:T(8,128)(2,1)S(1)} %constant_dynamic-slice_fusion.2), channel_id=1, source_target_pairs={{0,8},{2,10},{4,12},{6,14},{8,16},{10,18},{12,20},{14,22},{16,24},... | collective-permute-start | bytes 393224 | tf_op jit(solution)/shard_map/ppermute | solution.py:666
  405.5 2.8 collective-permute-done.50
  408.4 2.5 collective-permute-start.49
  411.4 2.2 collective-permute-done.47
  421.6 2.7 collective-permute-done.53
  424.4 2.9 collective-permute-done.57
  427.3 2.0 fusion.2
  430.1 2.0 collective-permute-done.56
  432.1 2.0 collective-permute-done.54
  435.0 3.6 collective-permute-start.60
  442.3 2.6 collective-permute-done.61
  444.9 4.6 collective-permute-done.60
  449.5 5.1 %collective-permute-done.58 = bf16[1,1,1,64,2176]{4,3,2,1,0:T(8,128)(2,1)S(1)} collective-permute-done((bf16[1,1,1,64,2176]{4,3,2,1,0:T(8,128)(2,1)S(1)}, bf16[1,1,1,64,2176]{4,3,2,1,0:T(8,128)(2,1)S(1)}, u32[]{:S(2)}, u32[]{:S(2)}) %collective-permute-start.58) | collective-permute-done | bytes 278560 | tf_op jit(solution)/shard_map/ppermute | solution.py:666
  454.6 7.5 %collective-permute-done.59 = bf16[1,1,1,64,2176]{4,3,2,1,0:T(8,128)(2,1)S(1)} collective-permute-done((bf16[1,1,1,64,2176]{4,3,2,1,0:T(8,128)(2,1)S(1)}, bf16[1,1,1,64,2176]{4,3,2,1,0:T(8,128)(2,1)S(1)}, u32[]{:S(2)}, u32[]{:S(2)}) %collective-permute-start.59) | collective-permute-done | bytes 278560 | tf_op jit(solution)/shard_map/ppermute | solution.py:666
  (396 shorter events, 122.8 us)
Async XLA Ops:
  5.7 23.9 %collective-permute-start.3 = (bf16[1,1,1,1,64,2176]{5,4,3,2,1,0:T(8,128)(2,1)S(1)}, bf16[1,1,1,1,64,2176]{5,4,3,2,1,0:T(8,128)(2,1)S(1)}, u32[]{:S(2)}, u32[]{:S(2)}) collective-permute-start(bf16[1,1,1,1,64,2176]{5,4,3,2,1,0:T(8,128)(2,1)S(1)} %pad_bitcast_fusion), channel_id=1, source_target_pairs={{0,8},{2,10},{4,12},{6,14},{8,16},{10,18},{12,20},{14,22},{16,24},... | collective-permute-start | bytes 835592 | tf_op jit(solution)/shard_map/ppermute | solution.py:666
  8.7 20.8 %collective-permute-start.2 = (bf16[1,1,1,1,64,2176]{5,4,3,2,1,0:T(8,128)(2,1)S(1)}, bf16[1,1,1,1,64,2176]{5,4,3,2,1,0:T(8,128)(2,1)S(1)}, u32[]{:S(2)}, u32[]{:S(2)}) collective-permute-start(bf16[1,1,1,1,64,2176]{5,4,3,2,1,0:T(8,128)(2,1)S(1)} %pad_bitcast_fusion), channel_id=1, source_target_pairs={{0,16},{2,18},{4,20},{6,22},{8,24},{10,26},{12,28},{14,30},{16,0},... | collective-permute-start | bytes 835592 | tf_op jit(solution)/shard_map/ppermute | solution.py:666
  11.3 15.3 %collective-permute-start.1 = (bf16[1,1,1,1,64,2176]{5,4,3,2,1,0:T(8,128)(2,1)S(1)}, bf16[1,1,1,1,64,2176]{5,4,3,2,1,0:T(8,128)(2,1)S(1)}, u32[]{:S(2)}, u32[]{:S(2)}) collective-permute-start(bf16[1,1,1,1,64,2176]{5,4,3,2,1,0:T(8,128)(2,1)S(1)} %pad_bitcast_fusion), channel_id=1, source_target_pairs={{0,24},{2,26},{4,28},{6,30},{8,0},{10,2},{12,4},{14,6},{16,8},{18,... | collective-permute-start | bytes 835592 | tf_op jit(solution)/shard_map/ppermute | solution.py:666
  13.6 39.7 %collective-permute-start = (bf16[64,1024]{1,0:T(8,128)(2,1)S(1)}, bf16[64,1024]{1,0:T(8,128)(2,1)S(1)}, u32[]{:S(2)}, u32[]{:S(2)}) collective-permute-start(bf16[64,1024]{1,0:T(8,128)(2,1)S(1)} %slice.298), channel_id=1, source_target_pairs={{0,1},{2,3},{4,5},{6,7},{8,9},{10,11},{12,13},{14,15},{16,17},{18,... | collective-permute-start | bytes 393224 | tf_op jit(solution)/shard_map/ppermute | solution.py:1484
  29.8 14.5 %collective-permute-start.5 = (bf16[1,4,1,1,32,2176]{5,4,3,2,1,0:T(8,128)(2,1)S(1)}, bf16[1,4,1,1,32,2176]{5,4,3,2,1,0:T(8,128)(2,1)S(1)}, u32[]{:S(2)}, u32[]{:S(2)}) collective-permute-start(bf16[1,4,1,1,32,2176]{5,4,3,2,1,0:T(8,128)(2,1)S(1)} %get-tuple-element.263), channel_id=1, source_target_pairs={{0,1},{1,0},{2,3},{3,2},{4,5},{5,4},{6,7},{7,6},{8,9},{9,8},{10,11... | collective-permute-start | bytes 1671176 | tf_op jit(solution)/shard_map/ppermute | solution.py:666
  32.1 14.2 %collective-permute-start.4 = (bf16[1,4,1,1,32,2176]{5,4,3,2,1,0:T(8,128)(2,1)S(1)}, bf16[1,4,1,1,32,2176]{5,4,3,2,1,0:T(8,128)(2,1)S(1)}, u32[]{:S(2)}, u32[]{:S(2)}) collective-permute-start(bf16[1,4,1,1,32,2176]{5,4,3,2,1,0:T(8,128)(2,1)S(1)} %get-tuple-element.264), channel_id=1, source_target_pairs={{0,4},{2,6},{4,0},{6,2},{8,12},{10,14},{12,8},{14,10},{16,20},{18,... | collective-permute-start | bytes 1671176 | tf_op jit(solution)/shard_map/ppermute | solution.py:666
  46.4 17.1 %collective-permute-start.6 = (bf16[1,1,1,1,64,4096]{5,4,3,2,1,0:T(8,128)(2,1)}, bf16[1,1,1,1,64,4096]{5,4,3,2,1,0:T(8,128)(2,1)}, u32[]{:S(2)}, u32[]{:S(2)}) collective-permute-start(bf16[1,1,1,1,64,4096]{5,4,3,2,1,0:T(8,128)(2,1)} %bitcast.1), channel_id=1, source_target_pairs={{0,8},{2,10},{4,12},{6,14},{8,16},{10,18},{12,20},{14,22},{16,24},... | collective-permute-start | bytes 1572872 | tf_op jit(solution)/shard_map/ppermute | solution.py:666
  53.6 25.1 %collective-permute-start.11 = (bf16[2,4,1,1,32,2176]{5,4,3,2,1,0:T(8,128)(2,1)S(1)}, bf16[2,4,1,1,32,2176]{5,4,3,2,1,0:T(8,128)(2,1)S(1)}, u32[]{:S(2)}, u32[]{:S(2)}) collective-permute-start(bf16[2,4,1,1,32,2176]{5,4,3,2,1,0:T(8,128)(2,1)S(1)} %maximum_select_fusion.7), channel_id=1, source_target_pairs={{0,4},{2,6},{4,0},{6,2},{8,12},{10,14},{12,8},{14,10},{16,20},{18,... | collective-permute-start | bytes 3342344 | tf_op jit(solution)/shard_map/ppermute | solution.py:666
  55.2 24.8 %collective-permute-start.9 = (bf16[1,4,2,1,32,2176]{5,4,3,2,1,0:T(8,128)(2,1)S(1)}, bf16[1,4,2,1,32,2176]{5,4,3,2,1,0:T(8,128)(2,1)S(1)}, u32[]{:S(2)}, u32[]{:S(2)}) collective-permute-start(bf16[1,4,2,1,32,2176]{5,4,3,2,1,0:T(8,128)(2,1)S(1)} %maximum_select_fusion.6), channel_id=1, source_target_pairs={{0,1},{1,0},{2,3},{3,2},{4,5},{5,4},{6,7},{7,6},{8,9},{9,8},{10,11... | collective-permute-start | bytes 3342344 | tf_op jit(solution)/shard_map/ppermute | solution.py:666
  63.6 13.8 %collective-permute-start.7 = (bf16[1,1,1,1,64,4096]{5,4,3,2,1,0:T(8,128)(2,1)}, bf16[1,1,1,1,64,4096]{5,4,3,2,1,0:T(8,128)(2,1)S(1)}, u32[]{:S(2)}, u32[]{:S(2)}) collective-permute-start(bf16[1,1,1,1,64,4096]{5,4,3,2,1,0:T(8,128)(2,1)} %collective-permute-done.6), channel_id=1, source_target_pairs={{0,8},{2,10},{4,12},{6,14},{8,16},{10,18},{12,20},{14,22},{16,24},... | collective-permute-start | bytes 1572872 | tf_op jit(solution)/shard_map/ppermute | solution.py:666
  77.3 12.6 %collective-permute-start.8 = (bf16[1,1,1,1,64,4096]{5,4,3,2,1,0:T(8,128)(2,1)S(1)}, bf16[1,1,1,1,64,4096]{5,4,3,2,1,0:T(8,128)(2,1)S(1)}, u32[]{:S(2)}, u32[]{:S(2)}) collective-permute-start(bf16[1,1,1,1,64,4096]{5,4,3,2,1,0:T(8,128)(2,1)S(1)} %collective-permute-done.7), channel_id=1, source_target_pairs={{0,8},{2,10},{4,12},{6,14},{8,16},{10,18},{12,20},{14,22},{16,24},... | collective-permute-start | bytes 1572872 | tf_op jit(solution)/shard_map/ppermute | solution.py:666
  79.0 14.6 %collective-permute-start.12 = (bf16[2,4,2,1,32,2176]{5,4,3,2,1,0:T(8,128)(2,1)S(1)}, bf16[2,4,2,1,32,2176]{5,4,3,2,1,0:T(8,128)(2,1)S(1)}, u32[]{:S(2)}, u32[]{:S(2)}) collective-permute-start(bf16[2,4,2,1,32,2176]{5,4,3,2,1,0:T(8,128)(2,1)S(1)} %maximum_select_fusion.3.refs_2_), channel_id=1, source_target_pairs={{0,2},{2,0},{4,6},{6,4},{8,10},{10,8},{12,14},{14,12},{16,18},{18,... | collective-permute-start | bytes 6684680 | tf_op jit(solution)/shard_map/ppermute | solution.py:666
  80.4 13.3 %collective-permute-start.10 = (bf16[2,4,2,1,32,2176]{5,4,3,2,1,0:T(8,128)(2,1)S(1)}, bf16[2,4,2,1,32,2176]{5,4,3,2,1,0:T(8,128)(2,1)S(1)}, u32[]{:S(2)}, u32[]{:S(2)}) collective-permute-start(bf16[2,4,2,1,32,2176]{5,4,3,2,1,0:T(8,128)(2,1)S(1)} %maximum_select_fusion.2.refs_0_), channel_id=1, source_target_pairs={{0,2},{2,0},{4,6},{6,4},{8,10},{10,8},{12,14},{14,12},{16,18},{18,... | collective-permute-start | bytes 6684680 | tf_op jit(solution)/shard_map/ppermute | solution.py:666
  100.3 21.2 %collective-permute-start.14 = (bf16[1,4,1,1,32,4096]{5,4,3,2,1,0:T(8,128)(2,1)S(1)}, bf16[1,4,1,1,32,4096]{5,4,3,2,1,0:T(8,128)(2,1)S(1)}, u32[]{:S(2)}, u32[]{:S(2)}) collective-permute-start(bf16[1,4,1,1,32,4096]{5,4,3,2,1,0:T(8,128)(2,1)S(1)} %get-tuple-element.137), channel_id=1, source_target_pairs={{0,1},{1,0},{2,3},{3,2},{4,5},{5,4},{6,7},{7,6},{8,9},{9,8},{10,11... | collective-permute-start | bytes 3145736 | tf_op jit(solution)/shard_map/ppermute | solution.py:666
  101.8 21.3 %collective-permute-start.13 = (bf16[1,4,1,1,32,4096]{5,4,3,2,1,0:T(8,128)(2,1)}, bf16[1,4,1,1,32,4096]{5,4,3,2,1,0:T(8,128)(2,1)S(1)}, u32[]{:S(2)}, u32[]{:S(2)}) collective-permute-start(bf16[1,4,1,1,32,4096]{5,4,3,2,1,0:T(8,128)(2,1)} %get-tuple-element.135), channel_id=1, source_target_pairs={{0,4},{2,6},{4,0},{6,2},{8,12},{10,14},{12,8},{14,10},{16,20},{18,... | collective-permute-start | bytes 3145736 | tf_op jit(solution)/shard_map/ppermute | solution.py:666
  125.8 43.9 %collective-permute-start.15 = (bf16[1,4,2,1,32,3072]{5,4,3,2,1,0:T(8,128)(2,1)S(1)}, bf16[1,4,2,1,32,3072]{5,4,3,2,1,0:T(8,128)(2,1)}, u32[]{:S(2)}, u32[]{:S(2)}) collective-permute-start(bf16[1,4,2,1,32,3072]{5,4,3,2,1,0:T(8,128)(2,1)S(1)} %slice.382), channel_id=1, source_target_pairs={{0,1},{1,0},{2,3},{3,2},{4,5},{5,4},{6,7},{7,6},{8,9},{9,8},{10,11... | collective-permute-start | bytes 4718600 | tf_op jit(solution)/shard_map/ppermute | solution.py:666
  126.3 43.5 %collective-permute-start.16 = (bf16[2,4,1,1,32,3072]{5,4,3,2,1,0:T(8,128)(2,1)S(1)}, bf16[2,4,1,1,32,3072]{5,4,3,2,1,0:T(8,128)(2,1)}, u32[]{:S(2)}, u32[]{:S(2)}) collective-permute-start(bf16[2,4,1,1,32,3072]{5,4,3,2,1,0:T(8,128)(2,1)S(1)} %slice.383), channel_id=1, source_target_pairs={{0,4},{2,6},{4,0},{6,2},{8,12},{10,14},{12,8},{14,10},{16,20},{18,... | collective-permute-start | bytes 4718600 | tf_op jit(solution)/shard_map/ppermute | solution.py:666
  175.8 10.3 %collective-permute-start.17 = (bf16[2,4,2,1,32,3072]{5,4,3,2,1,0:T(8,128)(2,1)S(1)}, bf16[2,4,2,1,32,3072]{5,4,3,2,1,0:T(8,128)(2,1)}, u32[]{:S(2)}, u32[]{:S(2)}) collective-permute-start(bf16[2,4,2,1,32,3072]{5,4,3,2,1,0:T(8,128)(2,1)S(1)} %maximum_select_fusion.refs_0_), channel_id=1, source_target_pairs={{0,2},{2,0},{4,6},{6,4},{8,10},{10,8},{12,14},{14,12},{16,18},{18,... | collective-permute-start | bytes 9437192 | tf_op jit(solution)/shard_map/ppermute | solution.py:666
  175.8 10.5 %collective-permute-start.18 = (bf16[2,4,2,1,32,3072]{5,4,3,2,1,0:T(8,128)(2,1)}, bf16[2,4,2,1,32,3072]{5,4,3,2,1,0:T(8,128)(2,1)}, u32[]{:S(2)}, u32[]{:S(2)}) collective-permute-start(bf16[2,4,2,1,32,3072]{5,4,3,2,1,0:T(8,128)(2,1)} %maximum_select_fusion.1.refs_2_), channel_id=1, source_target_pairs={{0,2},{2,0},{4,6},{6,4},{8,10},{10,8},{12,14},{14,12},{16,18},{18,... | collective-permute-start | bytes 9437192 | tf_op jit(solution)/shard_map/ppermute | solution.py:666
  179.4 22.0 %collective-permute-start.19 = (bf16[1,4,2,1,32,1024]{5,4,3,2,1,0:T(8,128)(2,1)}, bf16[1,4,2,1,32,1024]{5,4,3,2,1,0:T(8,128)(2,1)S(1)}, u32[]{:S(2)}, u32[]{:S(2)}) collective-permute-start(bf16[1,4,2,1,32,1024]{5,4,3,2,1,0:T(8,128)(2,1)} %slice.384), channel_id=1, source_target_pairs={{0,1},{1,0},{2,3},{3,2},{4,5},{5,4},{6,7},{7,6},{8,9},{9,8},{10,11... | collective-permute-start | bytes 1572872 | tf_op jit(solution)/shard_map/ppermute | solution.py:666
  181.0 20.4 %collective-permute-start.20 = (bf16[2,4,1,1,32,1024]{5,4,3,2,1,0:T(8,128)(2,1)}, bf16[2,4,1,1,32,1024]{5,4,3,2,1,0:T(8,128)(2,1)S(1)}, u32[]{:S(2)}, u32[]{:S(2)}) collective-permute-start(bf16[2,4,1,1,32,1024]{5,4,3,2,1,0:T(8,128)(2,1)} %slice.385), channel_id=1, source_target_pairs={{0,4},{2,6},{4,0},{6,2},{8,12},{10,14},{12,8},{14,10},{16,20},{18,... | collective-permute-start | bytes 1572872 | tf_op jit(solution)/shard_map/ppermute | solution.py:666
  201.1 44.4 %copy-start.9 = (f32[512,1024]{1,0:T(8,128)}, f32[512,1024]{1,0:T(8,128)S(1)}, u32[]{:S(2)}) copy-start(f32[512,1024]{1,0:T(8,128)S(1)} %get-tuple-element.246) | copy-start | bytes 6291460
  202.6 5.4 %collective-permute-start.22 = (bf16[2,4,2,1,32,1024]{5,4,3,2,1,0:T(8,128)(2,1)S(1)}, bf16[2,4,2,1,32,1024]{5,4,3,2,1,0:T(8,128)(2,1)S(1)}, u32[]{:S(2)}, u32[]{:S(2)}) collective-permute-start(bf16[2,4,2,1,32,1024]{5,4,3,2,1,0:T(8,128)(2,1)S(1)} %maximum_select_fusion.9.refs_2_), channel_id=1, source_target_pairs={{0,2},{2,0},{4,6},{6,4},{8,10},{10,8},{12,14},{14,12},{16,18},{18,... | collective-permute-start | bytes 3145736 | tf_op jit(solution)/shard_map/ppermute | solution.py:666
  203.2 4.8 %collective-permute-start.21 = (bf16[2,4,2,1,32,1024]{5,4,3,2,1,0:T(8,128)(2,1)S(1)}, bf16[2,4,2,1,32,1024]{5,4,3,2,1,0:T(8,128)(2,1)S(1)}, u32[]{:S(2)}, u32[]{:S(2)}) collective-permute-start(bf16[2,4,2,1,32,1024]{5,4,3,2,1,0:T(8,128)(2,1)S(1)} %maximum_select_fusion.8.refs_0_), channel_id=1, source_target_pairs={{0,2},{2,0},{4,6},{6,4},{8,10},{10,8},{12,14},{14,12},{16,18},{18,... | collective-permute-start | bytes 3145736 | tf_op jit(solution)/shard_map/ppermute | solution.py:666
  220.4 4.5 collective-permute-start.23
  229.7 51.9 %collective-permute-start.28 = (bf16[4,1,1,128,1024]{4,3,2,1,0:T(8,128)(2,1)}, bf16[4,1,1,128,1024]{4,3,2,1,0:T(8,128)(2,1)}, u32[]{:S(2)}, u32[]{:S(2)}) collective-permute-start(bf16[4,1,1,128,1024]{4,3,2,1,0:T(8,128)(2,1)} %broadcast_select_fusion.9), channel_id=1, source_target_pairs={{0,4},{2,6},{4,0},{6,2},{8,12},{10,14},{12,8},{14,10},{16,20},{18,... | collective-permute-start | bytes 3145736 | tf_op jit(solution)/shard_map/ppermute | solution.py:666
  237.2 9.6 %collective-permute-start.25 = (bf16[4,2,1,32,4096]{4,3,2,1,0:T(8,128)(2,1)}, bf16[4,2,1,32,4096]{4,3,2,1,0:T(8,128)(2,1)}, u32[]{:S(2)}, u32[]{:S(2)}) collective-permute-start(bf16[4,2,1,32,4096]{4,3,2,1,0:T(8,128)(2,1)} %get-tuple-element.259), channel_id=1, source_target_pairs={{0,2},{2,0},{4,6},{6,4},{8,10},{10,8},{12,14},{14,12},{16,18},{18,... | collective-permute-start | bytes 6291464 | tf_op jit(solution)/shard_map/ppermute | solution.py:666
  237.5 9.4 %collective-permute-start.24 = (bf16[4,2,1,32,4096]{4,3,2,1,0:T(8,128)(2,1)}, bf16[4,2,1,32,4096]{4,3,2,1,0:T(8,128)(2,1)}, u32[]{:S(2)}, u32[]{:S(2)}) collective-permute-start(bf16[4,2,1,32,4096]{4,3,2,1,0:T(8,128)(2,1)} %get-tuple-element.260), channel_id=1, source_target_pairs={{0,2},{2,0},{4,6},{6,4},{8,10},{10,8},{12,14},{14,12},{16,18},{18,... | collective-permute-start | bytes 6291464 | tf_op jit(solution)/shard_map/ppermute | solution.py:666
  252.9 33.4 %collective-permute-start.29 = (bf16[4,2,1,128,1024]{4,3,2,1,0:T(8,128)(2,1)}, bf16[4,2,1,128,1024]{4,3,2,1,0:T(8,128)(2,1)}, u32[]{:S(2)}, u32[]{:S(2)}) collective-permute-start(bf16[4,2,1,128,1024]{4,3,2,1,0:T(8,128)(2,1)} %broadcast_select_fusion.4), channel_id=1, source_target_pairs={{0,2},{2,0},{4,6},{6,4},{8,10},{10,8},{12,14},{14,12},{16,18},{18,... | collective-permute-start | bytes 6291464 | tf_op jit(solution)/shard_map/ppermute | solution.py:666
  259.3 25.6 %collective-permute-start.26 = (bf16[4,2,1,32,2048]{4,3,2,1,0:T(8,128)(2,1)}, bf16[4,2,1,32,2048]{4,3,2,1,0:T(8,128)(2,1)}, u32[]{:S(2)}, u32[]{:S(2)}) collective-permute-start(bf16[4,2,1,32,2048]{4,3,2,1,0:T(8,128)(2,1)} %broadcast_select_fusion.11), channel_id=1, source_target_pairs={{0,1},{1,0},{2,3},{3,2},{4,5},{5,4},{6,7},{7,6},{8,9},{9,8},{10,11... | collective-permute-start | bytes 3145736 | tf_op jit(solution)/shard_map/ppermute | solution.py:666
  261.0 25.3 %collective-permute-start.27 = (bf16[4,1,1,32,4096]{4,3,2,1,0:T(8,128)(2,1)}, bf16[4,1,1,32,4096]{4,3,2,1,0:T(8,128)(2,1)}, u32[]{:S(2)}, u32[]{:S(2)}) collective-permute-start(bf16[4,1,1,32,4096]{4,3,2,1,0:T(8,128)(2,1)} %broadcast_select_fusion.10), channel_id=1, source_target_pairs={{0,4},{2,6},{4,0},{6,2},{8,12},{10,14},{12,8},{14,10},{16,20},{18,... | collective-permute-start | bytes 3145736 | tf_op jit(solution)/shard_map/ppermute | solution.py:666
  297.1 55.1 %collective-permute-start.32 = (bf16[4,1,1,128,512]{4,3,2,1,0:T(8,128)(2,1)}, bf16[4,1,1,128,512]{4,3,2,1,0:T(8,128)(2,1)}, u32[]{:S(2)}, u32[]{:S(2)}) collective-permute-start(bf16[4,1,1,128,512]{4,3,2,1,0:T(8,128)(2,1)} %broadcast_select_fusion.15), channel_id=1, source_target_pairs={{0,1},{1,0},{2,3},{3,2},{4,5},{5,4},{6,7},{7,6},{8,9},{9,8},{10,11... | collective-permute-start | bytes 1572872 | tf_op jit(solution)/shard_map/ppermute | solution.py:666
  297.5 54.7 %collective-permute-start.31 = (bf16[4,1,1,32,2048]{4,3,2,1,0:T(8,128)(2,1)}, bf16[4,1,1,32,2048]{4,3,2,1,0:T(8,128)(2,1)S(1)}, u32[]{:S(2)}, u32[]{:S(2)}) collective-permute-start(bf16[4,1,1,32,2048]{4,3,2,1,0:T(8,128)(2,1)} %broadcast_select_fusion.16), channel_id=1, source_target_pairs={{0,1},{1,0},{2,3},{3,2},{4,5},{5,4},{6,7},{7,6},{8,9},{9,8},{10,11... | collective-permute-start | bytes 1572872 | tf_op jit(solution)/shard_map/ppermute | solution.py:666
  300.2 52.0 %collective-permute-start.33 = (bf16[4,1,1,128,1024]{4,3,2,1,0:T(8,128)(2,1)}, bf16[4,1,1,128,1024]{4,3,2,1,0:T(8,128)(2,1)S(1)}, u32[]{:S(2)}, u32[]{:S(2)}) collective-permute-start(bf16[4,1,1,128,1024]{4,3,2,1,0:T(8,128)(2,1)} %broadcast_select_fusion.8), channel_id=1, source_target_pairs={{0,4},{2,6},{4,0},{6,2},{8,12},{10,14},{12,8},{14,10},{16,20},{18,... | collective-permute-start | bytes 3145736 | tf_op jit(solution)/shard_map/ppermute | solution.py:666
  302.6 49.6 %collective-permute-start.30 = (bf16[4,1,1,32,2048]{4,3,2,1,0:T(8,128)(2,1)}, bf16[4,1,1,32,2048]{4,3,2,1,0:T(8,128)(2,1)}, u32[]{:S(2)}, u32[]{:S(2)}) collective-permute-start(bf16[4,1,1,32,2048]{4,3,2,1,0:T(8,128)(2,1)} %broadcast_select_fusion.17), channel_id=1, source_target_pairs={{0,4},{2,6},{4,0},{6,2},{8,12},{10,14},{12,8},{14,10},{16,20},{18,... | collective-permute-start | bytes 1572872 | tf_op jit(solution)/shard_map/ppermute | solution.py:666
  358.1 11.7 %collective-permute-start.36 = (bf16[1,1,1,128,512]{4,3,2,1,0:T(8,128)(2,1)S(1)}, bf16[1,1,1,128,512]{4,3,2,1,0:T(8,128)(2,1)S(1)}, u32[]{:S(2)}, u32[]{:S(2)}) collective-permute-start(bf16[1,1,1,128,512]{4,3,2,1,0:T(8,128)(2,1)S(1)} %constant_dynamic-slice_fusion.3), channel_id=1, source_target_pairs={{0,8},{2,10},{4,12},{6,14},{8,16},{10,18},{12,20},{14,22},{16,24},... | collective-permute-start | bytes 393224 | tf_op jit(solution)/shard_map/ppermute | solution.py:666
  358.2 11.7 %collective-permute-start.35 = (bf16[1,1,1,32,2048]{4,3,2,1,0:T(8,128)(2,1)S(1)}, bf16[1,1,1,32,2048]{4,3,2,1,0:T(8,128)(2,1)S(1)}, u32[]{:S(2)}, u32[]{:S(2)}) collective-permute-start(bf16[1,1,1,32,2048]{4,3,2,1,0:T(8,128)(2,1)S(1)} %constant_dynamic-slice_fusion.4), channel_id=1, source_target_pairs={{0,8},{2,10},{4,12},{6,14},{8,16},{10,18},{12,20},{14,22},{16,24},... | collective-permute-start | bytes 393224 | tf_op jit(solution)/shard_map/ppermute | solution.py:666
  358.3 11.6 %collective-permute-start.34 = (bf16[1,1,1,32,2048]{4,3,2,1,0:T(8,128)(2,1)S(1)}, bf16[1,1,1,32,2048]{4,3,2,1,0:T(8,128)(2,1)S(1)}, u32[]{:S(2)}, u32[]{:S(2)}) collective-permute-start(bf16[1,1,1,32,2048]{4,3,2,1,0:T(8,128)(2,1)S(1)} %constant_dynamic-slice_fusion.5), channel_id=1, source_target_pairs={{0,8},{2,10},{4,12},{6,14},{8,16},{10,18},{12,20},{14,22},{16,24},... | collective-permute-start | bytes 393224 | tf_op jit(solution)/shard_map/ppermute | solution.py:666
  359.1 11.2 %collective-permute-start.37 = (bf16[4,1,1,128,512]{4,3,2,1,0:T(8,128)(2,1)S(1)}, bf16[4,1,1,128,512]{4,3,2,1,0:T(8,128)(2,1)S(1)}, u32[]{:S(2)}, u32[]{:S(2)}) collective-permute-start(bf16[4,1,1,128,512]{4,3,2,1,0:T(8,128)(2,1)S(1)} %broadcast_select_fusion.14), channel_id=1, source_target_pairs={{0,1},{1,0},{2,3},{3,2},{4,5},{5,4},{6,7},{7,6},{8,9},{9,8},{10,11... | collective-permute-start | bytes 1572872 | tf_op jit(solution)/shard_map/ppermute | solution.py:666
  372.8 8.0 %collective-permute-start.39 = (bf16[4,2,1,32,4352]{4,3,2,1,0:T(8,128)(2,1)}, bf16[4,2,1,32,4352]{4,3,2,1,0:T(8,128)(2,1)S(1)}, u32[]{:S(2)}, u32[]{:S(2)}) collective-permute-start(bf16[4,2,1,32,4352]{4,3,2,1,0:T(8,128)(2,1)} %get-tuple-element.253), channel_id=1, source_target_pairs={{0,2},{2,0},{4,6},{6,4},{8,10},{10,8},{12,14},{14,12},{16,18},{18,... | collective-permute-start | bytes 6684680 | tf_op jit(solution)/shard_map/ppermute | solution.py:666
  372.8 8.0 %collective-permute-start.38 = (bf16[4,2,1,32,4352]{4,3,2,1,0:T(8,128)(2,1)}, bf16[4,2,1,32,4352]{4,3,2,1,0:T(8,128)(2,1)S(1)}, u32[]{:S(2)}, u32[]{:S(2)}) collective-permute-start(bf16[4,2,1,32,4352]{4,3,2,1,0:T(8,128)(2,1)} %get-tuple-element.254), channel_id=1, source_target_pairs={{0,2},{2,0},{4,6},{6,4},{8,10},{10,8},{12,14},{14,12},{16,18},{18,... | collective-permute-start | bytes 6684680 | tf_op jit(solution)/shard_map/ppermute | solution.py:666
  383.5 3.2 collective-permute-start.41
  383.8 33.5 %collective-permute-start.43 = (bf16[4,1,1,32,4352]{4,3,2,1,0:T(8,128)(2,1)S(1)}, bf16[4,1,1,32,4352]{4,3,2,1,0:T(8,128)(2,1)S(1)}, u32[]{:S(2)}, u32[]{:S(2)}) collective-permute-start(bf16[4,1,1,32,4352]{4,3,2,1,0:T(8,128)(2,1)S(1)} %broadcast_select_fusion.6), channel_id=1, source_target_pairs={{0,4},{2,6},{4,0},{6,2},{8,12},{10,14},{12,8},{14,10},{16,20},{18,... | collective-permute-start | bytes 3342344 | tf_op jit(solution)/shard_map/ppermute | solution.py:666
  385.5 31.9 %collective-permute-start.42 = (bf16[4,2,1,32,2176]{4,3,2,1,0:T(8,128)(2,1)S(1)}, bf16[4,2,1,32,2176]{4,3,2,1,0:T(8,128)(2,1)S(1)}, u32[]{:S(2)}, u32[]{:S(2)}) collective-permute-start(bf16[4,2,1,32,2176]{4,3,2,1,0:T(8,128)(2,1)S(1)} %broadcast_select_fusion.7), channel_id=1, source_target_pairs={{0,1},{1,0},{2,3},{3,2},{4,5},{5,4},{6,7},{7,6},{8,9},{9,8},{10,11... | collective-permute-start | bytes 3342344 | tf_op jit(solution)/shard_map/ppermute | solution.py:666
  386.7 7.4 %collective-permute-start.46 = (f32[16,1792]{1,0:T(8,128)S(1)}, f32[16,1792]{1,0:T(8,128)S(1)}, u32[]{:S(2)}, u32[]{:S(2)}) collective-permute-start(f32[16,1792]{1,0:T(8,128)S(1)} %fusion.60), channel_id=1, source_target_pairs={{0,24},{2,26},{4,28},{6,30},{8,0},{10,2},{12,4},{14,6},{16,8},{18,... | collective-permute-start | bytes 344072 | tf_op jit(solution)/shard_map/ppermute | solution.py:666
  389.8 15.6 %collective-permute-start.45 = (f32[16,1792]{1,0:T(8,128)S(1)}, f32[16,1792]{1,0:T(8,128)S(1)}, u32[]{:S(2)}, u32[]{:S(2)}) collective-permute-start(f32[16,1792]{1,0:T(8,128)S(1)} %fusion.60), channel_id=1, source_target_pairs={{0,16},{2,18},{4,20},{6,22},{8,24},{10,26},{12,28},{14,30},{16,0},... | collective-permute-start | bytes 344072 | tf_op jit(solution)/shard_map/ppermute | solution.py:666
  392.3 13.1 %collective-permute-start.44 = (f32[16,1792]{1,0:T(8,128)S(1)}, f32[16,1792]{1,0:T(8,128)S(1)}, u32[]{:S(2)}, u32[]{:S(2)}) collective-permute-start(f32[16,1792]{1,0:T(8,128)S(1)} %fusion.60), channel_id=1, source_target_pairs={{0,8},{2,10},{4,12},{6,14},{8,16},{10,18},{12,20},{14,22},{16,24},... | collective-permute-start | bytes 344072 | tf_op jit(solution)/shard_map/ppermute | solution.py:666
  394.1 14.3 %collective-permute-start.50 = (bf16[1,1,1,128,512]{4,3,2,1,0:T(8,128)(2,1)S(1)}, bf16[1,1,1,128,512]{4,3,2,1,0:T(8,128)(2,1)S(1)}, u32[]{:S(2)}, u32[]{:S(2)}) collective-permute-start(bf16[1,1,1,128,512]{4,3,2,1,0:T(8,128)(2,1)S(1)} %constant_dynamic-slice_fusion.2), channel_id=1, source_target_pairs={{0,8},{2,10},{4,12},{6,14},{8,16},{10,18},{12,20},{14,22},{16,24},... | collective-permute-start | bytes 393224 | tf_op jit(solution)/shard_map/ppermute | solution.py:666
  405.4 8.2 %collective-permute-start.47 = (bf16[1,1,1,32,2048]{4,3,2,1,0:T(8,128)(2,1)S(1)}, bf16[1,1,1,32,2048]{4,3,2,1,0:T(8,128)(2,1)S(1)}, u32[]{:S(2)}, u32[]{:S(2)}) collective-permute-start(bf16[1,1,1,32,2048]{4,3,2,1,0:T(8,128)(2,1)S(1)} %add_convert_fusion.26), channel_id=1, source_target_pairs={{0,8},{2,10},{4,12},{6,14},{8,16},{10,18},{12,20},{14,22},{16,24},... | collective-permute-start | bytes 393224 | tf_op jit(solution)/shard_map/ppermute | solution.py:666
  405.4 10.5 %collective-permute-start.48 = (bf16[1,1,1,32,2048]{4,3,2,1,0:T(8,128)(2,1)S(1)}, bf16[1,1,1,32,2048]{4,3,2,1,0:T(8,128)(2,1)S(1)}, u32[]{:S(2)}, u32[]{:S(2)}) collective-permute-start(bf16[1,1,1,32,2048]{4,3,2,1,0:T(8,128)(2,1)S(1)} %add_convert_fusion.25), channel_id=1, source_target_pairs={{0,8},{2,10},{4,12},{6,14},{8,16},{10,18},{12,20},{14,22},{16,24},... | collective-permute-start | bytes 393224 | tf_op jit(solution)/shard_map/ppermute | solution.py:666
  408.4 9.0 %collective-permute-start.49 = (bf16[1,1,1,128,512]{4,3,2,1,0:T(8,128)(2,1)S(1)}, bf16[1,1,1,128,512]{4,3,2,1,0:T(8,128)(2,1)S(1)}, u32[]{:S(2)}, u32[]{:S(2)}) collective-permute-start(bf16[1,1,1,128,512]{4,3,2,1,0:T(8,128)(2,1)S(1)} %add_convert_fusion.24), channel_id=1, source_target_pairs={{0,8},{2,10},{4,12},{6,14},{8,16},{10,18},{12,20},{14,22},{16,24},... | collective-permute-start | bytes 393224 | tf_op jit(solution)/shard_map/ppermute | solution.py:666
  413.7 7.9 %collective-permute-start.40 = (bf16[64,1024]{1,0:T(8,128)(2,1)S(1)}, bf16[64,1024]{1,0:T(8,128)(2,1)S(1)}, u32[]{:S(2)}, u32[]{:S(2)}) collective-permute-start(bf16[64,1024]{1,0:T(8,128)(2,1)S(1)} %slice.547), channel_id=1, source_target_pairs={{1,0},{3,2},{5,4},{7,6},{9,8},{11,10},{13,12},{15,14},{17,16},{19,... | collective-permute-start | bytes 393224 | tf_op jit(solution)/shard_map/ppermute | solution.py:1697
  418.3 6.1 %collective-permute-start.53 = (f32[16,1792]{1,0:T(8,128)S(1)}, f32[16,1792]{1,0:T(8,128)S(1)}, u32[]{:S(2)}, u32[]{:S(2)}) collective-permute-start(f32[16,1792]{1,0:T(8,128)S(1)} %add_add_fusion.2), channel_id=1, source_target_pairs={{0,4},{2,6},{4,0},{6,2},{8,12},{10,14},{12,8},{14,10},{16,20},{18,... | collective-permute-start | bytes 344072 | tf_op jit(solution)/shard_map/ppermute | solution.py:666
  419.1 8.2 %collective-permute-start.57 = (bf16[1,1,1,128,512]{4,3,2,1,0:T(8,128)(2,1)S(1)}, bf16[1,1,1,128,512]{4,3,2,1,0:T(8,128)(2,1)S(1)}, u32[]{:S(2)}, u32[]{:S(2)}) collective-permute-start(bf16[1,1,1,128,512]{4,3,2,1,0:T(8,128)(2,1)S(1)} %add_convert_fusion.20), channel_id=1, source_target_pairs={{0,8},{2,10},{4,12},{6,14},{8,16},{10,18},{12,20},{14,22},{16,24},... | collective-permute-start | bytes 393224 | tf_op jit(solution)/shard_map/ppermute | solution.py:666
  419.3 14.8 %collective-permute-start.52 = (bf16[4,1,1,32,2176]{4,3,2,1,0:T(8,128)(2,1)S(1)}, bf16[4,1,1,32,2176]{4,3,2,1,0:T(8,128)(2,1)S(1)}, u32[]{:S(2)}, u32[]{:S(2)}) collective-permute-start(bf16[4,1,1,32,2176]{4,3,2,1,0:T(8,128)(2,1)S(1)} %broadcast_select_fusion.12), channel_id=1, source_target_pairs={{0,1},{1,0},{2,3},{3,2},{4,5},{5,4},{6,7},{7,6},{8,9},{9,8},{10,11... | collective-permute-start | bytes 1671176 | tf_op jit(solution)/shard_map/ppermute | solution.py:666
  420.1 14.0 %collective-permute-start.51 = (bf16[4,1,1,32,2176]{4,3,2,1,0:T(8,128)(2,1)S(1)}, bf16[4,1,1,32,2176]{4,3,2,1,0:T(8,128)(2,1)S(1)}, u32[]{:S(2)}, u32[]{:S(2)}) collective-permute-start(bf16[4,1,1,32,2176]{4,3,2,1,0:T(8,128)(2,1)S(1)} %broadcast_select_fusion.13), channel_id=1, source_target_pairs={{0,4},{2,6},{4,0},{6,2},{8,12},{10,14},{12,8},{14,10},{16,20},{18,... | collective-permute-start | bytes 1671176 | tf_op jit(solution)/shard_map/ppermute | solution.py:666
  421.6 8.5 %collective-permute-start.55 = (bf16[1,1,1,32,2048]{4,3,2,1,0:T(8,128)(2,1)S(1)}, bf16[1,1,1,32,2048]{4,3,2,1,0:T(8,128)(2,1)S(1)}, u32[]{:S(2)}, u32[]{:S(2)}) collective-permute-start(bf16[1,1,1,32,2048]{4,3,2,1,0:T(8,128)(2,1)S(1)} %add_convert_fusion.22), channel_id=1, source_target_pairs={{0,8},{2,10},{4,12},{6,14},{8,16},{10,18},{12,20},{14,22},{16,24},... | collective-permute-start | bytes 393224 | tf_op jit(solution)/shard_map/ppermute | solution.py:666
  424.4 7.7 %collective-permute-start.56 = (bf16[1,1,1,128,512]{4,3,2,1,0:T(8,128)(2,1)S(1)}, bf16[1,1,1,128,512]{4,3,2,1,0:T(8,128)(2,1)S(1)}, u32[]{:S(2)}, u32[]{:S(2)}) collective-permute-start(bf16[1,1,1,128,512]{4,3,2,1,0:T(8,128)(2,1)S(1)} %add_convert_fusion.21), channel_id=1, source_target_pairs={{0,8},{2,10},{4,12},{6,14},{8,16},{10,18},{12,20},{14,22},{16,24},... | collective-permute-start | bytes 393224 | tf_op jit(solution)/shard_map/ppermute | solution.py:666
  427.3 6.8 %collective-permute-start.54 = (bf16[1,1,1,32,2048]{4,3,2,1,0:T(8,128)(2,1)S(1)}, bf16[1,1,1,32,2048]{4,3,2,1,0:T(8,128)(2,1)S(1)}, u32[]{:S(2)}, u32[]{:S(2)}) collective-permute-start(bf16[1,1,1,32,2048]{4,3,2,1,0:T(8,128)(2,1)S(1)} %add_convert_fusion.23), channel_id=1, source_target_pairs={{0,8},{2,10},{4,12},{6,14},{8,16},{10,18},{12,20},{14,22},{16,24},... | collective-permute-start | bytes 393224 | tf_op jit(solution)/shard_map/ppermute | solution.py:666
  434.6 10.3 %collective-permute-start.62 = (bf16[1,1,1,128,512]{4,3,2,1,0:T(8,128)(2,1)S(1)}, bf16[1,1,1,128,512]{4,3,2,1,0:T(8,128)(2,1)S(1)}, u32[]{:S(2)}, u32[]{:S(2)}) collective-permute-start(bf16[1,1,1,128,512]{4,3,2,1,0:T(8,128)(2,1)S(1)} %add_convert_fusion.19), channel_id=1, source_target_pairs={{0,8},{2,10},{4,12},{6,14},{8,16},{10,18},{12,20},{14,22},{16,24},... | collective-permute-start | bytes 393224 | tf_op jit(solution)/shard_map/ppermute | solution.py:666
  435.0 14.5 %collective-permute-start.60 = (bf16[1,1,1,64,2176]{4,3,2,1,0:T(8,128)(2,1)S(1)}, bf16[1,1,1,64,2176]{4,3,2,1,0:T(8,128)(2,1)S(1)}, u32[]{:S(2)}, u32[]{:S(2)}) collective-permute-start(bf16[1,1,1,64,2176]{4,3,2,1,0:T(8,128)(2,1)S(1)} %get-tuple-element.267), channel_id=1, source_target_pairs={{0,24},{2,26},{4,28},{6,30},{8,0},{10,2},{12,4},{14,6},{16,8},{18,... | collective-permute-start | bytes 835592 | tf_op jit(solution)/shard_map/ppermute | solution.py:666
  438.6 15.9 %collective-permute-start.58 = (bf16[1,1,1,64,2176]{4,3,2,1,0:T(8,128)(2,1)S(1)}, bf16[1,1,1,64,2176]{4,3,2,1,0:T(8,128)(2,1)S(1)}, u32[]{:S(2)}, u32[]{:S(2)}) collective-permute-start(bf16[1,1,1,64,2176]{4,3,2,1,0:T(8,128)(2,1)S(1)} %get-tuple-element.268), channel_id=1, source_target_pairs={{0,8},{2,10},{4,12},{6,14},{8,16},{10,18},{12,20},{14,22},{16,24},... | collective-permute-start | bytes 835592 | tf_op jit(solution)/shard_map/ppermute | solution.py:666
  438.6 23.4 %collective-permute-start.59 = (bf16[1,1,1,64,2176]{4,3,2,1,0:T(8,128)(2,1)S(1)}, bf16[1,1,1,64,2176]{4,3,2,1,0:T(8,128)(2,1)S(1)}, u32[]{:S(2)}, u32[]{:S(2)}) collective-permute-start(bf16[1,1,1,64,2176]{4,3,2,1,0:T(8,128)(2,1)S(1)} %get-tuple-element.269), channel_id=1, source_target_pairs={{0,16},{2,18},{4,20},{6,22},{8,24},{10,26},{12,28},{14,30},{16,0},... | collective-permute-start | bytes 835592 | tf_op jit(solution)/shard_map/ppermute | solution.py:666
  440.1 4.9 %collective-permute-start.61 = (f32[16,1792]{1,0:T(8,128)S(1)}, f32[16,1792]{1,0:T(8,128)S(1)}, u32[]{:S(2)}, u32[]{:S(2)}) collective-permute-start(f32[16,1792]{1,0:T(8,128)S(1)} %add.533), channel_id=1, source_target_pairs={{0,1},{1,0},{2,3},{3,2},{4,5},{5,4},{6,7},{7,6},{8,9},{9,8},{10,11... | collective-permute-start | bytes 344072 | tf_op jit(solution)/shard_map/ppermute | solution.py:666
  (69 other events, 512.9 us)
